TPU v7x, 512 devices: a whole 4x8x8 slice. The times are simulated.
512 devices in a mesh: grp: 4 (over x), comp: 128 (over y, z, core).
Axes of the slice: x: 4, y: 8, z: 8, core: 2. Of those that a mesh axis runs over, the one named last changes fastest.
Arguments:
- spectra: float32 [600, 196608], P('grp', 'comp'), may hold values from 0.05 to 2
- wind_speed: float32 [196608], P('comp'), may hold values from 4 to 24
- wind_dir: float32 [196608], P('comp'), may hold values from -3.140625 to 3.140625
- sea_cell: int32 [196608], P('comp'), may hold values from 0 to 2047, as said below
Outputs:
- spectra_grid: float32 [600, 1024, 256], P('grp', 'comp')
Inputs may be any that keep to these rules, and one draw needn't show every extreme that they name: `sea_cell`: each aligned block of 1536 entries names 1536 different cells of one tile of 8 x 256 cells (row * 256 + column).
All inputs are finite; a program needn't handle non-finite values.
Results may differ from a plain program's by a relative error of at most 0.0003.
Values sent between devices are 32-bit elements; how exact they have to be, the bound alone decides.
No kernel may reach another device: no remote copies, remote signals or barrier semaphores. Data moves between devices by JAX's collectives and lax.ppermute only.
A program may use at most 64 MiB of HBM per device.

v0:
```python
import math

import jax
import jax.numpy as jnp
from jax import lax
from jax.sharding import PartitionSpec as P

FREQ = 25
TROWS = 8
NY = 256
ADV_STEPS = 2


GRAV = 9.81
LOW_FREQ = 0.0418
FREQ_STEP = 1.1


def padded_2(block, sides, width):
    for axis, dim in sides:
        count = lax.axis_size(axis)
        forward = [(i, i + 1) for i in range(count - 1)]
        backward = [(target, source) for source, target in forward]
        low = lax.ppermute(
            lax.slice_in_dim(block, block.shape[dim] - width, None, axis=dim), axis, forward
        )
        high = lax.ppermute(lax.slice_in_dim(block, 0, width, axis=dim), axis, backward)
        block = jnp.concatenate([low, block, high], axis=dim)
    return block


def spectral_tables(first_dir, dir_count, total_dirs, freq_count):
    component = jnp.arange(dir_count * freq_count, dtype=jnp.int32)
    direction = (component // freq_count + first_dir).astype(jnp.float32)
    frequency = LOW_FREQ * jnp.power(
        jnp.float32(FREQ_STEP), (component % freq_count).astype(jnp.float32)
    )
    angles = 2.0 * math.pi * (direction + 0.5) / total_dirs
    angular = 2.0 * math.pi * frequency
    weight = 2.0 * math.pi / total_dirs * 0.1 * frequency
    return (angles, angular, weight)


def source_terms(spectra, energy, inverse, angles, angular, wind_speed, wind_dir):
    mean_freq = energy / inverse
    wavenumber = mean_freq * mean_freq / GRAV
    steepness = energy * wavenumber * wavenumber
    steep_ratio = steepness / (steepness + 0.02)
    forcing = 28.0 * 0.035 * wind_speed * jnp.cos(angles - wind_dir) * angular / GRAV
    rate_in = 0.1 * jnp.maximum(forcing - 1.0, 0.0)
    relative = angular / mean_freq
    rate_out = 0.4 * relative * relative * steep_ratio
    return spectra * jnp.exp(rate_in - rate_out)


def courant(angles, angular):
    reach = 0.45 * (2.0 * math.pi * LOW_FREQ) / angular
    return (reach * jnp.cos(angles), reach * jnp.sin(angles))


def koren_slope(slope_back, slope_ahead):
    middle = (slope_back + 2.0 * slope_ahead) / 3.0
    rising = jnp.maximum(0.0, jnp.minimum(jnp.minimum(2.0 * slope_ahead, middle), 2.0 * slope_back))
    falling = jnp.minimum(
        0.0, jnp.maximum(jnp.maximum(2.0 * slope_ahead, middle), 2.0 * slope_back)
    )
    return jnp.where(slope_back >= 0.0, rising, falling)


def face_flux(back_one, centre, ahead_one, ahead_two, number):
    forward = number >= 0.0
    upstream = jnp.where(forward, centre, ahead_one)
    slope_back = jnp.where(forward, centre - back_one, ahead_one - ahead_two)
    slope_ahead = jnp.where(forward, ahead_one - centre, centre - ahead_one)
    return number * (
        upstream + 0.5 * (1.0 - jnp.abs(number)) * koren_slope(slope_back, slope_ahead)
    )


def advect(padded, courant_x, courant_y):
    count = padded.shape[-2] - 4
    flux_rows = face_flux(
        padded[..., 0 : count + 1, :],
        padded[..., 1 : count + 2, :],
        padded[..., 2 : count + 3, :],
        padded[..., 3 : count + 4, :],
        courant_x,
    )
    centre = padded[..., 2 : count + 2, :]
    flux_cols = face_flux(
        jnp.roll(centre, 1, -1),
        centre,
        jnp.roll(centre, -1, -1),
        jnp.roll(centre, -2, -1),
        courant_y,
    )
    return (
        centre
        - (flux_rows[..., 1:, :] - flux_rows[..., :-1, :])
        - (flux_cols - jnp.roll(flux_cols, 1, -1))
    )


def local(spectra, wind_speed, wind_dir, sea_cell):
    local_comps = spectra.shape[0]
    dir_count = local_comps // FREQ
    group_index = lax.axis_index("grp")
    angles, angular, weight = spectral_tables(
        group_index * dir_count, dir_count, dir_count * lax.axis_size("grp"), FREQ
    )
    partial_energy = jnp.sum(weight[:, None] * spectra, axis=0)
    partial_inverse = jnp.sum((weight / angular)[:, None] * spectra, axis=0)
    energy, inverse = lax.psum((partial_energy, partial_inverse), "grp")
    sourced = source_terms(
        spectra,
        energy,
        inverse,
        angles[:, None],
        angular[:, None],
        wind_speed[None, :],
        wind_dir[None, :],
    )
    received = lax.all_to_all(sourced, "comp", split_axis=1, concat_axis=1, tiled=True)
    wave_field = jnp.zeros((local_comps, TROWS * NY), jnp.float32).at[:, sea_cell].set(received)
    wave_field = wave_field.reshape(local_comps, TROWS, NY)
    sea_mask = jnp.zeros((TROWS * NY,), jnp.float32).at[sea_cell].set(1.0).reshape(TROWS, NY)
    courant_x, courant_y = courant(angles, angular)
    courant_x = courant_x[:, None, None]
    courant_y = courant_y[:, None, None]
    for substep in range(ADV_STEPS):
        padded = padded_2(wave_field, (("comp", 1),), 2)
        wave_field = advect(padded, courant_x, courant_y) * sea_mask
    return wave_field


def solution(mesh):
    in_specs = (P("grp", "comp"), P("comp"), P("comp"), P("comp"))
    out_specs = P("grp", "comp", None)
    return jax.shard_map(local, mesh=mesh, in_specs=in_specs, out_specs=out_specs, check_vma=False)
```

profile of v0, /device:TPU:8, one launch (start us, length us, event | category | flops | bytes accessed | tf_op | source)
XLA Modules:
  0.0 125.3 jit_solution(4279639210668831532)
XLA Ops:
  0.0 0.8 broadcast_multiply_fusion
  0.8 1.4 %multiply_reduce_fusion = (f32[1536]{0:T(1024)S(1)}, f32[1536]{0:T(1024)S(1)}) fusion(f32[150,1536]{1,0:T(8,128)} %param.4, f32[150]{0:T(256)S(1)} %get-tuple-element.24, f32[150]{0:T(256)S(1)} %get-tuple-element.23), kind=kLoop, calls=%fused_computation.54 | loop fusion | flops 918528 | bytes 935088 | tf_op jit(solution)/shard_map/reduce_sum | solution.py:112
  2.2 16.9 %all-reduce = (f32[1536]{0:T(1024)S(1)}, f32[1536]{0:T(1024)S(1)}) all-reduce(f32[1536]{0:T(1024)S(1)} %get-tuple-element.6, f32[1536]{0:T(1024)S(1)} %get-tuple-element.5), channel_id=1, replica_groups=mesh['grp'=4,'comp'=128] {'grp'}, use_global_device_ids=true, to_apply=%region_1.2 | all-reduce | flops 3072 | bytes 24576 | tf_op jit(solution)/shard_map/psum | solution.py:113
  19.2 4.2 %fusion.24 = f32[150,1536]{1,0:T(8,128)S(1)} fusion(f32[150,1536]{1,0:T(8,128)S(1)} %copy-done, f32[1536]{0:T(1024)S(1)} %get-tuple-element.9, f32[1536]{0:T(1024)S(1)} %get-tuple-element.10, f32[150]{0:T(256)S(1)} %get-tuple-element.32, f32[1536]{0:T(1024)} %param.6, f32[150]{0:T(256)S(1)} %get-tuple-element.31, f32[1536]{0:T(1024)S(1)} %broadcast_multiply_fusion), kind=kLoop, calls=%fused_computation.53 | loop fusion | flops 2995200 | bytes 1868976 | tf_op jit(solution)/shard_map/mul | solution.py:53
  23.4 1.6 %copy.37 = f32[150,1536]{0,1:T(8,128)} copy(f32[150,1536]{1,0:T(8,128)S(1)} %fusion.24) | data formatting | bytes 1843200 | tf_op jit(solution)/shard_map/mul | solution.py:53
  25.0 1.5 %all_to_all.8 = f32[150,128,12]{0,2,1:T(8,128)S(1)} reshape(f32[150,1536]{0,1:T(8,128)} %copy.37) | data formatting | bytes 1843200 | tf_op jit(solution)/shard_map/all_to_all | solution.py:123
  26.4 3.5 %reshape.121 = f32[128,1,1800]{2,1,0:T(1,128)} reshape(f32[128,12,150]{2,1,0:T(8,128)S(1)} %bitcast.14) | data formatting | bytes 1843200
  30.0 17.5 %all-to-all-start = ((f32[128,1,1800]{2,1,0:T(1,128)}), f32[128,1,1800]{2,1,0:T(1,128)S(1)}, u32[]{:S(2)}, u32[]{:S(2)}) async-start(f32[128,1,1800]{2,1,0:T(1,128)} %reshape.121), calls=%async_computation | async-start | bytes 1966080 | tf_op jit(solution)/shard_map/all_to_all | solution.py:123
  47.5 6.4 %scatter_custom_fusion.1 = f32[2048]{0:T(1024)S(1)} fusion(s32[1536]{0:T(1024)S(1)} %compare_select_fusion, f32[1536]{0:T(1024)S(1)} %broadcast.447, f32[]{:T(128)} %constant.24.clone.1), kind=kCustom, calls=%fused_computation.59 | custom fusion | bytes 8196 | tf_op jit(solution)/shard_map/scatter | solution.py:126
  54.1 23.4 %all-to-all-done = f32[128,1,1800]{2,1,0:T(1,128)S(1)} async-done(((f32[128,1,1800]{2,1,0:T(1,128)}), f32[128,1,1800]{2,1,0:T(1,128)S(1)}, u32[]{:S(2)}, u32[]{:S(2)}) %all-to-all-start) | async-done | bytes 921632 | tf_op jit(solution)/shard_map/all_to_all | solution.py:123
  77.5 0.5 broadcast.467
  78.0 3.0 %reduce = f32[128,1800]{1,0:T(8,128)S(1)} reduce(f32[128,1,1800]{2,1,0:T(1,128)S(1)} %all-to-all-done, f32[]{:T(128)} %broadcast.467), dimensions={1}, to_apply=%all_to_all.9.reduce_sub_computation | reduce | bytes 1843204 | tf_op jit(solution)/shard_map/all_to_all | solution.py:123
  81.0 2.1 %reshape.122 = f32[128,12,150]{2,1,0:T(8,128)S(1)} reshape(f32[128,1800]{1,0:T(8,128)S(1)} %reduce) | data formatting | bytes 1843200
  83.1 1.3 %reshape.100 = f32[150,1536]{0,1:T(8,128)} reshape(f32[150,128,12]{0,2,1:T(8,128)S(1)} %bitcast.15) | data formatting | bytes 1843200 | tf_op jit(solution)/shard_map/all_to_all | solution.py:123
  84.5 8.0 %scatter_custom_fusion = f32[150,2048]{0,1:T(8,128)S(1)} fusion(s32[1536]{0:T(1024)S(1)} %compare_select_fusion, f32[150,1536]{0,1:T(8,128)} %reshape.100, f32[]{:T(128)} %constant.24.clone.1), kind=kCustom, calls=%fused_computation.2 | custom fusion | bytes 2150404 | tf_op jit(solution)/shard_map/scatter | solution.py:124
  92.4 0.8 copy.42
  93.3 0.4 fusion.39
  94.4 1.9 %collective-permute-start = (f32[150,2,256]{2,0,1:T(8,128)S(1)}, f32[150,2,256]{2,0,1:T(8,128)S(1)}, u32[]{:S(2)}, u32[]{:S(2)}) collective-permute-start(f32[150,2,256]{2,0,1:T(8,128)S(1)} %get-tuple-element.21), channel_id=1, source_target_pairs={{0,1},{1,2},{2,3},{3,4},{4,5},{5,6},{6,7},{7,8},{8,9},{9,10},{10,1... | collective-permute-start | bytes 921608 | tf_op jit(solution)/shard_map/ppermute | solution.py:24
  96.3 5.8 %collective-permute-start.1 = (f32[150,2,256]{2,0,1:T(8,128)S(1)}, f32[150,2,256]{2,0,1:T(8,128)S(1)}, u32[]{:S(2)}, u32[]{:S(2)}) collective-permute-start(f32[150,2,256]{2,0,1:T(8,128)S(1)} %get-tuple-element.22), channel_id=1, source_target_pairs={{1,0},{2,1},{3,2},{4,3},{5,4},{6,5},{7,6},{8,7},{9,8},{10,9},{11,1... | collective-permute-start | bytes 921608 | tf_op jit(solution)/shard_map/ppermute | solution.py:27
  102.1 1.2 add_multiply_fusion.3
  103.5 1.2 collective-permute-done
  104.7 1.8 %collective-permute-done.1 = f32[150,2,256]{2,0,1:T(8,128)S(1)} collective-permute-done((f32[150,2,256]{2,0,1:T(8,128)S(1)}, f32[150,2,256]{2,0,1:T(8,128)S(1)}, u32[]{:S(2)}, u32[]{:S(2)}) %collective-permute-start.1) | collective-permute-done | bytes 307232 | tf_op jit(solution)/shard_map/ppermute | solution.py:27
  106.5 1.5 %add_multiply_fusion.1 = f32[150,9,256]{2,0,1:T(8,128)S(1)} fusion(f32[150,2,256]{2,0,1:T(8,128)S(1)} %collective-permute-done.1, f32[150,8,256]{2,0,1:T(8,128)S(1)} %copy.42, f32[150,2,256]{2,0,1:T(8,128)S(1)} %collective-permute-done, f32[150]{0:T(256)S(1)} %get-tuple-element.27, f32[150]{0:T(256)S(1)} %get-tuple-element.28, ...), kind=kLoop, calls=%fused_computation.27 | loop fusion | flops 8985600 | bytes 3226950 | tf_op jit(solution)/shard_map/mul | solution.py:75
  108.0 0.5 fusion.17
  109.6 1.9 %collective-permute-start.2 = (f32[150,2,256]{2,0,1:T(8,128)S(1)}, f32[150,2,256]{2,0,1:T(8,128)S(1)}, u32[]{:S(2)}, u32[]{:S(2)}) collective-permute-start(f32[150,2,256]{2,0,1:T(8,128)S(1)} %get-tuple-element.15), channel_id=1, source_target_pairs={{0,1},{1,2},{2,3},{3,4},{4,5},{5,6},{6,7},{7,8},{8,9},{9,10},{10,1... | collective-permute-start | bytes 921608 | tf_op jit(solution)/shard_map/ppermute | solution.py:24
  111.5 6.1 %collective-permute-start.3 = (f32[150,2,256]{2,0,1:T(8,128)S(1)}, f32[150,2,256]{2,0,1:T(8,128)S(1)}, u32[]{:S(2)}, u32[]{:S(2)}) collective-permute-start(f32[150,2,256]{2,0,1:T(8,128)S(1)} %get-tuple-element.16), channel_id=1, source_target_pairs={{1,0},{2,1},{3,2},{4,3},{5,4},{6,5},{7,6},{8,7},{9,8},{10,9},{11,1... | collective-permute-start | bytes 921608 | tf_op jit(solution)/shard_map/ppermute | solution.py:27
  117.7 1.2 add_multiply_fusion.2
  119.2 0.9 collective-permute-done.2
  120.1 1.8 %collective-permute-done.3 = f32[150,2,256]{2,0,1:T(8,128)S(1)} collective-permute-done((f32[150,2,256]{2,0,1:T(8,128)S(1)}, f32[150,2,256]{2,0,1:T(8,128)S(1)}, u32[]{:S(2)}, u32[]{:S(2)}) %collective-permute-start.3) | collective-permute-done | bytes 307232 | tf_op jit(solution)/shard_map/ppermute | solution.py:27
  121.9 1.5 %add_multiply_fusion = f32[150,9,256]{2,0,1:T(8,128)S(1)} fusion(f32[150,2,256]{2,0,1:T(8,128)S(1)} %collective-permute-done.3, f32[150,8,256]{2,0,1:T(8,128)S(1)} %fusion.17, f32[150,2,256]{2,0,1:T(8,128)S(1)} %collective-permute-done.2, f32[150]{0:T(256)S(1)} %get-tuple-element.27, f32[150]{0:T(256)S(1)} %get-tuple-element.28, ...), kind=kLoop, calls=%fused_computation.26 | loop fusion | flops 8985600 | bytes 3226950 | tf_op jit(solution)/shard_map/mul | solution.py:75
  123.4 0.5 fusion.14
  123.9 1.4 %copy.53 = f32[150,8,256]{2,1,0:T(8,128)} copy(f32[150,8,256]{2,0,1:T(8,128)S(1)} %fusion.14) | data formatting | bytes 2457600 | tf_op jit(solution)/shard_map/mul | solution.py:132
  (24 shorter events, 2.5 us)
Async XLA Ops:
  0.0 19.2 %copy-start = (f32[150,1536]{1,0:T(8,128)S(1)}, f32[150,1536]{1,0:T(8,128)}, u32[]{:S(2)}) copy-start(f32[150,1536]{1,0:T(8,128)} %param.4) | copy-start | bytes 2764804
  30.0 17.5 %copy-start.1 = (s32[1536]{0:T(1024)S(1)}, s32[1536]{0:T(1024)}, u32[]{:S(2)}) copy-start(s32[1536]{0:T(1024)} %param.7) | copy-start | bytes 18436
  30.0 47.5 %all-to-all-start = ((f32[128,1,1800]{2,1,0:T(1,128)}), f32[128,1,1800]{2,1,0:T(1,128)S(1)}, u32[]{:S(2)}, u32[]{:S(2)}) async-start(f32[128,1,1800]{2,1,0:T(1,128)} %reshape.121), calls=%async_computation | async-start | bytes 1966080 | tf_op jit(solution)/shard_map/all_to_all | solution.py:123
  94.4 10.3 %collective-permute-start = (f32[150,2,256]{2,0,1:T(8,128)S(1)}, f32[150,2,256]{2,0,1:T(8,128)S(1)}, u32[]{:S(2)}, u32[]{:S(2)}) collective-permute-start(f32[150,2,256]{2,0,1:T(8,128)S(1)} %get-tuple-element.21), channel_id=1, source_target_pairs={{0,1},{1,2},{2,3},{3,4},{4,5},{5,6},{6,7},{7,8},{8,9},{9,10},{10,1... | collective-permute-start | bytes 921608 | tf_op jit(solution)/shard_map/ppermute | solution.py:24
  96.3 10.2 %collective-permute-start.1 = (f32[150,2,256]{2,0,1:T(8,128)S(1)}, f32[150,2,256]{2,0,1:T(8,128)S(1)}, u32[]{:S(2)}, u32[]{:S(2)}) collective-permute-start(f32[150,2,256]{2,0,1:T(8,128)S(1)} %get-tuple-element.22), channel_id=1, source_target_pairs={{1,0},{2,1},{3,2},{4,3},{5,4},{6,5},{7,6},{8,7},{9,8},{10,9},{11,1... | collective-permute-start | bytes 921608 | tf_op jit(solution)/shard_map/ppermute | solution.py:27
  109.6 10.5 %collective-permute-start.2 = (f32[150,2,256]{2,0,1:T(8,128)S(1)}, f32[150,2,256]{2,0,1:T(8,128)S(1)}, u32[]{:S(2)}, u32[]{:S(2)}) collective-permute-start(f32[150,2,256]{2,0,1:T(8,128)S(1)} %get-tuple-element.15), channel_id=1, source_target_pairs={{0,1},{1,2},{2,3},{3,4},{4,5},{5,6},{6,7},{7,8},{8,9},{9,10},{10,1... | collective-permute-start | bytes 921608 | tf_op jit(solution)/shard_map/ppermute | solution.py:24
  111.5 10.3 %collective-permute-start.3 = (f32[150,2,256]{2,0,1:T(8,128)S(1)}, f32[150,2,256]{2,0,1:T(8,128)S(1)}, u32[]{:S(2)}, u32[]{:S(2)}) collective-permute-start(f32[150,2,256]{2,0,1:T(8,128)S(1)} %get-tuple-element.16), channel_id=1, source_target_pairs={{1,0},{2,1},{3,2},{4,3},{5,4},{6,5},{7,6},{8,7},{9,8},{10,9},{11,1... | collective-permute-start | bytes 921608 | tf_op jit(solution)/shard_map/ppermute | solution.py:27
where the time goes:
time: 126 us; the launch traced here: 125 us
  starting transfers between devices  33.2 us (26%)
  local copies, waits for them, and re-layouts  29.8 us (24%)
  waiting for transfers between devices  29.1 us (23%)
  blocking collectives  16.9 us (13%)
  other arithmetic  16.1 us (13%)
    all_to_all x1, waiting for transfers between devices, local(): lax.all_to_all(sourced, 'comp', split_axis=1, concat_axis=1, tiled=True)  23.4 us
    all_to_all x1, starting transfers between devices, local(): lax.all_to_all(sourced, 'comp', split_axis=1, concat_axis=1, tiled=True)  17.5 us
    psum x1, blocking collectives, local(): energy, inverse = lax.psum((partial_energy, partial_inverse), 'grp')  16.9 us
    ppermute x2, starting transfers between devices, padded_2(): lax.ppermute(lax.slice_in_dim(block, 0, width, axis=dim), axis, backward)  11.9 us
    scatter x1, local copies, waits for them, and re-layouts, local(): jnp.zeros((local_comps, TROWS * NY), jnp.float32).at[:, sea_cell]  7.98 us
    scatter x1, local copies, waits for them, and re-layouts, local(): jnp.zeros((TROWS * NY,), jnp.float32).at[sea_cell].set(1.0)  6.36 us
    unnamed x6, local copies, waits for them, and re-layouts  5.64 us
    mul x4, other arithmetic, face_flux(): number * (upstream + 0.5 * (1.0 - jnp.abs(number)) * koren_slope(slope_ba...  5.49 us
  transfers between devices with their start and end apart: 5, of which 5 were waited for; matrix products, arithmetic and copies ran while one was open for 8% of the time, Pallas kernels for 0%

commit v1 on v0

v1 whole, which is shorter than its diff:
```python
import functools
import math

import jax
import jax.numpy as jnp
import numpy as np
from jax import lax
from jax.experimental import pallas as pl
from jax.experimental.pallas import tpu as pltpu
from jax.sharding import PartitionSpec as P

DIRS = 24
FREQ = 25
TROWS = 8
NY = 256
SEA = 1536
SEND = 12
GROUPS = 4
TILES = 128
LOCAL = DIRS * FREQ // GROUPS
ROWS = 152
MASK_ROW = LOCAL
MAIN = 128
EXTRA = ROWS - MAIN
PER_TILE = 5
SLOTS = 15
GRAV = 9.81
LOW_FREQ = 0.0418
FREQ_STEP = 1.1

VMEM = pl.BlockSpec(memory_space=pltpu.VMEM)
SMEM = pl.BlockSpec(memory_space=pltpu.SMEM)
BIG = pltpu.CompilerParams(vmem_limit_bytes=48 * 1024 * 1024)

W_E, W_I, C_COS, C_SIN, C_OUT, U_X, K_X, U_Y, K_Y = range(9)


def coefficient_table():
    table = np.zeros((GROUPS, ROWS, 128), np.float64)
    for group in range(GROUPS):
        for row in range(LOCAL):
            d, j = row // FREQ + group * (DIRS // GROUPS), row % FREQ
            angle = 2.0 * math.pi * (d + 0.5) / DIRS
            freq = LOW_FREQ * FREQ_STEP**j
            s = 2.0 * math.pi * freq
            w = 2.0 * math.pi / DIRS * 0.1 * freq
            reach = 0.45 * (2.0 * math.pi * LOW_FREQ) / s
            ux, uy = abs(reach * math.cos(angle)), abs(reach * math.sin(angle))
            push = 0.1 * 28.0 * 0.035 * s / GRAV
            table[group, row, :9] = (
                w, w / s, push * math.cos(angle), push * math.sin(angle), 0.4 * s * s,
                ux, ux * (1.0 - ux), uy, uy * (1.0 - uy),
            )
    return table.astype(np.float32)


def pack_kernel(x_ref, wind_ref, out_ref, z_ref, b_ref):
    b_ref[0 : LOCAL - MAIN, :] = x_ref[MAIN:LOCAL, :]
    b_ref[LOCAL - MAIN : EXTRA, :] = wind_ref[...]
    b_ref[EXTRA:128, :] = jnp.zeros((128 - EXTRA, SEA), jnp.float32)
    for block in range(SEA // 128):
        cols = slice(block * 128, block * 128 + 128)
        z_ref[0, cols, :] = x_ref[0:MAIN, cols].T
        z_ref[1, cols, :] = b_ref[:, cols].T
    for k in range(SEND):
        out_ref[pl.ds(k, TILES, stride=SLOTS), :] = z_ref[0, pl.ds(k, TILES, stride=SEND), :]
    for tile in range(SLOTS - SEND):
        total = None
        for k in range(tile * PER_TILE, min(SEND, (tile + 1) * PER_TILE)):
            piece = z_ref[1, pl.ds(k, TILES, stride=SEND), :]
            shift = (k % PER_TILE) * EXTRA
            piece = pltpu.roll(piece, shift, 1) if shift else piece
            total = piece if total is None else total + piece
        out_ref[pl.ds(SEND + tile, TILES, stride=SLOTS), :] = total


def moments_kernel(r_ref, tab_ref, y_ref, wind_ref, e_ref):
    extra = None
    we = jnp.broadcast_to(tab_ref[:, W_E : W_E + 1], (ROWS, 128))
    wi = jnp.broadcast_to(tab_ref[:, W_I : W_I + 1], (ROWS, 128))
    for k in range(SEND):
        if k % PER_TILE == 0:
            extra = r_ref[pl.ds(SEND + k // PER_TILE, TILES, stride=SLOTS), :].T
        part = extra[(k % PER_TILE) * EXTRA : (k % PER_TILE + 1) * EXTRA, :]
        main = r_ref[pl.ds(k, TILES, stride=SLOTS), :].T
        y_ref[k, 0:MAIN, :] = main
        y_ref[k, MAIN:ROWS, :] = part
        wind_ref[k : k + 1, :] = part[LOCAL - MAIN : LOCAL - MAIN + 1, :]
        wind_ref[SEND + k : SEND + k + 1, :] = part[LOCAL - MAIN + 1 : EXTRA, :]
        y = y_ref[k]
        energy = jnp.sum(y * we, axis=0, keepdims=True)
        inverse = jnp.sum(y * wi, axis=0, keepdims=True)
        for g in range(GROUPS):
            e_ref[g, k : k + 1, :] = energy
            e_ref[g, SEND + k : SEND + k + 1, :] = inverse


def onehot_kernel(cell_ref, out_ref):
    lane = lax.broadcasted_iota(jnp.int32, (128, 128), 1)
    for k in range(SEND):
        cell = jnp.broadcast_to(cell_ref[k : k + 1, :], (128, 128)).T
        for tile in range(TROWS * NY // 128):
            hit = cell == lane + tile * 128
            out_ref[k * 128 : (k + 1) * 128, tile * 128 : (tile + 1) * 128] = jnp.where(
                hit, 1.0, 0.0
            ).astype(jnp.bfloat16)


def place_kernel(y_ref, wind_ref, e_ref, tab_ref, hot_ref, low_ref, mid_ref, up_ref, s_ref):
    moments = e_ref[0] + e_ref[1] + e_ref[2] + e_ref[3]
    energy, inverse = moments[0:SEND], moments[SEND : 2 * SEND]
    mean = energy / inverse
    wavenumber = mean * mean / GRAV
    steepness = energy * wavenumber * wavenumber
    ratio = steepness / (steepness + 0.02)
    decay = ratio / (mean * mean)
    speed, heading = wind_ref[0:SEND, :], wind_ref[SEND : 2 * SEND, :]
    along = speed * jnp.cos(heading)
    across = speed * jnp.sin(heading)
    ccos = jnp.broadcast_to(tab_ref[:, C_COS : C_COS + 1], (ROWS, 128))
    csin = jnp.broadcast_to(tab_ref[:, C_SIN : C_SIN + 1], (ROWS, 128))
    cout = jnp.broadcast_to(tab_ref[:, C_OUT : C_OUT + 1], (ROWS, 128))
    row = lax.broadcasted_iota(jnp.int32, (ROWS, 128), 0)
    for k in range(SEND):
        grow = ccos * along[k : k + 1] + csin * across[k : k + 1]
        rate = jnp.maximum(grow - 0.1, 0.0) - cout * decay[k : k + 1]
        value = y_ref[k] * jnp.exp(rate)
        value = jnp.where(row < LOCAL, value, jnp.where(row == MASK_ROW, 1.0, 0.0))
        s_ref[:, k * 128 : (k + 1) * 128] = value
    value = s_ref[...]
    high = value.astype(jnp.bfloat16)
    rest = (value - high.astype(jnp.float32)).astype(jnp.bfloat16)
    for e in range(TROWS):
        hot = hot_ref[:, e * NY : (e + 1) * NY]
        out = jnp.dot(high, hot, preferred_element_type=jnp.float32)
        out = out + jnp.dot(rest, hot, preferred_element_type=jnp.float32)
        if e < 2:
            low_ref[e] = out
        elif e < 4:
            mid_ref[e - 2] = out
        else:
            up_ref[e - 4] = out


def limited(a, b):
    m = (a + (b + b)) * (1.0 / 6.0)
    rising = jnp.maximum(jnp.minimum(m, jnp.minimum(a, b)), 0.0)
    falling = jnp.minimum(jnp.maximum(m, jnp.maximum(a, b)), 0.0)
    return rising + falling


def advance(q, mask, coef, forward):
    ux, kx, uy, ky = coef
    step, back = (NY - 1, 1) if forward else (1, NY - 1)
    diff = [q[i + 1] - q[i] for i in range(len(q) - 1)]
    flux = [None] + [
        ux * q[i] + kx * limited(diff[i - 1], diff[i]) for i in range(1, len(q) - 1)
    ]
    new = []
    for i in range(2, len(q) - 1):
        ahead = pltpu.roll(q[i], step, 1) - q[i]
        behind = pltpu.roll(ahead, back, 1)
        side = uy * q[i] + ky * limited(behind, ahead)
        div = (flux[i] - flux[i - 1]) + (side - pltpu.roll(side, back, 1))
        new.append((q[i] - div) * mask[i - 2])
    return new


def advect_kernel(flag_ref, tab_ref, below_ref, low_ref, mid_ref, up_ref, above_ref, out_ref,
                  mask_ref, coef_ref, turn_ref):
    cells = [(below_ref, i) for i in range(4)] + [(low_ref, i) for i in range(2)]
    cells += [(mid_ref, i) for i in range(2)] + [(up_ref, i) for i in range(4)]
    cells += [(above_ref, i) for i in range(2)]
    for i in range(2, 13):
        ref, at = cells[i]
        mask_ref[i - 2] = jnp.broadcast_to(ref[at, MASK_ROW : MASK_ROW + 1, :], (8, NY))
    for n, column in enumerate((U_X, K_X, U_Y, K_Y)):
        coef_ref[n] = jnp.broadcast_to(tab_ref[:, column : column + 1], (ROWS, NY))
    mirrored = flag_ref[0]

    def tile(start, count, forward):
        rows = pl.ds(start, 8)
        q = [ref[at, rows, :] for ref, at in cells]
        coef = [coef_ref[n, rows, :] for n in range(4)]
        q = advance(q, [mask_ref[i] for i in range(11)], coef, forward)
        q = advance(q, [mask_ref[i] for i in range(2, 10)], coef, forward)
        for e in range(TROWS):
            r = e + (TROWS - 1 - 2 * e) * mirrored
            for half in range(2):
                turn_ref[half, pl.ds(r, 8, stride=TROWS), :] = q[e][:, half * 128 : half * 128 + 128]
        for i in range(count):
            for half in range(2):
                out_ref[start + i, :, half * 128 : half * 128 + 128] = turn_ref[
                    half, i * TROWS : (i + 1) * TROWS, :
                ]

    def sweep(forward):
        def body(i, carry):
            tile(pl.multiple_of(i * 8, 8), 8, forward)
            return carry

        lax.fori_loop(0, LOCAL // 8, body, 0)
        tile(LOCAL // 8 * 8, LOCAL % 8, forward)

    @pl.when(flag_ref[1] == 0)
    def _():
        sweep(True)

    @pl.when(flag_ref[1] == 1)
    def _():
        sweep(False)


def call(kernel, shapes, scratch, ins, *args):
    return pl.pallas_call(
        kernel,
        out_shape=shapes,
        in_specs=ins,
        out_specs=jax.tree.map(lambda _: VMEM, shapes),
        scratch_shapes=scratch,
        compiler_params=BIG,
    )(*args)


def f32(*shape):
    return jax.ShapeDtypeStruct(shape, jnp.float32)


def local(spectra, wind_speed, wind_dir, sea_cell):
    group = lax.axis_index("grp")
    table = lax.dynamic_index_in_dim(jnp.asarray(coefficient_table()), group, 0, keepdims=False)
    mirror_x = ((group == 1) | (group == 2)).astype(jnp.int32)
    mirror_y = (group >= 2).astype(jnp.int32)
    flags = jnp.stack([mirror_x, mirror_y])
    wind = jnp.stack([wind_speed, wind_dir])
    packed = call(
        pack_kernel,
        f32(TILES * SLOTS, 128),
        [pltpu.VMEM((2, SEA, 128), jnp.float32), pltpu.VMEM((128, SEA), jnp.float32)],
        [VMEM] * 2,
        spectra,
        wind,
    )
    received = lax.all_to_all(
        packed.reshape(TILES, 1, SLOTS * 128), "comp", split_axis=0, concat_axis=0, tiled=True
    ).reshape(TILES * SLOTS, 128)
    cells = sea_cell.reshape(TILES, SEND).T
    cells = cells ^ (mirror_x * (NY * (TROWS - 1)))
    hot = call(
        onehot_kernel,
        jax.ShapeDtypeStruct((SEA, TROWS * NY), jnp.bfloat16),
        [],
        [VMEM],
        cells,
    )
    points, wind_here, partial = call(
        moments_kernel,
        (f32(SEND, ROWS, 128), f32(2 * SEND, 128), f32(GROUPS, 2 * SEND, 128)),
        [],
        [VMEM] * 2,
        received,
        table,
    )
    partial = lax.all_to_all(partial, "grp", split_axis=0, concat_axis=0, tiled=True)
    low, mid, up = call(
        place_kernel,
        (f32(2, ROWS, NY), f32(2, ROWS, NY), f32(4, ROWS, NY)),
        [pltpu.VMEM((ROWS, SEA), jnp.float32)],
        [VMEM] * 5,
        points,
        wind_here,
        partial,
        table,
        hot,
    )
    ahead, back = [], []
    for g in range(GROUPS):
        for i in range(TILES - 1):
            rise, fall = (g * TILES + i, g * TILES + i + 1), (g * TILES + i + 1, g * TILES + i)
            ahead.append(fall if g in (1, 2) else rise)
            back.append(rise if g in (1, 2) else fall)
    below = lax.ppermute(up, ("grp", "comp"), ahead)
    above = lax.ppermute(low, ("grp", "comp"), back)
    return call(
        advect_kernel,
        f32(LOCAL, TROWS, NY),
        [
            pltpu.VMEM((11, 8, NY), jnp.float32),
            pltpu.VMEM((4, ROWS, NY), jnp.float32),
            pltpu.VMEM((2, 8 * TROWS, 128), jnp.float32),
        ],
        [SMEM] + [VMEM] * 6,
        flags,
        table,
        below,
        low,
        mid,
        up,
        above,
    )


def solution(mesh):
    in_specs = (P("grp", "comp"), P("comp"), P("comp"), P("comp"))
    out_specs = P("grp", "comp", None)
    return jax.shard_map(local, mesh=mesh, in_specs=in_specs, out_specs=out_specs, check_vma=False)
```

time: 126 us -> 92.9 us (0.74)
  local copies, waits for them, and re-layouts: 29.8 us -> 3.64 us
  Pallas kernels: 0 us -> 22.8 us
  blocking collectives: 16.9 us -> 0 us
  other arithmetic: 16.1 us -> 0.79 us
  waiting for transfers between devices: 29.1 us -> 35.7 us
  starting transfers between devices: 33.2 us -> 29.3 us
    pallas_call x0 -> x5, Pallas kernels: none -> 22.8 us  [call(): pl.pallas_call(kernel, out_shape=shapes, in_specs=ins, out_specs=jax.tree...]
    psum x1 -> x0, blocking collectives: 16.9 us -> none  [local(): energy, inverse = lax.psum((partial_energy, partial_inverse), 'grp')]
    scatter x2 -> x0, local copies, waits for them, and re-layouts: 14.3 us -> none  [the longest x1 7.98 us: local(): jnp.zeros((local_comps, TROWS * NY), jnp.float32).at[:, sea_cell]]
    mul x11 -> x0, other arithmetic: 11.6 us -> none  [the longest x4 5.49 us: face_flux(): number * (upstream + 0.5 * (1.0 - jnp.abs(number)) * koren_slope(slope_ba...]
    ppermute x4 -> x2, starting transfers between devices: 15.7 us -> 7.67 us  [the longest x1 5.75 us: local(): above = lax.ppermute(low, ('grp', 'comp'), back)]
    all_to_all x1 -> x2, waiting for transfers between devices: 23.4 us -> 29.8 us  [the longest x1 29.1 us: local(): lax.all_to_all(packed.reshape(TILES, 1, SLOTS * 128), 'comp', split_axis=...]
    unnamed x6 -> x2, local copies, waits for them, and re-layouts: 5.64 us -> 1.18 us
    all_to_all x1 -> x2, starting transfers between devices: 17.5 us -> 21.7 us  [the longest x1 17.4 us: local(): lax.all_to_all(packed.reshape(TILES, 1, SLOTS * 128), 'comp', split_axis=...]
  transfers between devices with their start and end apart: 5 -> 4, of which waited for: 5 -> 4; matrix products, arithmetic and copies ran while one was open for 8% -> 2% of each run, Pallas kernels for 0% -> 4%
where the time goes in v1:
time: 92.9 us; the launch traced here: 92.3 us
  waiting for transfers between devices  35.7 us (38%)
  starting transfers between devices  29.3 us (32%)
  Pallas kernels  22.8 us (25%)
  local copies, waits for them, and re-layouts  3.64 us (4%)
    all_to_all x1, waiting for transfers between devices, local(): lax.all_to_all(packed.reshape(TILES, 1, SLOTS * 128), 'comp', split_axis=...  29.1 us
    pallas_call x5, Pallas kernels, call(): pl.pallas_call(kernel, out_shape=shapes, in_specs=ins, out_specs=jax.tree...  22.8 us
    all_to_all x1, starting transfers between devices, local(): lax.all_to_all(packed.reshape(TILES, 1, SLOTS * 128), 'comp', split_axis=...  17.4 us
    ppermute x1, starting transfers between devices, local(): above = lax.ppermute(low, ('grp', 'comp'), back)  5.75 us
    ppermute x1, waiting for transfers between devices, local(): above = lax.ppermute(low, ('grp', 'comp'), back)  4.31 us
    all_to_all x1, starting transfers between devices, local(): lax.all_to_all(partial, 'grp', split_axis=0, concat_axis=0, tiled=True)  4.29 us
    ppermute x1, starting transfers between devices, local(): below = lax.ppermute(up, ('grp', 'comp'), ahead)  1.92 us
  transfers between devices with their start and end apart: 4, of which 4 were waited for; matrix products, arithmetic and copies ran while one was open for 2% of the time, Pallas kernels for 4%

profile of v1, /device:TPU:8, one launch (start us, length us, event | category | flops | bytes accessed | tf_op | source)
XLA Modules:
  0.0 92.3 jit_solution(5247827177234545582)
XLA Ops:
  0.0 0.7 stack.26
  0.7 0.7 stack.27
  1.4 0.0 copy-start
  1.4 1.2 %copy-done = f32[150,1536]{1,0:T(8,128)S(1)} copy-done((f32[150,1536]{1,0:T(8,128)S(1)}, f32[150,1536]{1,0:T(8,128)}, u32[]{:S(2)}) %copy-start) | copy-done | bytes 921624
  2.6 1.7 %shard_map.55 = f32[1920,128]{1,0:T(8,128)} custom-call(f32[150,1536]{1,0:T(8,128)S(1)} %copy-done, f32[2,1536]{1,0:T(2,128)S(1)} %pad_maximum_fusion.wind_ref), custom_call_target="tpu_custom_call" | custom-call | tf_op jit(solution)/shard_map/pallas_call | solution.py:215
  4.3 17.4 %all-to-all-start = ((f32[128,1,1920]{2,1,0:T(1,128)}), f32[128,1,1920]{2,1,0:T(1,128)S(1)}, u32[]{:S(2)}, u32[]{:S(2)}) async-start(f32[128,1,1920]{2,1,0:T(1,128)} %bitcast.3), calls=%async_computation | async-start | bytes 1966080 | tf_op jit(solution)/shard_map/all_to_all | solution.py:244
  21.7 0.9 dynamic-slice_bitcast_fusion.tab_ref
  22.6 29.1 %all-to-all-done = f32[128,1,1920]{2,1,0:T(1,128)S(1)} async-done(((f32[128,1,1920]{2,1,0:T(1,128)}), f32[128,1,1920]{2,1,0:T(1,128)S(1)}, u32[]{:S(2)}, u32[]{:S(2)}) %all-to-all-start) | async-done | bytes 983072 | tf_op jit(solution)/shard_map/all_to_all | solution.py:244
  51.7 1.0 %shard_map.56 = (f32[12,152,128]{2,1,0:T(8,128)S(1)}, f32[24,128]{1,0:T(8,128)S(1)}, f32[4,24,128]{2,1,0:T(8,128)}) custom-call(f32[1920,128]{1,0:T(8,128)S(1)} %bitcast.7, f32[152,128]{1,0:T(8,128)S(1)} %dynamic-slice_bitcast_fusion.tab_ref), custom_call_target="tpu_custom_call" | custom-call | tf_op jit(solution)/shard_map/pallas_call | solution.py:215
  52.7 4.3 %all-to-all-start.1 = ((f32[4,24,128]{2,1,0:T(8,128)}), f32[4,24,128]{2,1,0:T(8,128)S(1)}, u32[]{:S(2)}, u32[]{:S(2)}) async-start(f32[4,24,128]{2,1,0:T(8,128)} %get-tuple-element.13), calls=%async_computation.1 | async-start | bytes 98304 | tf_op jit(solution)/shard_map/all_to_all | solution.py:264
  57.0 0.7 broadcast_xor_fusion
  57.7 0.1 xor.12
  57.8 0.1 copy.8
  57.8 4.0 %shard_map.57.hot_ref = bf16[1536,2048]{1,0:T(8,128)(2,1)} custom-call(s32[12,128]{1,0:T(8,128)S(1)} %bitcast.8), custom_call_target="tpu_custom_call" | custom-call | tf_op jit(solution)/shard_map/pallas_call | solution.py:215
  61.8 0.7 all-to-all-done.1.e_ref
  62.5 5.3 %shard_map.58 = (f32[2,152,256]{2,1,0:T(8,128)S(1)}, f32[2,152,256]{2,1,0:T(8,128)S(1)}, f32[4,152,256]{2,1,0:T(8,128)S(1)}) custom-call(f32[12,152,128]{2,1,0:T(8,128)S(1)} %get-tuple-element.11.y_ref, f32[24,128]{1,0:T(8,128)S(1)} %get-tuple-element.12.wind_ref, f32[4,24,128]{2,1,0:T(8,128)S(1)} %all-to-all-done.1.e_ref, ...), custom_call_target="tpu_custom_call" | custom-call | tf_op jit(solution)/shard_map/pallas_call | solution.py:215
  67.8 1.9 %collective-permute-start = (f32[4,152,256]{2,1,0:T(8,128)S(1)}, f32[4,152,256]{2,1,0:T(8,128)S(1)}, u32[]{:S(2)}, u32[]{:S(2)}) collective-permute-start(f32[4,152,256]{2,1,0:T(8,128)S(1)} %get-tuple-element.14.up_ref), channel_id=1, source_target_pairs={{0,1},{1,2},{2,3},{3,4},{4,5},{5,6},{6,7},{7,8},{8,9},{9,10},{10,1... | collective-permute-start | bytes 1867784 | tf_op jit(solution)/shard_map/ppermute | solution.py:282
  69.7 5.8 %collective-permute-start.1 = (f32[2,152,256]{2,1,0:T(8,128)S(1)}, f32[2,152,256]{2,1,0:T(8,128)S(1)}, u32[]{:S(2)}, u32[]{:S(2)}) collective-permute-start(f32[2,152,256]{2,1,0:T(8,128)S(1)} %get-tuple-element.15.low_ref), channel_id=1, source_target_pairs={{1,0},{2,1},{3,2},{4,3},{5,4},{6,5},{7,6},{8,7},{9,8},{10,9},{11,1... | collective-permute-start | bytes 933896 | tf_op jit(solution)/shard_map/ppermute | solution.py:283
  75.5 0.1 add_convert_fusion.flag_ref
  75.6 4.3 %collective-permute-done.1.above_ref = f32[2,152,256]{2,1,0:T(8,128)S(1)} collective-permute-done((f32[2,152,256]{2,1,0:T(8,128)S(1)}, f32[2,152,256]{2,1,0:T(8,128)S(1)}, u32[]{:S(2)}, u32[]{:S(2)}) %collective-permute-start.1) | collective-permute-done | bytes 311328 | tf_op jit(solution)/shard_map/ppermute | solution.py:283
  79.9 1.6 %collective-permute-done.below_ref = f32[4,152,256]{2,1,0:T(8,128)S(1)} collective-permute-done((f32[4,152,256]{2,1,0:T(8,128)S(1)}, f32[4,152,256]{2,1,0:T(8,128)S(1)}, u32[]{:S(2)}, u32[]{:S(2)}) %collective-permute-start) | collective-permute-done | bytes 622624 | tf_op jit(solution)/shard_map/ppermute | solution.py:282
  81.5 10.9 %shard_map.59 = f32[150,8,256]{2,1,0:T(8,128)} custom-call(s32[2]{0:T(128)S(1)} %add_convert_fusion.flag_ref, f32[152,128]{1,0:T(8,128)S(1)} %dynamic-slice_bitcast_fusion.tab_ref, f32[4,152,256]{2,1,0:T(8,128)S(1)} %collective-permute-done.below_ref, f32[2,152,256]{2,1,0:T(8,128)S(1)} %get-tuple-element.15.low_ref, ...), custom_call_target="tpu_custom_call" | custom-call | tf_op jit(solution)/shard_map/pallas_call | solution.py:215
  (1 shorter events, 0.0 us)
Async XLA Ops:
  1.4 1.2 %copy-start = (f32[150,1536]{1,0:T(8,128)S(1)}, f32[150,1536]{1,0:T(8,128)}, u32[]{:S(2)}) copy-start(f32[150,1536]{1,0:T(8,128)} %x_ref.1) | copy-start | bytes 2764804
  4.3 47.4 %all-to-all-start = ((f32[128,1,1920]{2,1,0:T(1,128)}), f32[128,1,1920]{2,1,0:T(1,128)S(1)}, u32[]{:S(2)}, u32[]{:S(2)}) async-start(f32[128,1,1920]{2,1,0:T(1,128)} %bitcast.3), calls=%async_computation | async-start | bytes 1966080 | tf_op jit(solution)/shard_map/all_to_all | solution.py:244
  52.7 9.8 %all-to-all-start.1 = ((f32[4,24,128]{2,1,0:T(8,128)}), f32[4,24,128]{2,1,0:T(8,128)S(1)}, u32[]{:S(2)}, u32[]{:S(2)}) async-start(f32[4,24,128]{2,1,0:T(8,128)} %get-tuple-element.13), calls=%async_computation.1 | async-start | bytes 98304 | tf_op jit(solution)/shard_map/all_to_all | solution.py:264
  67.8 13.7 %collective-permute-start = (f32[4,152,256]{2,1,0:T(8,128)S(1)}, f32[4,152,256]{2,1,0:T(8,128)S(1)}, u32[]{:S(2)}, u32[]{:S(2)}) collective-permute-start(f32[4,152,256]{2,1,0:T(8,128)S(1)} %get-tuple-element.14.up_ref), channel_id=1, source_target_pairs={{0,1},{1,2},{2,3},{3,4},{4,5},{5,6},{6,7},{7,8},{8,9},{9,10},{10,1... | collective-permute-start | bytes 1867784 | tf_op jit(solution)/shard_map/ppermute | solution.py:282
  69.7 10.2 %collective-permute-start.1 = (f32[2,152,256]{2,1,0:T(8,128)S(1)}, f32[2,152,256]{2,1,0:T(8,128)S(1)}, u32[]{:S(2)}, u32[]{:S(2)}) collective-permute-start(f32[2,152,256]{2,1,0:T(8,128)S(1)} %get-tuple-element.15.low_ref), channel_id=1, source_target_pairs={{1,0},{2,1},{3,2},{4,3},{5,4},{6,5},{7,6},{8,7},{9,8},{10,9},{11,1... | collective-permute-start | bytes 933896 | tf_op jit(solution)/shard_map/ppermute | solution.py:283

commit v2 on v1

--- a/solution.py
+++ b/solution.py
@@ -19,6 +19,7 @@
 TILES = 128
 LOCAL = DIRS * FREQ // GROUPS
 ROWS = 152
+DEPTH = 160
 MASK_ROW = LOCAL
 MAIN = 128
 EXTRA = ROWS - MAIN
@@ -30,7 +31,6 @@
 
 VMEM = pl.BlockSpec(memory_space=pltpu.VMEM)
 SMEM = pl.BlockSpec(memory_space=pltpu.SMEM)
-BIG = pltpu.CompilerParams(vmem_limit_bytes=48 * 1024 * 1024)
 
 W_E, W_I, C_COS, C_SIN, C_OUT, U_X, K_X, U_Y, K_Y = range(9)
 
@@ -54,9 +54,12 @@
     return table.astype(np.float32)
 
 
-def pack_kernel(x_ref, wind_ref, out_ref, z_ref, b_ref):
+def pack_kernel(x_ref, speed_ref, heading_ref, out_ref, z_ref, b_ref):
     b_ref[0 : LOCAL - MAIN, :] = x_ref[MAIN:LOCAL, :]
-    b_ref[LOCAL - MAIN : EXTRA, :] = wind_ref[...]
+    for block in range(SEA // 128):
+        cols = slice(block * 128, block * 128 + 128)
+        b_ref[LOCAL - MAIN : LOCAL - MAIN + 1, cols] = speed_ref[block : block + 1, :]
+        b_ref[LOCAL - MAIN + 1 : EXTRA, cols] = heading_ref[block : block + 1, :]
     b_ref[EXTRA:128, :] = jnp.zeros((128 - EXTRA, SEA), jnp.float32)
     for block in range(SEA // 128):
         cols = slice(block * 128, block * 128 + 128)
@@ -101,12 +104,17 @@
         cell = jnp.broadcast_to(cell_ref[k : k + 1, :], (128, 128)).T
         for tile in range(TROWS * NY // 128):
             hit = cell == lane + tile * 128
-            out_ref[k * 128 : (k + 1) * 128, tile * 128 : (tile + 1) * 128] = jnp.where(
-                hit, 1.0, 0.0
-            ).astype(jnp.bfloat16)
-
-
-def place_kernel(y_ref, wind_ref, e_ref, tab_ref, hot_ref, low_ref, mid_ref, up_ref, s_ref):
+            lanes = slice(tile % 8 * 128, tile % 8 * 128 + 128)
+            out_ref[tile // 8, k * 128 : (k + 1) * 128, lanes] = jnp.where(hit, 1.0, 0.0).astype(
+                jnp.bfloat16
+            )
+
+
+def place_kernel(y_ref, wind_ref, e_ref, tab_ref, hot_ref, low_ref, mid_ref, up_ref, s_ref,
+                 held_ref, sem):
+    copies = [pltpu.make_async_copy(hot_ref.at[h], held_ref.at[h], sem.at[h]) for h in range(2)]
+    copies[1].start()
+    copies[0].start()
     moments = e_ref[0] + e_ref[1] + e_ref[2] + e_ref[3]
     energy, inverse = moments[0:SEND], moments[SEND : 2 * SEND]
     mean = energy / inverse
@@ -121,25 +129,29 @@
     csin = jnp.broadcast_to(tab_ref[:, C_SIN : C_SIN + 1], (ROWS, 128))
     cout = jnp.broadcast_to(tab_ref[:, C_OUT : C_OUT + 1], (ROWS, 128))
     row = lax.broadcasted_iota(jnp.int32, (ROWS, 128), 0)
+    s_ref[ROWS:DEPTH, :] = jnp.zeros((DEPTH - ROWS, SEA), jnp.float32)
     for k in range(SEND):
         grow = ccos * along[k : k + 1] + csin * across[k : k + 1]
         rate = jnp.maximum(grow - 0.1, 0.0) - cout * decay[k : k + 1]
         value = y_ref[k] * jnp.exp(rate)
         value = jnp.where(row < LOCAL, value, jnp.where(row == MASK_ROW, 1.0, 0.0))
-        s_ref[:, k * 128 : (k + 1) * 128] = value
+        s_ref[0:ROWS, k * 128 : (k + 1) * 128] = value
     value = s_ref[...]
     high = value.astype(jnp.bfloat16)
     rest = (value - high.astype(jnp.float32)).astype(jnp.bfloat16)
-    for e in range(TROWS):
-        hot = hot_ref[:, e * NY : (e + 1) * NY]
-        out = jnp.dot(high, hot, preferred_element_type=jnp.float32)
-        out = out + jnp.dot(rest, hot, preferred_element_type=jnp.float32)
-        if e < 2:
-            low_ref[e] = out
-        elif e < 4:
-            mid_ref[e - 2] = out
-        else:
-            up_ref[e - 4] = out
+    both = jnp.concatenate([high, rest], axis=0)
+    for half in (1, 0):
+        copies[half].wait()
+        for i in range(4):
+            hot = held_ref[half, :, i * NY : (i + 1) * NY]
+            out = jnp.dot(both, hot, preferred_element_type=jnp.float32)
+            out = out[0:ROWS] + out[DEPTH : DEPTH + ROWS]
+            if half == 1:
+                up_ref[i] = out
+            elif i < 2:
+                low_ref[i] = out
+            else:
+                mid_ref[i - 2] = out
 
 
 def limited(a, b):
@@ -211,14 +223,14 @@
         sweep(False)
 
 
-def call(kernel, shapes, scratch, ins, *args):
+def call(kernel, shapes, scratch, ins, *args, limit=20):
     return pl.pallas_call(
         kernel,
         out_shape=shapes,
         in_specs=ins,
         out_specs=jax.tree.map(lambda _: VMEM, shapes),
         scratch_shapes=scratch,
-        compiler_params=BIG,
+        compiler_params=pltpu.CompilerParams(vmem_limit_bytes=limit * 1024 * 1024),
     )(*args)
 
 
@@ -232,14 +244,14 @@
     mirror_x = ((group == 1) | (group == 2)).astype(jnp.int32)
     mirror_y = (group >= 2).astype(jnp.int32)
     flags = jnp.stack([mirror_x, mirror_y])
-    wind = jnp.stack([wind_speed, wind_dir])
     packed = call(
         pack_kernel,
         f32(TILES * SLOTS, 128),
         [pltpu.VMEM((2, SEA, 128), jnp.float32), pltpu.VMEM((128, SEA), jnp.float32)],
-        [VMEM] * 2,
+        [VMEM] * 3,
         spectra,
-        wind,
+        wind_speed.reshape(SEA // 128, 128),
+        wind_dir.reshape(SEA // 128, 128),
     )
     received = lax.all_to_all(
         packed.reshape(TILES, 1, SLOTS * 128), "comp", split_axis=0, concat_axis=0, tiled=True
@@ -248,11 +260,12 @@
     cells = cells ^ (mirror_x * (NY * (TROWS - 1)))
     hot = call(
         onehot_kernel,
-        jax.ShapeDtypeStruct((SEA, TROWS * NY), jnp.bfloat16),
+        jax.ShapeDtypeStruct((2, SEA, 4 * NY), jnp.bfloat16),
         [],
         [VMEM],
         cells,
     )
+    received, hot = lax.optimization_barrier((received, hot))
     points, wind_here, partial = call(
         moments_kernel,
         (f32(SEND, ROWS, 128), f32(2 * SEND, 128), f32(GROUPS, 2 * SEND, 128)),
@@ -265,13 +278,18 @@
     low, mid, up = call(
         place_kernel,
         (f32(2, ROWS, NY), f32(2, ROWS, NY), f32(4, ROWS, NY)),
-        [pltpu.VMEM((ROWS, SEA), jnp.float32)],
-        [VMEM] * 5,
+        [
+            pltpu.VMEM((DEPTH, SEA), jnp.float32),
+            pltpu.VMEM((2, SEA, 4 * NY), jnp.bfloat16),
+            pltpu.SemaphoreType.DMA((2,)),
+        ],
+        [VMEM] * 4 + [pl.BlockSpec(memory_space=pltpu.HBM)],
         points,
         wind_here,
         partial,
         table,
         hot,
+        limit=50,
     )
     ahead, back = [], []
     for g in range(GROUPS):

time: 92.9 us -> 91.2 us (0.982)
  blocking collectives: 0 us -> 9.63 us
  waiting for transfers between devices: 35.7 us -> 30.2 us
  starting transfers between devices: 29.3 us -> 25 us
  Pallas kernels: 22.8 us -> 18.7 us
  local copies, waits for them, and re-layouts: 3.64 us -> 6.29 us
    all_to_all x0 -> x1, blocking collectives: none -> 9.63 us  [local(): lax.all_to_all(partial, 'grp', split_axis=0, concat_axis=0, tiled=True)]
    all_to_all x1, waiting for transfers between devices: 29.1 us -> 24.3 us  [local(): lax.all_to_all(packed.reshape(TILES, 1, SLOTS * 128), 'comp', split_axis=...]
    all_to_all x1 -> x0, starting transfers between devices: 4.29 us -> none  [local(): lax.all_to_all(partial, 'grp', split_axis=0, concat_axis=0, tiled=True)]
    unnamed x2 -> x8, local copies, waits for them, and re-layouts: 1.18 us -> 5.24 us
    pallas_call x5, Pallas kernels: 22.8 us -> 18.7 us  [call(): pl.pallas_call(kernel, out_shape=shapes, in_specs=ins, out_specs=jax.tree...]
    another operation x2 -> x0, local copies, waits for them, and re-layouts: 1.4 us -> none  [local(): wind = jnp.stack([wind_speed, wind_dir])]
  transfers between devices with their start and end apart: 4 -> 3, of which waited for: 4 -> 3; matrix products, arithmetic and copies ran while one was open for 2% -> 2% of each run, Pallas kernels for 4% -> 1%
where the time goes in v2:
time: 91.2 us; the launch traced here: 90.7 us
  waiting for transfers between devices  30.2 us (33%)
  starting transfers between devices  25 us (27%)
  Pallas kernels  18.7 us (21%)
  blocking collectives  9.63 us (11%)
  local copies, waits for them, and re-layouts  6.29 us (7%)
    all_to_all x1, waiting for transfers between devices, local(): lax.all_to_all(packed.reshape(TILES, 1, SLOTS * 128), 'comp', split_axis=...  24.3 us
    pallas_call x5, Pallas kernels, call(): pl.pallas_call(kernel, out_shape=shapes, in_specs=ins, out_specs=jax.tree...  18.7 us
    all_to_all x1, starting transfers between devices, local(): lax.all_to_all(packed.reshape(TILES, 1, SLOTS * 128), 'comp', split_axis=...  17.4 us
    all_to_all x1, blocking collectives, local(): lax.all_to_all(partial, 'grp', split_axis=0, concat_axis=0, tiled=True)  9.63 us
    ppermute x1, starting transfers between devices, local(): above = lax.ppermute(low, ('grp', 'comp'), back)  5.75 us
    unnamed x8, local copies, waits for them, and re-layouts  5.24 us
    ppermute x1, waiting for transfers between devices, local(): above = lax.ppermute(low, ('grp', 'comp'), back)  4.31 us
    ppermute x1, starting transfers between devices, local(): below = lax.ppermute(up, ('grp', 'comp'), ahead)  1.92 us
  transfers between devices with their start and end apart: 3, of which 3 were waited for; matrix products, arithmetic and copies ran while one was open for 2% of the time, Pallas kernels for 1%

profile of v2, /device:TPU:8, one launch (start us, length us, event | category | flops | bytes accessed | tf_op | source)
XLA Modules:
  0.0 90.7 jit_solution(8635530326883163249)
XLA Ops:
  0.0 0.0 copy-start.1
  0.0 1.2 %copy-done.1 = f32[150,1536]{1,0:T(8,128)S(1)} copy-done((f32[150,1536]{1,0:T(8,128)S(1)}, f32[150,1536]{1,0:T(8,128)}, u32[]{:S(2)}) %copy-start.1) | copy-done | bytes 921624
  1.2 0.0 copy-start.2
  1.2 0.7 copy-done.2
  1.9 0.0 copy-start.3
  1.9 0.7 copy-done.3
  2.6 1.7 %shard_map.55 = f32[1920,128]{1,0:T(8,128)} custom-call(f32[150,1536]{1,0:T(8,128)S(1)} %copy-done.1, f32[12,128]{1,0:T(8,128)S(1)} %bitcast.11, f32[12,128]{1,0:T(8,128)S(1)} %bitcast.12), custom_call_target="tpu_custom_call" | custom-call | tf_op jit(solution)/shard_map/pallas_call | solution.py:227
  4.2 17.4 %all-to-all-start = ((f32[128,1,1920]{2,1,0:T(1,128)}), f32[128,1,1920]{2,1,0:T(1,128)S(1)}, u32[]{:S(2)}, u32[]{:S(2)}) async-start(f32[128,1,1920]{2,1,0:T(1,128)} %bitcast.5), calls=%async_computation | async-start | bytes 1966080 | tf_op jit(solution)/shard_map/all_to_all | solution.py:256
  21.6 0.7 broadcast_xor_fusion
  22.3 0.1 xor.12
  22.4 0.1 copy.8
  22.5 1.3 %shard_map.56.hot_ref = bf16[2,1536,1024]{2,1,0:T(8,128)(2,1)S(1)} custom-call(s32[12,128]{1,0:T(8,128)S(1)} %bitcast.10), custom_call_target="tpu_custom_call" | custom-call | tf_op jit(solution)/shard_map/pallas_call | solution.py:227
  23.8 0.0 copy-start
  23.8 2.7 %copy-done = bf16[2,1536,1024]{2,1,0:T(8,128)(2,1)} copy-done((bf16[2,1536,1024]{2,1,0:T(8,128)(2,1)}, bf16[2,1536,1024]{2,1,0:T(8,128)(2,1)S(1)}, u32[]{:S(2)}) %copy-start) | copy-done | bytes 6291480
  26.5 0.9 dynamic-slice_bitcast_fusion.tab_ref
  27.4 24.3 %all-to-all-done = f32[128,1,1920]{2,1,0:T(1,128)S(1)} async-done(((f32[128,1,1920]{2,1,0:T(1,128)}), f32[128,1,1920]{2,1,0:T(1,128)S(1)}, u32[]{:S(2)}, u32[]{:S(2)}) %all-to-all-start) | async-done | bytes 983072 | tf_op jit(solution)/shard_map/all_to_all | solution.py:256
  51.6 0.4 shard_map.57
  52.0 9.6 %all_to_all.10.e_ref = f32[4,24,128]{2,1,0:T(8,128)S(1)} all-to-all(f32[4,24,128]{2,1,0:T(8,128)S(1)} %get-tuple-element.16), channel_id=1, replica_groups=mesh['grp'=4,'comp'=128] {'grp'}, dimensions={0} | all-to-all | bytes 98304 | tf_op jit(solution)/shard_map/all_to_all | solution.py:277
  61.7 4.5 %shard_map.58 = (f32[2,152,256]{2,1,0:T(8,128)S(1)}, f32[2,152,256]{2,1,0:T(8,128)S(1)}, f32[4,152,256]{2,1,0:T(8,128)S(1)}) custom-call(f32[12,152,128]{2,1,0:T(8,128)S(1)} %get-tuple-element.14.y_ref, f32[24,128]{1,0:T(8,128)S(1)} %get-tuple-element.15.wind_ref, f32[4,24,128]{2,1,0:T(8,128)S(1)} %all_to_all.10.e_ref, ...), custom_call_target="tpu_custom_call" | custom-call | tf_op jit(solution)/shard_map/pallas_call | solution.py:227
  66.2 1.9 %collective-permute-start = (f32[4,152,256]{2,1,0:T(8,128)S(1)}, f32[4,152,256]{2,1,0:T(8,128)S(1)}, u32[]{:S(2)}, u32[]{:S(2)}) collective-permute-start(f32[4,152,256]{2,1,0:T(8,128)S(1)} %get-tuple-element.18.up_ref), channel_id=1, source_target_pairs={{0,1},{1,2},{2,3},{3,4},{4,5},{5,6},{6,7},{7,8},{8,9},{9,10},{10,1... | collective-permute-start | bytes 1867784 | tf_op jit(solution)/shard_map/ppermute | solution.py:300
  68.1 5.8 %collective-permute-start.1 = (f32[2,152,256]{2,1,0:T(8,128)S(1)}, f32[2,152,256]{2,1,0:T(8,128)S(1)}, u32[]{:S(2)}, u32[]{:S(2)}) collective-permute-start(f32[2,152,256]{2,1,0:T(8,128)S(1)} %get-tuple-element.19.low_ref), channel_id=1, source_target_pairs={{1,0},{2,1},{3,2},{4,3},{5,4},{6,5},{7,6},{8,7},{9,8},{10,9},{11,1... | collective-permute-start | bytes 933896 | tf_op jit(solution)/shard_map/ppermute | solution.py:301
  73.9 0.1 add_convert_fusion.flag_ref
  74.0 4.3 %collective-permute-done.1.above_ref = f32[2,152,256]{2,1,0:T(8,128)S(1)} collective-permute-done((f32[2,152,256]{2,1,0:T(8,128)S(1)}, f32[2,152,256]{2,1,0:T(8,128)S(1)}, u32[]{:S(2)}, u32[]{:S(2)}) %collective-permute-start.1) | collective-permute-done | bytes 311328 | tf_op jit(solution)/shard_map/ppermute | solution.py:301
  78.3 1.6 %collective-permute-done.below_ref = f32[4,152,256]{2,1,0:T(8,128)S(1)} collective-permute-done((f32[4,152,256]{2,1,0:T(8,128)S(1)}, f32[4,152,256]{2,1,0:T(8,128)S(1)}, u32[]{:S(2)}, u32[]{:S(2)}) %collective-permute-start) | collective-permute-done | bytes 622624 | tf_op jit(solution)/shard_map/ppermute | solution.py:300
  79.9 10.9 %shard_map.59 = f32[150,8,256]{2,1,0:T(8,128)} custom-call(s32[2]{0:T(128)S(1)} %add_convert_fusion.flag_ref, f32[152,128]{1,0:T(8,128)S(1)} %dynamic-slice_bitcast_fusion.tab_ref, f32[4,152,256]{2,1,0:T(8,128)S(1)} %collective-permute-done.below_ref, f32[2,152,256]{2,1,0:T(8,128)S(1)} %get-tuple-element.19.low_ref, ...), custom_call_target="tpu_custom_call" | custom-call | tf_op jit(solution)/shard_map/pallas_call | solution.py:227
Async XLA Ops:
  0.0 1.2 %copy-start.1 = (f32[150,1536]{1,0:T(8,128)S(1)}, f32[150,1536]{1,0:T(8,128)}, u32[]{:S(2)}) copy-start(f32[150,1536]{1,0:T(8,128)} %x_ref.1) | copy-start | bytes 2764804
  1.2 0.7 copy-start.2
  1.9 0.7 copy-start.3
  4.2 47.4 %all-to-all-start = ((f32[128,1,1920]{2,1,0:T(1,128)}), f32[128,1,1920]{2,1,0:T(1,128)S(1)}, u32[]{:S(2)}, u32[]{:S(2)}) async-start(f32[128,1,1920]{2,1,0:T(1,128)} %bitcast.5), calls=%async_computation | async-start | bytes 1966080 | tf_op jit(solution)/shard_map/all_to_all | solution.py:256
  23.8 2.7 %copy-start = (bf16[2,1536,1024]{2,1,0:T(8,128)(2,1)}, bf16[2,1536,1024]{2,1,0:T(8,128)(2,1)S(1)}, u32[]{:S(2)}) copy-start(bf16[2,1536,1024]{2,1,0:T(8,128)(2,1)S(1)} %shard_map.56.hot_ref) | copy-start | bytes 18874372
  66.2 13.7 %collective-permute-start = (f32[4,152,256]{2,1,0:T(8,128)S(1)}, f32[4,152,256]{2,1,0:T(8,128)S(1)}, u32[]{:S(2)}, u32[]{:S(2)}) collective-permute-start(f32[4,152,256]{2,1,0:T(8,128)S(1)} %get-tuple-element.18.up_ref), channel_id=1, source_target_pairs={{0,1},{1,2},{2,3},{3,4},{4,5},{5,6},{6,7},{7,8},{8,9},{9,10},{10,1... | collective-permute-start | bytes 1867784 | tf_op jit(solution)/shard_map/ppermute | solution.py:300
  68.1 10.2 %collective-permute-start.1 = (f32[2,152,256]{2,1,0:T(8,128)S(1)}, f32[2,152,256]{2,1,0:T(8,128)S(1)}, u32[]{:S(2)}, u32[]{:S(2)}) collective-permute-start(f32[2,152,256]{2,1,0:T(8,128)S(1)} %get-tuple-element.19.low_ref), channel_id=1, source_target_pairs={{1,0},{2,1},{3,2},{4,3},{5,4},{6,5},{7,6},{8,7},{9,8},{10,9},{11,1... | collective-permute-start | bytes 933896 | tf_op jit(solution)/shard_map/ppermute | solution.py:301

commit v3 on v2

--- a/solution.py
+++ b/solution.py
@@ -20,7 +20,6 @@
 LOCAL = DIRS * FREQ // GROUPS
 ROWS = 152
 DEPTH = 160
-MASK_ROW = LOCAL
 MAIN = 128
 EXTRA = ROWS - MAIN
 PER_TILE = 5
@@ -32,11 +31,17 @@
 VMEM = pl.BlockSpec(memory_space=pltpu.VMEM)
 SMEM = pl.BlockSpec(memory_space=pltpu.SMEM)
 
-W_E, W_I, C_COS, C_SIN, C_OUT, U_X, K_X, U_Y, K_Y = range(9)
-
-
-def coefficient_table():
+W_E, W_I, C_COS, C_SIN, C_OUT = range(5)
+PHASES = 32
+PACKS = 4
+SHORT = PHASES // PACKS
+LINES = (PHASES + SHORT) * 8
+CHUNK = 4
+
+
+def coefficient_tables():
     table = np.zeros((GROUPS, ROWS, 128), np.float64)
+    courant = np.zeros((GROUPS, 8, 256), np.float64)
     for group in range(GROUPS):
         for row in range(LOCAL):
             d, j = row // FREQ + group * (DIRS // GROUPS), row % FREQ
@@ -47,11 +52,16 @@
             reach = 0.45 * (2.0 * math.pi * LOW_FREQ) / s
             ux, uy = abs(reach * math.cos(angle)), abs(reach * math.sin(angle))
             push = 0.1 * 28.0 * 0.035 * s / GRAV
-            table[group, row, :9] = (
-                w, w / s, push * math.cos(angle), push * math.sin(angle), 0.4 * s * s,
-                ux, ux * (1.0 - ux), uy, uy * (1.0 - uy),
+            table[group, row, :5] = (
+                w, w / s, push * math.cos(angle), push * math.sin(angle), 0.4 * s * s
             )
-    return table.astype(np.float32)
+            if row < MAIN:
+                lanes = [row]
+            else:
+                lanes = [128 + pack * 32 + row - MAIN for pack in range(PACKS)]
+            for lane in lanes:
+                courant[group, :4, lane] = (ux, ux * (1.0 - ux), uy, uy * (1.0 - uy))
+    return table.astype(np.float32), courant.astype(np.float32)
 
 
 def pack_kernel(x_ref, speed_ref, heading_ref, out_ref, z_ref, b_ref):
@@ -99,20 +109,31 @@
 
 
 def onehot_kernel(cell_ref, out_ref):
-    lane = lax.broadcasted_iota(jnp.int32, (128, 128), 1)
-    for k in range(SEND):
-        cell = jnp.broadcast_to(cell_ref[k : k + 1, :], (128, 128)).T
-        for tile in range(TROWS * NY // 128):
-            hit = cell == lane + tile * 128
-            lanes = slice(tile % 8 * 128, tile % 8 * 128 + 128)
-            out_ref[tile // 8, k * 128 : (k + 1) * 128, lanes] = jnp.where(hit, 1.0, 0.0).astype(
-                jnp.bfloat16
-            )
+    row = lax.broadcasted_iota(jnp.int32, (16, 128), 0)
+    base = row % 8 * 32 + row // 8
+    spots = [cell_ref[k : k + 1, :] - base for k in range(SEND)]
+
+    def body(e, carry):
+        for phase in range(0, PHASES, 2):
+            pack, short = phase // SHORT, phase % SHORT
+            line = ((e // 4 * PACKS + pack) * 4 + e % 4) * SHORT * 8 + short * 8
+            for k in range(SEND):
+                hit = spots[k] == e * NY + phase
+                out_ref[pl.ds(pl.multiple_of(line, 16), 16), k * 128 : (k + 1) * 128] = jnp.where(
+                    hit, 1.0, 0.0
+                ).astype(jnp.bfloat16)
+        return carry
+
+    lax.fori_loop(0, TROWS, body, 0)
 
 
 def place_kernel(y_ref, wind_ref, e_ref, tab_ref, hot_ref, low_ref, mid_ref, up_ref, s_ref,
-                 held_ref, sem):
-    copies = [pltpu.make_async_copy(hot_ref.at[h], held_ref.at[h], sem.at[h]) for h in range(2)]
+                 held_ref, side_ref, sem):
+    half = TROWS * NY // 2
+    copies = [
+        pltpu.make_async_copy(hot_ref.at[pl.ds(h * half, half)], held_ref.at[h], sem.at[h])
+        for h in range(2)
+    ]
     copies[1].start()
     copies[0].start()
     moments = e_ref[0] + e_ref[1] + e_ref[2] + e_ref[3]
@@ -134,93 +155,175 @@
         grow = ccos * along[k : k + 1] + csin * across[k : k + 1]
         rate = jnp.maximum(grow - 0.1, 0.0) - cout * decay[k : k + 1]
         value = y_ref[k] * jnp.exp(rate)
-        value = jnp.where(row < LOCAL, value, jnp.where(row == MASK_ROW, 1.0, 0.0))
+        value = jnp.where(row < LOCAL, value, 0.0)
         s_ref[0:ROWS, k * 128 : (k + 1) * 128] = value
     value = s_ref[...]
     high = value.astype(jnp.bfloat16)
     rest = (value - high.astype(jnp.float32)).astype(jnp.bfloat16)
-    both = jnp.concatenate([high, rest], axis=0)
-    for half in (1, 0):
-        copies[half].wait()
-        for i in range(4):
-            hot = held_ref[half, :, i * NY : (i + 1) * NY]
-            out = jnp.dot(both, hot, preferred_element_type=jnp.float32)
-            out = out[0:ROWS] + out[DEPTH : DEPTH + ROWS]
-            if half == 1:
-                up_ref[i] = out
-            elif i < 2:
-                low_ref[i] = out
-            else:
-                mid_ref[i - 2] = out
+    main = jnp.concatenate([high[0:MAIN], rest[0:MAIN]], axis=0)
+    side_ref[...] = jnp.zeros(side_ref.shape, jnp.bfloat16)
+    for pack in range(PACKS):
+        side_ref[pack, pack * 32 : pack * 32 + 32, :] = high[MAIN:DEPTH]
+        side_ref[pack, 128 + pack * 32 : 128 + pack * 32 + 32, :] = rest[MAIN:DEPTH]
+    turned = (((1,), (1,)), ((), ()))
+    block = SHORT * 8
+    for h in (1, 0):
+        copies[h].wait()
+        refs = [(up_ref, i) for i in range(4)]
+        if h == 0:
+            refs = [(low_ref, 0), (low_ref, 1), (mid_ref, 0), (mid_ref, 1)]
+        out = lax.dot_general(held_ref[h], main, turned, preferred_element_type=jnp.float32)
+        out = out[:, 0:128] + out[:, 128:256]
+        for pack in range(PACKS):
+            for i, (ref, at) in enumerate(refs):
+                line = (pack * 4 + i) * block
+                ref[at, pack * block : (pack + 1) * block, :] = out[line : line + block]
+        total = None
+        for pack in range(PACKS):
+            hot = held_ref[h, pack * 4 * block : (pack + 1) * 4 * block, :]
+            out = lax.dot_general(hot, side_ref[pack], turned, preferred_element_type=jnp.float32)
+            total = out if total is None else total + out
+        total = total[:, 0:128] + total[:, 128:256]
+        for i, (ref, at) in enumerate(refs):
+            ref[at, PHASES * 8 : LINES, :] = total[i * block : (i + 1) * block]
 
 
 def limited(a, b):
     m = (a + (b + b)) * (1.0 / 6.0)
-    rising = jnp.maximum(jnp.minimum(m, jnp.minimum(a, b)), 0.0)
-    falling = jnp.minimum(jnp.maximum(m, jnp.maximum(a, b)), 0.0)
-    return rising + falling
-
-
-def advance(q, mask, coef, forward):
+    least = jnp.minimum(jnp.maximum(a, b), 0.0)
+    most = jnp.maximum(jnp.minimum(a, b), 0.0)
+    return jnp.minimum(jnp.maximum(m, least), most)
+
+
+def next_main(x):
+    return pltpu.roll(x, 7, 0)
+
+
+def last_main(x):
+    return pltpu.roll(x, 1, 0)
+
+
+def next_side(x):
+    lane = lax.broadcasted_iota(jnp.int32, (8, 128), 1)
+    x = pltpu.roll(x, 96, 1)
+    return jnp.where(lane >= 96, pltpu.roll(x, 7, 0), x)
+
+
+def last_side(x):
+    lane = lax.broadcasted_iota(jnp.int32, (8, 128), 1)
+    x = pltpu.roll(x, 32, 1)
+    return jnp.where(lane < 32, pltpu.roll(x, 1, 0), x)
+
+
+def substep(rows, seas, put, keep_ref, coef, base, phases, after, before):
     ux, kx, uy, ky = coef
-    step, back = (NY - 1, 1) if forward else (1, NY - 1)
-    diff = [q[i + 1] - q[i] for i in range(len(q) - 1)]
-    flux = [None] + [
-        ux * q[i] + kx * limited(diff[i - 1], diff[i]) for i in range(1, len(q) - 1)
-    ]
-    new = []
-    for i in range(2, len(q) - 1):
-        ahead = pltpu.roll(q[i], step, 1) - q[i]
-        behind = pltpu.roll(ahead, back, 1)
-        side = uy * q[i] + ky * limited(behind, ahead)
-        div = (flux[i] - flux[i - 1]) + (side - pltpu.roll(side, back, 1))
-        new.append((q[i] - div) * mask[i - 2])
-    return new
+    count = len(rows) - 3
+
+    def load(spot, phase):
+        ref, at = spot
+        return ref[at, pl.ds(pl.multiple_of(base + phase * 8, 8), 8), :]
+
+    for i in range(count):
+        spot = rows[i + 2]
+        end = load(spot, phases - 1)
+        ahead = load(spot, 0) - before(end)
+        prior = before(end - load(spot, phases - 2))
+        keep_ref[i, 0] = ahead
+        keep_ref[i, 1] = uy * before(end) + ky * limited(prior, ahead)
+
+    def body(chunk, carry):
+        first = chunk * CHUNK
+        following = jnp.where(first + CHUNK == phases, 0, first + CHUNK)
+        wraps = first + CHUNK == phases
+        q = [load(rows[1], first + j) for j in range(CHUNK)]
+        diff = [q[j] - load(rows[0], first + j) for j in range(CHUNK)]
+        flux = None
+        for i in range(-1, count):
+            up = [load(rows[i + 3], first + j) for j in range(CHUNK)]
+            slope = [up[j] - q[j] for j in range(CHUNK)]
+            gone = [ux * q[j] + kx * limited(diff[j], slope[j]) for j in range(CHUNK)]
+            if i >= 0:
+                behind, past = keep_ref[i, 0], keep_ref[i, 1]
+                edge = load(rows[i + 2], following)
+                edge = jnp.where(wraps, after(edge), edge)
+                for j in range(CHUNK):
+                    ahead = (q[j + 1] if j + 1 < CHUNK else edge) - q[j]
+                    side = uy * q[j] + ky * limited(behind, ahead)
+                    new = q[j] - ((gone[j] - flux[j]) + (side - past))
+                    sea = q[j] if seas is None else load(seas[i], first + j)
+                    put(i, first + j, jnp.where(sea > 0.0, new, 0.0))
+                    behind, past = ahead, side
+                keep_ref[i, 0] = behind
+                keep_ref[i, 1] = past
+            q, diff, flux = up, slope, gone
+        return carry
+
+    lax.fori_loop(0, phases // CHUNK, body, 0)
 
 
 def advect_kernel(flag_ref, tab_ref, below_ref, low_ref, mid_ref, up_ref, above_ref, out_ref,
-                  mask_ref, coef_ref, turn_ref):
+                  once_ref, twice_ref, keep_ref, turn_ref, rest_ref):
     cells = [(below_ref, i) for i in range(4)] + [(low_ref, i) for i in range(2)]
     cells += [(mid_ref, i) for i in range(2)] + [(up_ref, i) for i in range(4)]
     cells += [(above_ref, i) for i in range(2)]
-    for i in range(2, 13):
-        ref, at = cells[i]
-        mask_ref[i - 2] = jnp.broadcast_to(ref[at, MASK_ROW : MASK_ROW + 1, :], (8, NY))
-    for n, column in enumerate((U_X, K_X, U_Y, K_Y)):
-        coef_ref[n] = jnp.broadcast_to(tab_ref[:, column : column + 1], (ROWS, NY))
-    mirrored = flag_ref[0]
-
-    def tile(start, count, forward):
-        rows = pl.ds(start, 8)
-        q = [ref[at, rows, :] for ref, at in cells]
-        coef = [coef_ref[n, rows, :] for n in range(4)]
-        q = advance(q, [mask_ref[i] for i in range(11)], coef, forward)
-        q = advance(q, [mask_ref[i] for i in range(2, 10)], coef, forward)
-        for e in range(TROWS):
-            r = e + (TROWS - 1 - 2 * e) * mirrored
-            for half in range(2):
-                turn_ref[half, pl.ds(r, 8, stride=TROWS), :] = q[e][:, half * 128 : half * 128 + 128]
-        for i in range(count):
-            for half in range(2):
-                out_ref[start + i, :, half * 128 : half * 128 + 128] = turn_ref[
-                    half, i * TROWS : (i + 1) * TROWS, :
-                ]
-
-    def sweep(forward):
-        def body(i, carry):
-            tile(pl.multiple_of(i * 8, 8), 8, forward)
-            return carry
-
-        lax.fori_loop(0, LOCAL // 8, body, 0)
-        tile(LOCAL // 8 * 8, LOCAL % 8, forward)
-
-    @pl.when(flag_ref[1] == 0)
-    def _():
-        sweep(True)
-
-    @pl.when(flag_ref[1] == 1)
-    def _():
-        sweep(False)
+    rows_back = flag_ref[0]
+    cols_back = flag_ref[1]
+    halves = (
+        (0, PHASES, 0, next_main, last_main),
+        (PHASES * 8, SHORT, 128, next_side, last_side),
+    )
+    for base, phases, lanes, after, before in halves:
+        coef = [
+            jnp.broadcast_to(tab_ref[n : n + 1, lanes : lanes + 128], (8, 128)) for n in range(4)
+        ]
+
+        def put_once(i, phase, value):
+            once_ref[i, pl.ds(pl.multiple_of(base + phase * 8, 8), 8), :] = value
+
+        def put_twice(i, phase, value):
+            if base == 0:
+                phase = phase + (PHASES - 1 - 2 * phase) * cols_back
+            line = i * LINES + base + phase * 8
+            twice_ref[pl.ds(pl.multiple_of(line, 8), 8), :] = value
+
+        substep(cells, None, put_once, keep_ref, coef, base, phases, after, before)
+        once = [(once_ref, i) for i in range(11)]
+        substep(once, cells[4:12], put_twice, keep_ref, coef, base, phases, after, before)
+
+    for e in range(TROWS):
+        r = e + (TROWS - 1 - 2 * e) * rows_back
+        for half in range(2):
+            parts = []
+            for s in range(half * 4, half * 4 + 4):
+                start = e * LINES + s + (7 - 2 * s) * cols_back
+                parts.append(twice_ref[pl.ds(start, PHASES, stride=8), :])
+            block = jnp.concatenate(parts, axis=0).T
+            turn_ref[half, pl.ds(r, MAIN, stride=TROWS), :] = block
+        line = e * LINES + PHASES * 8
+        block = jnp.concatenate(
+            [twice_ref[line : line + SHORT * 8, :], jnp.zeros((128 - SHORT * 8, 128), jnp.float32)],
+            axis=0,
+        ).T
+        for pack in range(PACKS):
+            rest_ref[pack, pl.ds(r, 32, stride=TROWS), :] = block[pack * 32 : pack * 32 + 32]
+    spot = lax.broadcasted_iota(jnp.int32, (PACKS * 128, NY), 0)
+    col = lax.broadcasted_iota(jnp.int32, (PACKS * 128, NY), 1)
+    col = col + (NY - 1 - 2 * col) * cols_back
+    pack, inner = spot // 128, spot % 128
+    wanted = inner % 8 * 32 + pack * SHORT + inner // 8
+    order = jnp.where((wanted == col) & (inner < SHORT * 8), 1.0, 0.0).astype(jnp.bfloat16)
+    value = jnp.concatenate([rest_ref[pack] for pack in range(PACKS)], axis=1)
+    high = value.astype(jnp.bfloat16)
+    rest = (value - high.astype(jnp.float32)).astype(jnp.bfloat16)
+    value = jnp.dot(high, order, preferred_element_type=jnp.float32)
+    value = value + jnp.dot(rest, order, preferred_element_type=jnp.float32)
+    for i in range(LOCAL - MAIN):
+        out_ref[MAIN + i] = value[i * TROWS : (i + 1) * TROWS, :]
+    for i in range(MAIN):
+        for half in range(2):
+            out_ref[i, :, half * 128 : half * 128 + 128] = turn_ref[
+                half, i * TROWS : (i + 1) * TROWS, :
+            ]
 
 
 def call(kernel, shapes, scratch, ins, *args, limit=20):
@@ -240,7 +343,10 @@
 
 def local(spectra, wind_speed, wind_dir, sea_cell):
     group = lax.axis_index("grp")
-    table = lax.dynamic_index_in_dim(jnp.asarray(coefficient_table()), group, 0, keepdims=False)
+    table, courant = (
+        lax.dynamic_index_in_dim(jnp.asarray(t), group, 0, keepdims=False)
+        for t in coefficient_tables()
+    )
     mirror_x = ((group == 1) | (group == 2)).astype(jnp.int32)
     mirror_y = (group >= 2).astype(jnp.int32)
     flags = jnp.stack([mirror_x, mirror_y])
@@ -257,10 +363,10 @@
         packed.reshape(TILES, 1, SLOTS * 128), "comp", split_axis=0, concat_axis=0, tiled=True
     ).reshape(TILES * SLOTS, 128)
     cells = sea_cell.reshape(TILES, SEND).T
-    cells = cells ^ (mirror_x * (NY * (TROWS - 1)))
+    cells = cells ^ (mirror_x * (NY * (TROWS - 1)) + mirror_y * (NY - 1))
     hot = call(
         onehot_kernel,
-        jax.ShapeDtypeStruct((2, SEA, 4 * NY), jnp.bfloat16),
+        jax.ShapeDtypeStruct((TROWS * NY, SEA), jnp.bfloat16),
         [],
         [VMEM],
         cells,
@@ -277,10 +383,11 @@
     partial = lax.all_to_all(partial, "grp", split_axis=0, concat_axis=0, tiled=True)
     low, mid, up = call(
         place_kernel,
-        (f32(2, ROWS, NY), f32(2, ROWS, NY), f32(4, ROWS, NY)),
+        (f32(2, LINES, 128), f32(2, LINES, 128), f32(4, LINES, 128)),
         [
             pltpu.VMEM((DEPTH, SEA), jnp.float32),
-            pltpu.VMEM((2, SEA, 4 * NY), jnp.bfloat16),
+            pltpu.VMEM((2, TROWS * NY // 2, SEA), jnp.bfloat16),
+            pltpu.VMEM((PACKS, 256, SEA), jnp.bfloat16),
             pltpu.SemaphoreType.DMA((2,)),
         ],
         [VMEM] * 4 + [pl.BlockSpec(memory_space=pltpu.HBM)],
@@ -303,13 +410,15 @@
         advect_kernel,
         f32(LOCAL, TROWS, NY),
         [
-            pltpu.VMEM((11, 8, NY), jnp.float32),
-            pltpu.VMEM((4, ROWS, NY), jnp.float32),
-            pltpu.VMEM((2, 8 * TROWS, 128), jnp.float32),
+            pltpu.VMEM((11, LINES, 128), jnp.float32),
+            pltpu.VMEM((TROWS * LINES, 128), jnp.float32),
+            pltpu.VMEM((11, 2, 8, 128), jnp.float32),
+            pltpu.VMEM((2, MAIN * TROWS, 128), jnp.float32),
+            pltpu.VMEM((PACKS, 32 * TROWS, 128), jnp.float32),
         ],
         [SMEM] + [VMEM] * 6,
         flags,
-        table,
+        courant,
         below,
         low,
         mid,

time: 91.2 us -> 88.1 us (0.966)
  Pallas kernels: 18.7 us -> 15.6 us
    pallas_call x5, Pallas kernels: 18.7 us -> 15.6 us  [call(): pl.pallas_call(kernel, out_shape=shapes, in_specs=ins, out_specs=jax.tree...]
  transfers between devices with their start and end apart: 3 -> 3, of which waited for: 3 -> 3; matrix products, arithmetic and copies ran while one was open for 2% -> 3% of each run, Pallas kernels for 1% -> 2%
where the time goes in v3:
time: 88.1 us; the launch traced here: 87.6 us
  waiting for transfers between devices  29.4 us (33%)
  starting transfers between devices  25 us (28%)
  Pallas kernels  15.6 us (18%)
  blocking collectives  9.63 us (11%)
  local copies, waits for them, and re-layouts  6.99 us (8%)
    all_to_all x1, waiting for transfers between devices, local(): lax.all_to_all(packed.reshape(TILES, 1, SLOTS * 128), 'comp', split_axis=...  23.9 us
    all_to_all x1, starting transfers between devices, local(): lax.all_to_all(packed.reshape(TILES, 1, SLOTS * 128), 'comp', split_axis=...  17.4 us
    pallas_call x5, Pallas kernels, call(): pl.pallas_call(kernel, out_shape=shapes, in_specs=ins, out_specs=jax.tree...  15.6 us
    all_to_all x1, blocking collectives, local(): lax.all_to_all(partial, 'grp', split_axis=0, concat_axis=0, tiled=True)  9.63 us
    ppermute x1, starting transfers between devices, local(): above = lax.ppermute(low, ('grp', 'comp'), back)  5.75 us
    unnamed x8, local copies, waits for them, and re-layouts  5.24 us
    ppermute x1, waiting for transfers between devices, local(): above = lax.ppermute(low, ('grp', 'comp'), back)  3.79 us
    ppermute x1, starting transfers between devices, local(): below = lax.ppermute(up, ('grp', 'comp'), ahead)  1.92 us
  transfers between devices with their start and end apart: 3, of which 3 were waited for; matrix products, arithmetic and copies ran while one was open for 3% of the time, Pallas kernels for 2%

profile of v3, /device:TPU:8, one launch (start us, length us, event | category | flops | bytes accessed | tf_op | source)
XLA Modules:
  0.0 87.6 jit_solution(14470087388379006191)
XLA Ops:
  0.0 0.0 copy-start.1
  0.0 1.2 %copy-done.1 = f32[150,1536]{1,0:T(8,128)S(1)} copy-done((f32[150,1536]{1,0:T(8,128)S(1)}, f32[150,1536]{1,0:T(8,128)}, u32[]{:S(2)}) %copy-start.1) | copy-done | bytes 921624
  1.2 0.0 copy-start.2
  1.2 0.7 copy-done.2
  1.9 0.0 copy-start.3
  1.9 0.7 copy-done.3
  2.6 1.7 %shard_map.64 = f32[1920,128]{1,0:T(8,128)} custom-call(f32[150,1536]{1,0:T(8,128)S(1)} %copy-done.1, f32[12,128]{1,0:T(8,128)S(1)} %bitcast.13, f32[12,128]{1,0:T(8,128)S(1)} %bitcast.14), custom_call_target="tpu_custom_call" | custom-call | tf_op jit(solution)/shard_map/pallas_call | solution.py:330
  4.2 17.4 %all-to-all-start = ((f32[128,1,1920]{2,1,0:T(1,128)}), f32[128,1,1920]{2,1,0:T(1,128)S(1)}, u32[]{:S(2)}, u32[]{:S(2)}) async-start(f32[128,1,1920]{2,1,0:T(1,128)} %bitcast.5), calls=%async_computation | async-start | bytes 1966080 | tf_op jit(solution)/shard_map/all_to_all | solution.py:362
  21.6 0.7 broadcast_xor_fusion
  22.3 0.1 xor.12
  22.4 0.1 copy.9
  22.5 1.7 %shard_map.65.hot_ref = bf16[2048,1536]{1,0:T(8,128)(2,1)S(1)} custom-call(s32[12,128]{1,0:T(8,128)S(1)} %bitcast.12), custom_call_target="tpu_custom_call" | custom-call | tf_op jit(solution)/shard_map/pallas_call | solution.py:330
  24.2 0.0 copy-start
  24.2 2.7 %copy-done = bf16[2048,1536]{1,0:T(8,128)(2,1)} copy-done((bf16[2048,1536]{1,0:T(8,128)(2,1)}, bf16[2048,1536]{1,0:T(8,128)(2,1)S(1)}, u32[]{:S(2)}) %copy-start) | copy-done | bytes 6291480
  26.9 0.9 %dynamic-slice_bitcast_fusion.tab_ref = f32[152,128]{1,0:T(8,128)S(1)} fusion(f32[4,152,128]{2,1,0:T(8,128)} %constant.30.clone, s32[]{:T(128)S(6)} %select_n.6), kind=kLoop, calls=%fused_computation | loop fusion | bytes 155652 | tf_op jit(solution)/shard_map/jit(dynamic_index_in_dim)/squeeze | solution.py:347
  27.8 23.9 %all-to-all-done = f32[128,1,1920]{2,1,0:T(1,128)S(1)} async-done(((f32[128,1,1920]{2,1,0:T(1,128)}), f32[128,1,1920]{2,1,0:T(1,128)S(1)}, u32[]{:S(2)}, u32[]{:S(2)}) %all-to-all-start) | async-done | bytes 983072 | tf_op jit(solution)/shard_map/all_to_all | solution.py:362
  51.6 0.4 shard_map.66
  52.0 9.6 %all_to_all.10.e_ref = f32[4,24,128]{2,1,0:T(8,128)S(1)} all-to-all(f32[4,24,128]{2,1,0:T(8,128)S(1)} %get-tuple-element.16), channel_id=1, replica_groups=mesh['grp'=4,'comp'=128] {'grp'}, dimensions={0} | all-to-all | bytes 98304 | tf_op jit(solution)/shard_map/all_to_all | solution.py:383
  61.7 5.8 %shard_map.67 = (f32[2,320,128]{2,1,0:T(8,128)S(1)}, f32[2,320,128]{2,1,0:T(8,128)S(1)}, f32[4,320,128]{2,1,0:T(8,128)S(1)}) custom-call(f32[12,152,128]{2,1,0:T(8,128)S(1)} %get-tuple-element.14.y_ref, f32[24,128]{1,0:T(8,128)S(1)} %get-tuple-element.15.wind_ref, f32[4,24,128]{2,1,0:T(8,128)S(1)} %all_to_all.10.e_ref, ...), custom_call_target="tpu_custom_call" | custom-call | tf_op jit(solution)/shard_map/pallas_call | solution.py:330
  67.5 1.9 %collective-permute-start = (f32[4,320,128]{2,1,0:T(8,128)S(1)}, f32[4,320,128]{2,1,0:T(8,128)S(1)}, u32[]{:S(2)}, u32[]{:S(2)}) collective-permute-start(f32[4,320,128]{2,1,0:T(8,128)S(1)} %get-tuple-element.18.up_ref), channel_id=1, source_target_pairs={{0,1},{1,2},{2,3},{3,4},{4,5},{5,6},{6,7},{7,8},{8,9},{9,10},{10,1... | collective-permute-start | bytes 1966088 | tf_op jit(solution)/shard_map/ppermute | solution.py:407
  69.4 5.8 %collective-permute-start.1 = (f32[2,320,128]{2,1,0:T(8,128)S(1)}, f32[2,320,128]{2,1,0:T(8,128)S(1)}, u32[]{:S(2)}, u32[]{:S(2)}) collective-permute-start(f32[2,320,128]{2,1,0:T(8,128)S(1)} %get-tuple-element.19.low_ref), channel_id=1, source_target_pairs={{1,0},{2,1},{3,2},{4,3},{5,4},{6,5},{7,6},{8,7},{9,8},{10,9},{11,1... | collective-permute-start | bytes 983048 | tf_op jit(solution)/shard_map/ppermute | solution.py:408
  75.1 0.1 add_convert_fusion.flag_ref
  75.2 0.7 dynamic-slice_bitcast_fusion.1.tab_ref
  75.9 3.8 %collective-permute-done.1.above_ref = f32[2,320,128]{2,1,0:T(8,128)S(1)} collective-permute-done((f32[2,320,128]{2,1,0:T(8,128)S(1)}, f32[2,320,128]{2,1,0:T(8,128)S(1)}, u32[]{:S(2)}, u32[]{:S(2)}) %collective-permute-start.1) | collective-permute-done | bytes 327712 | tf_op jit(solution)/shard_map/ppermute | solution.py:408
  79.7 1.8 %collective-permute-done.below_ref = f32[4,320,128]{2,1,0:T(8,128)S(1)} collective-permute-done((f32[4,320,128]{2,1,0:T(8,128)S(1)}, f32[4,320,128]{2,1,0:T(8,128)S(1)}, u32[]{:S(2)}, u32[]{:S(2)}) %collective-permute-start) | collective-permute-done | bytes 655392 | tf_op jit(solution)/shard_map/ppermute | solution.py:407
  81.5 6.1 %shard_map.68 = f32[150,8,256]{2,1,0:T(8,128)} custom-call(s32[2]{0:T(128)S(1)} %add_convert_fusion.flag_ref, f32[8,256]{1,0:T(8,128)S(1)} %dynamic-slice_bitcast_fusion.1.tab_ref, f32[4,320,128]{2,1,0:T(8,128)S(1)} %collective-permute-done.below_ref, f32[2,320,128]{2,1,0:T(8,128)S(1)} %get-tuple-element.19.low_ref, ...), custom_call_target="tpu_custom_call" | custom-call | tf_op jit(solution)/shard_map/pallas_call | solution.py:330
Async XLA Ops:
  0.0 1.2 %copy-start.1 = (f32[150,1536]{1,0:T(8,128)S(1)}, f32[150,1536]{1,0:T(8,128)}, u32[]{:S(2)}) copy-start(f32[150,1536]{1,0:T(8,128)} %x_ref.1) | copy-start | bytes 2764804
  1.2 0.7 copy-start.2
  1.9 0.7 copy-start.3
  4.2 47.4 %all-to-all-start = ((f32[128,1,1920]{2,1,0:T(1,128)}), f32[128,1,1920]{2,1,0:T(1,128)S(1)}, u32[]{:S(2)}, u32[]{:S(2)}) async-start(f32[128,1,1920]{2,1,0:T(1,128)} %bitcast.5), calls=%async_computation | async-start | bytes 1966080 | tf_op jit(solution)/shard_map/all_to_all | solution.py:362
  24.2 2.7 %copy-start = (bf16[2048,1536]{1,0:T(8,128)(2,1)}, bf16[2048,1536]{1,0:T(8,128)(2,1)S(1)}, u32[]{:S(2)}) copy-start(bf16[2048,1536]{1,0:T(8,128)(2,1)S(1)} %shard_map.65.hot_ref) | copy-start | bytes 18874372
  67.5 14.0 %collective-permute-start = (f32[4,320,128]{2,1,0:T(8,128)S(1)}, f32[4,320,128]{2,1,0:T(8,128)S(1)}, u32[]{:S(2)}, u32[]{:S(2)}) collective-permute-start(f32[4,320,128]{2,1,0:T(8,128)S(1)} %get-tuple-element.18.up_ref), channel_id=1, source_target_pairs={{0,1},{1,2},{2,3},{3,4},{4,5},{5,6},{6,7},{7,8},{8,9},{9,10},{10,1... | collective-permute-start | bytes 1966088 | tf_op jit(solution)/shard_map/ppermute | solution.py:407
  69.4 10.3 %collective-permute-start.1 = (f32[2,320,128]{2,1,0:T(8,128)S(1)}, f32[2,320,128]{2,1,0:T(8,128)S(1)}, u32[]{:S(2)}, u32[]{:S(2)}) collective-permute-start(f32[2,320,128]{2,1,0:T(8,128)S(1)} %get-tuple-element.19.low_ref), channel_id=1, source_target_pairs={{1,0},{2,1},{3,2},{4,3},{5,4},{6,5},{7,6},{8,7},{9,8},{10,9},{11,1... | collective-permute-start | bytes 983048 | tf_op jit(solution)/shard_map/ppermute | solution.py:408

commit v4 on v3

--- a/solution.py
+++ b/solution.py
@@ -37,6 +37,8 @@
 SHORT = PHASES // PACKS
 LINES = (PHASES + SHORT) * 8
 CHUNK = 4
+PARTS = 4
+HALF = TROWS * NY // 2
 
 
 def coefficient_tables():
@@ -64,27 +66,62 @@
     return table.astype(np.float32), courant.astype(np.float32)
 
 
-def pack_kernel(x_ref, speed_ref, heading_ref, out_ref, z_ref, b_ref):
-    b_ref[0 : LOCAL - MAIN, :] = x_ref[MAIN:LOCAL, :]
-    for block in range(SEA // 128):
-        cols = slice(block * 128, block * 128 + 128)
-        b_ref[LOCAL - MAIN : LOCAL - MAIN + 1, cols] = speed_ref[block : block + 1, :]
-        b_ref[LOCAL - MAIN + 1 : EXTRA, cols] = heading_ref[block : block + 1, :]
-    b_ref[EXTRA:128, :] = jnp.zeros((128 - EXTRA, SEA), jnp.float32)
-    for block in range(SEA // 128):
-        cols = slice(block * 128, block * 128 + 128)
-        z_ref[0, cols, :] = x_ref[0:MAIN, cols].T
-        z_ref[1, cols, :] = b_ref[:, cols].T
-    for k in range(SEND):
-        out_ref[pl.ds(k, TILES, stride=SLOTS), :] = z_ref[0, pl.ds(k, TILES, stride=SEND), :]
-    for tile in range(SLOTS - SEND):
-        total = None
-        for k in range(tile * PER_TILE, min(SEND, (tile + 1) * PER_TILE)):
-            piece = z_ref[1, pl.ds(k, TILES, stride=SEND), :]
-            shift = (k % PER_TILE) * EXTRA
-            piece = pltpu.roll(piece, shift, 1) if shift else piece
-            total = piece if total is None else total + piece
-        out_ref[pl.ds(SEND + tile, TILES, stride=SLOTS), :] = total
+def pack_kernel(x_hbm, speed_hbm, heading_hbm, out_hbm, x_ref, wind_ref, z_ref, b_ref, m_ref,
+                sem_in, sem_wind, sem_out):
+    width = SEA // PARTS
+    tiles = TILES // PARTS
+    ins = [
+        pltpu.make_async_copy(x_hbm.at[:, pl.ds(c * width, width)], x_ref.at[c], sem_in.at[c])
+        for c in range(PARTS)
+    ]
+    winds = [
+        pltpu.make_async_copy(ref, wind_ref.at[i], sem_wind.at[i])
+        for i, ref in enumerate((speed_hbm, heading_hbm))
+    ]
+    outs = [
+        pltpu.make_async_copy(
+            m_ref.at[pl.ds(c * tiles * SLOTS, tiles * SLOTS)],
+            out_hbm.at[pl.ds(c * tiles * SLOTS, tiles * SLOTS)],
+            sem_out.at[c],
+        )
+        for c in range(PARTS)
+    ]
+    ins[0].start()
+    winds[0].start()
+    winds[1].start()
+    for c in range(1, PARTS):
+        ins[c].start()
+    b_ref[EXTRA:128, :] = jnp.zeros((128 - EXTRA, width), jnp.float32)
+    for c in range(PARTS):
+        ins[c].wait()
+        if c == 0:
+            winds[0].wait()
+            winds[1].wait()
+        b_ref[0 : LOCAL - MAIN, :] = x_ref[c, MAIN:LOCAL, :]
+        for block in range(width // 128):
+            cols = slice(block * 128, block * 128 + 128)
+            at = c * (width // 128) + block
+            for i in range(2):
+                row = LOCAL - MAIN + i
+                b_ref[row : row + 1, cols] = wind_ref[i, at : at + 1, :]
+            z_ref[0, cols, :] = x_ref[c, 0:MAIN, cols].T
+            z_ref[1, cols, :] = b_ref[:, cols].T
+        first = c * tiles * SLOTS
+        for k in range(SEND):
+            m_ref[pl.ds(first + k, tiles, stride=SLOTS), :] = z_ref[
+                0, pl.ds(k, tiles, stride=SEND), :
+            ]
+        for tile in range(SLOTS - SEND):
+            total = None
+            for k in range(tile * PER_TILE, min(SEND, (tile + 1) * PER_TILE)):
+                piece = z_ref[1, pl.ds(k, tiles, stride=SEND), :]
+                shift = (k % PER_TILE) * EXTRA
+                piece = pltpu.roll(piece, shift, 1) if shift else piece
+                total = piece if total is None else total + piece
+            m_ref[pl.ds(first + SEND + tile, tiles, stride=SLOTS), :] = total
+        outs[c].start()
+    for c in range(PARTS):
+        outs[c].wait()
 
 
 def moments_kernel(r_ref, tab_ref, y_ref, wind_ref, e_ref):
@@ -127,12 +164,29 @@
     lax.fori_loop(0, TROWS, body, 0)
 
 
-def place_kernel(y_ref, wind_ref, e_ref, tab_ref, hot_ref, low_ref, mid_ref, up_ref, s_ref,
-                 held_ref, side_ref, sem):
-    half = TROWS * NY // 2
+def spread(held_ref, main, side, refs):
+    turned = (((1,), (1,)), ((), ()))
+    block = SHORT * 8
+    out = lax.dot_general(held_ref[...], main, turned, preferred_element_type=jnp.float32)
+    out = out[:, 0:128] + out[:, 128:256]
+    rest = lax.dot_general(held_ref[...], side, turned, preferred_element_type=jnp.float32)
+    rest = rest[:, 0:128] + rest[:, 128:256]
+    lane = lax.broadcasted_iota(jnp.int32, (block, 128), 1)
+    for i, (ref, at) in enumerate(refs):
+        total = None
+        for pack in range(PACKS):
+            line = (pack * 4 + i) * block
+            ref[at, pack * block : (pack + 1) * block, :] = out[line : line + block]
+            part = rest[line : line + block]
+            total = part if total is None else jnp.where(lane < pack * 32, total, part)
+        ref[at, PHASES * 8 : LINES, :] = total
+
+
+def place_kernel(y_ref, wind_ref, e_ref, tab_ref, hot_ref, up_ref, main_ref, side_ref, kept_ref,
+                 s_ref, held_ref, sem):
     copies = [
-        pltpu.make_async_copy(hot_ref.at[pl.ds(h * half, half)], held_ref.at[h], sem.at[h])
-        for h in range(2)
+        pltpu.make_async_copy(hot_ref.at[pl.ds(h * HALF, HALF)], ref, sem.at[h])
+        for h, ref in enumerate((kept_ref, held_ref))
     ]
     copies[1].start()
     copies[0].start()
@@ -160,32 +214,19 @@
     value = s_ref[...]
     high = value.astype(jnp.bfloat16)
     rest = (value - high.astype(jnp.float32)).astype(jnp.bfloat16)
-    main = jnp.concatenate([high[0:MAIN], rest[0:MAIN]], axis=0)
-    side_ref[...] = jnp.zeros(side_ref.shape, jnp.bfloat16)
+    main_ref[0:MAIN, :] = high[0:MAIN]
+    main_ref[MAIN:256, :] = rest[0:MAIN]
     for pack in range(PACKS):
-        side_ref[pack, pack * 32 : pack * 32 + 32, :] = high[MAIN:DEPTH]
-        side_ref[pack, 128 + pack * 32 : 128 + pack * 32 + 32, :] = rest[MAIN:DEPTH]
-    turned = (((1,), (1,)), ((), ()))
-    block = SHORT * 8
-    for h in (1, 0):
-        copies[h].wait()
-        refs = [(up_ref, i) for i in range(4)]
-        if h == 0:
-            refs = [(low_ref, 0), (low_ref, 1), (mid_ref, 0), (mid_ref, 1)]
-        out = lax.dot_general(held_ref[h], main, turned, preferred_element_type=jnp.float32)
-        out = out[:, 0:128] + out[:, 128:256]
-        for pack in range(PACKS):
-            for i, (ref, at) in enumerate(refs):
-                line = (pack * 4 + i) * block
-                ref[at, pack * block : (pack + 1) * block, :] = out[line : line + block]
-        total = None
-        for pack in range(PACKS):
-            hot = held_ref[h, pack * 4 * block : (pack + 1) * 4 * block, :]
-            out = lax.dot_general(hot, side_ref[pack], turned, preferred_element_type=jnp.float32)
-            total = out if total is None else total + out
-        total = total[:, 0:128] + total[:, 128:256]
-        for i, (ref, at) in enumerate(refs):
-            ref[at, PHASES * 8 : LINES, :] = total[i * block : (i + 1) * block]
+        side_ref[pack * 32 : pack * 32 + 32, :] = high[MAIN:DEPTH]
+        side_ref[128 + pack * 32 : 128 + pack * 32 + 32, :] = rest[MAIN:DEPTH]
+    copies[1].wait()
+    spread(held_ref, main_ref[...], side_ref[...], [(up_ref, i) for i in range(4)])
+    copies[0].wait()
+
+
+def place_rest_kernel(main_ref, side_ref, kept_ref, low_ref, mid_ref):
+    refs = [(low_ref, 0), (low_ref, 1), (mid_ref, 0), (mid_ref, 1)]
+    spread(kept_ref, main_ref[...], side_ref[...], refs)
 
 
 def limited(a, b):
@@ -261,47 +302,77 @@
     lax.fori_loop(0, phases // CHUNK, body, 0)
 
 
-def advect_kernel(flag_ref, tab_ref, below_ref, low_ref, mid_ref, up_ref, above_ref, out_ref,
-                  once_ref, twice_ref, keep_ref, turn_ref, rest_ref):
+def halves(tab_ref):
+    for base, phases, lanes, after, before in (
+        (0, PHASES, 0, next_main, last_main),
+        (PHASES * 8, SHORT, 128, next_side, last_side),
+    ):
+        coef = [
+            jnp.broadcast_to(tab_ref[n : n + 1, lanes : lanes + 128], (8, 128)) for n in range(4)
+        ]
+        yield coef, base, phases, after, before
+
+
+def writer(ref, base, offset):
+    def put(i, phase, value):
+        ref[i + offset, pl.ds(pl.multiple_of(base + phase * 8, 8), 8), :] = value
+
+    return put
+
+
+def last_writer(ref, base, offset, cols_back):
+    def put(i, phase, value):
+        if base == 0:
+            phase = phase + (PHASES - 1 - 2 * phase) * cols_back
+        line = (i + offset) * LINES + base + phase * 8
+        ref[pl.ds(pl.multiple_of(line, 8), 8), :] = value
+
+    return put
+
+
+def inner_kernel(flag_ref, tab_ref, low_ref, mid_ref, up_ref, once_ref, twice_ref, keep_ref):
+    cells = [(low_ref, 0), (low_ref, 1), (mid_ref, 0), (mid_ref, 1)]
+    cells += [(up_ref, i) for i in range(4)]
+    once = [(once_ref, i) for i in range(5)]
+    for half in halves(tab_ref):
+        base = half[1]
+        substep(cells, None, writer(once_ref, base, 0), keep_ref, *half)
+        put = last_writer(twice_ref, base, 0, flag_ref[1])
+        substep(once, cells[4:6], put, keep_ref, *half)
+
+
+def outer_kernel(flag_ref, tab_ref, below_ref, low_ref, mid_ref, up_ref, above_ref, inner_ref,
+                 inner_twice_ref, out_ref, once_ref, twice_ref, keep_ref, turn_ref, rest_ref):
     cells = [(below_ref, i) for i in range(4)] + [(low_ref, i) for i in range(2)]
     cells += [(mid_ref, i) for i in range(2)] + [(up_ref, i) for i in range(4)]
     cells += [(above_ref, i) for i in range(2)]
+    once = [(once_ref, i) for i in range(4)] + [(inner_ref, i) for i in range(5)]
+    once += [(once_ref, i) for i in range(4, 6)]
     rows_back = flag_ref[0]
     cols_back = flag_ref[1]
-    halves = (
-        (0, PHASES, 0, next_main, last_main),
-        (PHASES * 8, SHORT, 128, next_side, last_side),
-    )
-    for base, phases, lanes, after, before in halves:
-        coef = [
-            jnp.broadcast_to(tab_ref[n : n + 1, lanes : lanes + 128], (8, 128)) for n in range(4)
-        ]
-
-        def put_once(i, phase, value):
-            once_ref[i, pl.ds(pl.multiple_of(base + phase * 8, 8), 8), :] = value
-
-        def put_twice(i, phase, value):
-            if base == 0:
-                phase = phase + (PHASES - 1 - 2 * phase) * cols_back
-            line = i * LINES + base + phase * 8
-            twice_ref[pl.ds(pl.multiple_of(line, 8), 8), :] = value
-
-        substep(cells, None, put_once, keep_ref, coef, base, phases, after, before)
-        once = [(once_ref, i) for i in range(11)]
-        substep(once, cells[4:12], put_twice, keep_ref, coef, base, phases, after, before)
-
-    for e in range(TROWS):
+    for half in halves(tab_ref):
+        base = half[1]
+        substep(cells[0:7], None, writer(once_ref, base, 0), keep_ref, *half)
+        substep(cells[9:14], None, writer(once_ref, base, 4), keep_ref, *half)
+        put = last_writer(twice_ref, base, 0, cols_back)
+        substep(once[0:7], cells[4:8], put, keep_ref, *half)
+        put = last_writer(twice_ref, base, 4, cols_back)
+        substep(once[6:11], cells[10:12], put, keep_ref, *half)
+
+    where = [(twice_ref, i) for i in range(4)] + [(inner_twice_ref, i) for i in range(2)]
+    where += [(twice_ref, i) for i in range(4, 6)]
+    for e, (ref, at) in enumerate(where):
         r = e + (TROWS - 1 - 2 * e) * rows_back
         for half in range(2):
             parts = []
             for s in range(half * 4, half * 4 + 4):
-                start = e * LINES + s + (7 - 2 * s) * cols_back
-                parts.append(twice_ref[pl.ds(start, PHASES, stride=8), :])
+                start = at * LINES + s + (7 - 2 * s) * cols_back
+                parts.append(ref[pl.ds(start, PHASES, stride=8), :])
             block = jnp.concatenate(parts, axis=0).T
             turn_ref[half, pl.ds(r, MAIN, stride=TROWS), :] = block
-        line = e * LINES + PHASES * 8
+        line = at * LINES + PHASES * 8
         block = jnp.concatenate(
-            [twice_ref[line : line + SHORT * 8, :], jnp.zeros((128 - SHORT * 8, 128), jnp.float32)],
+            [ref[line : line + SHORT * 8, :], jnp.zeros((128 - SHORT * 8, 128), jnp.float32)],
             axis=0,
         ).T
         for pack in range(PACKS):
@@ -326,13 +397,15 @@
             ]
 
 
-def call(kernel, shapes, scratch, ins, *args, limit=20):
+def call(kernel, shapes, scratch, ins, *args, limit=20, us=0, outs=None):
+    cost = pl.CostEstimate(flops=us * 10**9, bytes_accessed=us * 3 * 10**6, transcendentals=0)
     return pl.pallas_call(
         kernel,
         out_shape=shapes,
         in_specs=ins,
-        out_specs=jax.tree.map(lambda _: VMEM, shapes),
+        out_specs=outs or jax.tree.map(lambda _: VMEM, shapes),
         scratch_shapes=scratch,
+        cost_estimate=cost if us else None,
         compiler_params=pltpu.CompilerParams(vmem_limit_bytes=limit * 1024 * 1024),
     )(*args)
 
@@ -350,14 +423,26 @@
     mirror_x = ((group == 1) | (group == 2)).astype(jnp.int32)
     mirror_y = (group >= 2).astype(jnp.int32)
     flags = jnp.stack([mirror_x, mirror_y])
+    hbm = pl.BlockSpec(memory_space=pltpu.HBM)
     packed = call(
         pack_kernel,
         f32(TILES * SLOTS, 128),
-        [pltpu.VMEM((2, SEA, 128), jnp.float32), pltpu.VMEM((128, SEA), jnp.float32)],
-        [VMEM] * 3,
+        [
+            pltpu.VMEM((PARTS, LOCAL, SEA // PARTS), jnp.float32),
+            pltpu.VMEM((2, SEA // 128, 128), jnp.float32),
+            pltpu.VMEM((2, SEA // PARTS, 128), jnp.float32),
+            pltpu.VMEM((128, SEA // PARTS), jnp.float32),
+            pltpu.VMEM((TILES * SLOTS, 128), jnp.float32),
+            pltpu.SemaphoreType.DMA((PARTS,)),
+            pltpu.SemaphoreType.DMA((2,)),
+            pltpu.SemaphoreType.DMA((PARTS,)),
+        ],
+        [hbm] * 3,
         spectra,
         wind_speed.reshape(SEA // 128, 128),
         wind_dir.reshape(SEA // 128, 128),
+        limit=57,
+        outs=hbm,
     )
     received = lax.all_to_all(
         packed.reshape(TILES, 1, SLOTS * 128), "comp", split_axis=0, concat_axis=0, tiled=True
@@ -381,22 +466,32 @@
         table,
     )
     partial = lax.all_to_all(partial, "grp", split_axis=0, concat_axis=0, tiled=True)
-    low, mid, up = call(
+    bf16 = functools.partial(jax.ShapeDtypeStruct, dtype=jnp.bfloat16)
+    up, main, side, kept = call(
         place_kernel,
-        (f32(2, LINES, 128), f32(2, LINES, 128), f32(4, LINES, 128)),
+        (f32(4, LINES, 128), bf16((256, SEA)), bf16((256, SEA)), bf16((HALF, SEA))),
         [
             pltpu.VMEM((DEPTH, SEA), jnp.float32),
-            pltpu.VMEM((2, TROWS * NY // 2, SEA), jnp.bfloat16),
-            pltpu.VMEM((PACKS, 256, SEA), jnp.bfloat16),
+            pltpu.VMEM((HALF, SEA), jnp.bfloat16),
             pltpu.SemaphoreType.DMA((2,)),
         ],
-        [VMEM] * 4 + [pl.BlockSpec(memory_space=pltpu.HBM)],
+        [VMEM] * 4 + [hbm],
         points,
         wind_here,
         partial,
         table,
         hot,
-        limit=50,
+        limit=44,
+    )
+    low, mid = call(
+        place_rest_kernel,
+        (f32(2, LINES, 128), f32(2, LINES, 128)),
+        [],
+        [VMEM] * 3,
+        main,
+        side,
+        kept,
+        us=2,
     )
     ahead, back = [], []
     for g in range(GROUPS):
@@ -406,17 +501,29 @@
             back.append(rise if g in (1, 2) else fall)
     below = lax.ppermute(up, ("grp", "comp"), ahead)
     above = lax.ppermute(low, ("grp", "comp"), back)
+    once, twice = call(
+        inner_kernel,
+        (f32(5, LINES, 128), f32(2 * LINES, 128)),
+        [pltpu.VMEM((5, 2, 8, 128), jnp.float32)],
+        [SMEM] + [VMEM] * 4,
+        flags,
+        courant,
+        low,
+        mid,
+        up,
+        us=3,
+    )
     return call(
-        advect_kernel,
+        outer_kernel,
         f32(LOCAL, TROWS, NY),
         [
-            pltpu.VMEM((11, LINES, 128), jnp.float32),
-            pltpu.VMEM((TROWS * LINES, 128), jnp.float32),
-            pltpu.VMEM((11, 2, 8, 128), jnp.float32),
+            pltpu.VMEM((6, LINES, 128), jnp.float32),
+            pltpu.VMEM((6 * LINES, 128), jnp.float32),
+            pltpu.VMEM((4, 2, 8, 128), jnp.float32),
             pltpu.VMEM((2, MAIN * TROWS, 128), jnp.float32),
             pltpu.VMEM((PACKS, 32 * TROWS, 128), jnp.float32),
         ],
-        [SMEM] + [VMEM] * 6,
+        [SMEM] + [VMEM] * 8,
         flags,
         courant,
         below,
@@ -424,6 +531,8 @@
         mid,
         up,
         above,
+        once,
+        twice,
     )
 
 

time: 88.1 us -> 84.8 us (0.963)
  Pallas kernels: 15.6 us -> 18.4 us
  waiting for transfers between devices: 29.4 us -> 26.7 us
  local copies, waits for them, and re-layouts: 6.99 us -> 4.42 us
    pallas_call x5 -> x7, Pallas kernels: 15.6 us -> 18.4 us  [call(): pl.pallas_call(kernel, out_shape=shapes, in_specs=ins, out_specs=outs or...]
    unnamed x8 -> x4, local copies, waits for them, and re-layouts: 5.24 us -> 2.66 us
    ppermute x1, waiting for transfers between devices: 1.75 us -> 0.01 us  [local(): below = lax.ppermute(up, ('grp', 'comp'), ahead)]
    ppermute x1, waiting for transfers between devices: 3.79 us -> 2.15 us  [local(): above = lax.ppermute(low, ('grp', 'comp'), back)]
  transfers between devices with their start and end apart: 3 -> 3, of which waited for: 3 -> 2; matrix products, arithmetic and copies ran while one was open for 3% -> 2% of each run, Pallas kernels for 2% -> 7%
where the time goes in v4:
time: 84.8 us; the launch traced here: 84.5 us
  waiting for transfers between devices  26.7 us (31%)
  starting transfers between devices  25.1 us (30%)
  Pallas kernels  18.4 us (22%)
  blocking collectives  9.63 us (11%)
  local copies, waits for them, and re-layouts  4.42 us (5%)
    all_to_all x1, waiting for transfers between devices, local(): lax.all_to_all(packed.reshape(TILES, 1, SLOTS * 128), 'comp', split_axis=...  24.5 us
    pallas_call x7, Pallas kernels, call(): pl.pallas_call(kernel, out_shape=shapes, in_specs=ins, out_specs=outs or...  18.4 us
    all_to_all x1, starting transfers between devices, local(): lax.all_to_all(packed.reshape(TILES, 1, SLOTS * 128), 'comp', split_axis=...  17.4 us
    all_to_all x1, blocking collectives, local(): lax.all_to_all(partial, 'grp', split_axis=0, concat_axis=0, tiled=True)  9.63 us
    ppermute x1, starting transfers between devices, local(): above = lax.ppermute(low, ('grp', 'comp'), back)  5.75 us
    unnamed x4, local copies, waits for them, and re-layouts  2.66 us
    ppermute x1, waiting for transfers between devices, local(): above = lax.ppermute(low, ('grp', 'comp'), back)  2.15 us
    ppermute x1, starting transfers between devices, local(): below = lax.ppermute(up, ('grp', 'comp'), ahead)  1.92 us
  transfers between devices with their start and end apart: 3, of which 2 were waited for; matrix products, arithmetic and copies ran while one was open for 2% of the time, Pallas kernels for 7%

profile of v4, /device:TPU:8, one launch (start us, length us, event | category | flops | bytes accessed | tf_op | source)
XLA Modules:
  0.0 84.5 jit_solution(15282046931437364781)
XLA Ops:
  0.0 0.0 copy-start.1
  0.0 3.0 %shard_map.64 = f32[1920,128]{1,0:T(8,128)} custom-call(f32[150,1536]{1,0:T(8,128)} %x_hbm.1, f32[12,128]{1,0:T(8,128)} %bitcast.14, f32[12,128]{1,0:T(8,128)} %bitcast.15), custom_call_target="tpu_custom_call" | custom-call | tf_op jit(solution)/shard_map/pallas_call | solution.py:402
  3.0 17.4 %all-to-all-start = ((f32[128,1,1920]{2,1,0:T(1,128)}), f32[128,1,1920]{2,1,0:T(1,128)S(1)}, u32[]{:S(2)}, u32[]{:S(2)}) async-start(f32[128,1,1920]{2,1,0:T(1,128)} %bitcast.13), calls=%async_computation | async-start | bytes 1966080 | tf_op jit(solution)/shard_map/all_to_all | solution.py:447
  20.4 0.0 copy-done.1
  20.4 0.1 xor.12
  20.5 0.1 copy.9
  20.6 1.7 %shard_map.65.hot_ref = bf16[2048,1536]{1,0:T(8,128)(2,1)S(1)} custom-call(s32[12,128]{1,0:T(8,128)S(1)} %bitcast.12), custom_call_target="tpu_custom_call" | custom-call | tf_op jit(solution)/shard_map/pallas_call | solution.py:402
  22.3 0.0 copy-start
  22.3 2.7 %copy-done = bf16[2048,1536]{1,0:T(8,128)(2,1)} copy-done((bf16[2048,1536]{1,0:T(8,128)(2,1)}, bf16[2048,1536]{1,0:T(8,128)(2,1)S(1)}, u32[]{:S(2)}) %copy-start) | copy-done | bytes 6291480
  25.0 0.9 %dynamic-slice_bitcast_fusion.tab_ref = f32[152,128]{1,0:T(8,128)S(1)} fusion(f32[4,152,128]{2,1,0:T(8,128)} %constant.30.clone, s32[]{:T(128)S(6)} %select_n.6), kind=kLoop, calls=%fused_computation | loop fusion | bytes 155652 | tf_op jit(solution)/shard_map/jit(dynamic_index_in_dim)/squeeze | solution.py:420
  25.9 24.5 %all-to-all-done = f32[128,1,1920]{2,1,0:T(1,128)S(1)} async-done(((f32[128,1,1920]{2,1,0:T(1,128)}), f32[128,1,1920]{2,1,0:T(1,128)S(1)}, u32[]{:S(2)}, u32[]{:S(2)}) %all-to-all-start) | async-done | bytes 983072 | tf_op jit(solution)/shard_map/all_to_all | solution.py:447
  50.4 0.4 shard_map.66
  50.8 9.6 %all_to_all.10.e_ref = f32[4,24,128]{2,1,0:T(8,128)S(1)} all-to-all(f32[4,24,128]{2,1,0:T(8,128)S(1)} %get-tuple-element.21), channel_id=1, replica_groups=mesh['grp'=4,'comp'=128] {'grp'}, dimensions={0} | all-to-all | bytes 98304 | tf_op jit(solution)/shard_map/all_to_all | solution.py:468
  60.4 3.7 %shard_map.67 = (f32[4,320,128]{2,1,0:T(8,128)S(1)}, bf16[256,1536]{1,0:T(8,128)(2,1)S(1)}, bf16[256,1536]{1,0:T(8,128)(2,1)S(1)}, bf16[1024,1536]{1,0:T(8,128)(2,1)S(1)}) custom-call(f32[12,152,128]{2,1,0:T(8,128)S(1)} %get-tuple-element.19.y_ref, f32[24,128]{1,0:T(8,128)S(1)} %get-tuple-element.20.wind_ref, f32[4,24,128]{2,1,0:T(8,128)S(1)} %all_to_all.10.e_ref, ...), custom_call_target="tpu_custom_call" | custom-call | tf_op jit(solution)/shard_map/pallas_call | solution.py:402
  64.2 1.9 %collective-permute-start = (f32[4,320,128]{2,1,0:T(8,128)S(1)}, f32[4,320,128]{2,1,0:T(8,128)S(1)}, u32[]{:S(2)}, u32[]{:S(2)}) collective-permute-start(f32[4,320,128]{2,1,0:T(8,128)S(1)} %get-tuple-element.23.up_ref), channel_id=1, source_target_pairs={{0,1},{1,2},{2,3},{3,4},{4,5},{5,6},{6,7},{7,8},{8,9},{9,10},{10,1... | collective-permute-start | bytes 1966088 | tf_op jit(solution)/shard_map/ppermute | solution.py:502
  66.1 0.7 dynamic-slice_bitcast_fusion.1.tab_ref
  66.8 1.8 %shard_map.68 = (f32[2,320,128]{2,1,0:T(8,128)S(1)}, f32[2,320,128]{2,1,0:T(8,128)S(1)}) custom-call(bf16[256,1536]{1,0:T(8,128)(2,1)S(1)} %get-tuple-element.24.main_ref, bf16[256,1536]{1,0:T(8,128)(2,1)S(1)} %get-tuple-element.25.side_ref, bf16[1024,1536]{1,0:T(8,128)(2,1)S(1)} %get-tuple-element.26.kept_ref), custom_call_target="tpu_custom_call" | custom-call | flops 2000000000 | bytes 6000000 | tf_op jit(solution)/shard_map/pallas_call | solution.py:402
  68.6 5.8 %collective-permute-start.1 = (f32[2,320,128]{2,1,0:T(8,128)S(1)}, f32[2,320,128]{2,1,0:T(8,128)S(1)}, u32[]{:S(2)}, u32[]{:S(2)}) collective-permute-start(f32[2,320,128]{2,1,0:T(8,128)S(1)} %get-tuple-element.27.low_ref), channel_id=1, source_target_pairs={{1,0},{2,1},{3,2},{4,3},{5,4},{6,5},{7,6},{8,7},{9,8},{10,9},{11,1... | collective-permute-start | bytes 983048 | tf_op jit(solution)/shard_map/ppermute | solution.py:503
  74.4 0.1 add_convert_fusion.flag_ref
  74.5 2.3 %shard_map.69 = (f32[5,320,128]{2,1,0:T(8,128)S(1)}, f32[640,128]{1,0:T(8,128)S(1)}) custom-call(s32[2]{0:T(128)S(1)} %add_convert_fusion.flag_ref, f32[8,256]{1,0:T(8,128)S(1)} %dynamic-slice_bitcast_fusion.1.tab_ref, f32[2,320,128]{2,1,0:T(8,128)S(1)} %get-tuple-element.27.low_ref, f32[2,320,128]{2,1,0:T(8,128)S(1)} %get-tuple-element.28.mid_ref, ...), custom_call_target="tpu_custom_call" | custom-call | flops 3000000000 | bytes 9000000 | tf_op jit(solution)/shard_map/pallas_call | solution.py:402
  76.8 2.2 %collective-permute-done.1.above_ref = f32[2,320,128]{2,1,0:T(8,128)S(1)} collective-permute-done((f32[2,320,128]{2,1,0:T(8,128)S(1)}, f32[2,320,128]{2,1,0:T(8,128)S(1)}, u32[]{:S(2)}, u32[]{:S(2)}) %collective-permute-start.1) | collective-permute-done | bytes 327712 | tf_op jit(solution)/shard_map/ppermute | solution.py:503
  78.9 0.0 collective-permute-done.below_ref
  79.0 5.5 %shard_map.70 = f32[150,8,256]{2,1,0:T(8,128)} custom-call(s32[2]{0:T(128)S(1)} %add_convert_fusion.flag_ref, f32[8,256]{1,0:T(8,128)S(1)} %dynamic-slice_bitcast_fusion.1.tab_ref, f32[4,320,128]{2,1,0:T(8,128)S(1)} %collective-permute-done.below_ref, f32[2,320,128]{2,1,0:T(8,128)S(1)} %get-tuple-element.27.low_ref, ...), custom_call_target="tpu_custom_call" | custom-call | tf_op jit(solution)/shard_map/pallas_call | solution.py:402
  (1 shorter events, 0.0 us)
Async XLA Ops:
  0.0 20.4 %copy-start.1 = (s32[1536]{0:T(1024)S(1)}, s32[1536]{0:T(1024)}, u32[]{:S(2)}) copy-start(s32[1536]{0:T(1024)} %param.9) | copy-start | bytes 18436
  3.0 47.4 %all-to-all-start = ((f32[128,1,1920]{2,1,0:T(1,128)}), f32[128,1,1920]{2,1,0:T(1,128)S(1)}, u32[]{:S(2)}, u32[]{:S(2)}) async-start(f32[128,1,1920]{2,1,0:T(1,128)} %bitcast.13), calls=%async_computation | async-start | bytes 1966080 | tf_op jit(solution)/shard_map/all_to_all | solution.py:447
  22.3 2.7 %copy-start = (bf16[2048,1536]{1,0:T(8,128)(2,1)}, bf16[2048,1536]{1,0:T(8,128)(2,1)S(1)}, u32[]{:S(2)}) copy-start(bf16[2048,1536]{1,0:T(8,128)(2,1)S(1)} %shard_map.65.hot_ref) | copy-start | bytes 18874372
  64.2 14.8 %collective-permute-start = (f32[4,320,128]{2,1,0:T(8,128)S(1)}, f32[4,320,128]{2,1,0:T(8,128)S(1)}, u32[]{:S(2)}, u32[]{:S(2)}) collective-permute-start(f32[4,320,128]{2,1,0:T(8,128)S(1)} %get-tuple-element.23.up_ref), channel_id=1, source_target_pairs={{0,1},{1,2},{2,3},{3,4},{4,5},{5,6},{6,7},{7,8},{8,9},{9,10},{10,1... | collective-permute-start | bytes 1966088 | tf_op jit(solution)/shard_map/ppermute | solution.py:502
  68.6 10.3 %collective-permute-start.1 = (f32[2,320,128]{2,1,0:T(8,128)S(1)}, f32[2,320,128]{2,1,0:T(8,128)S(1)}, u32[]{:S(2)}, u32[]{:S(2)}) collective-permute-start(f32[2,320,128]{2,1,0:T(8,128)S(1)} %get-tuple-element.27.low_ref), channel_id=1, source_target_pairs={{1,0},{2,1},{3,2},{4,3},{5,4},{6,5},{7,6},{8,7},{9,8},{10,9},{11,1... | collective-permute-start | bytes 983048 | tf_op jit(solution)/shard_map/ppermute | solution.py:503

commit v5 on v4

--- a/solution.py
+++ b/solution.py
@@ -37,6 +37,7 @@
 SHORT = PHASES // PACKS
 LINES = (PHASES + SHORT) * 8
 CHUNK = 4
+PAD = 8
 PARTS = 4
 HALF = TROWS * NY // 2
 
@@ -164,7 +165,7 @@
     lax.fori_loop(0, TROWS, body, 0)
 
 
-def spread(held_ref, main, side, refs):
+def spread(held_ref, main, side, ref):
     turned = (((1,), (1,)), ((), ()))
     block = SHORT * 8
     out = lax.dot_general(held_ref[...], main, turned, preferred_element_type=jnp.float32)
@@ -172,24 +173,24 @@
     rest = lax.dot_general(held_ref[...], side, turned, preferred_element_type=jnp.float32)
     rest = rest[:, 0:128] + rest[:, 128:256]
     lane = lax.broadcasted_iota(jnp.int32, (block, 128), 1)
-    for i, (ref, at) in enumerate(refs):
+    for i in range(4):
         total = None
         for pack in range(PACKS):
             line = (pack * 4 + i) * block
-            ref[at, pack * block : (pack + 1) * block, :] = out[line : line + block]
+            ref[i, pack * block : (pack + 1) * block, :] = out[line : line + block]
             part = rest[line : line + block]
             total = part if total is None else jnp.where(lane < pack * 32, total, part)
-        ref[at, PHASES * 8 : LINES, :] = total
-
-
-def place_kernel(y_ref, wind_ref, e_ref, tab_ref, hot_ref, up_ref, main_ref, side_ref, kept_ref,
-                 s_ref, held_ref, sem):
+        ref[i, PHASES * 8 : LINES, :] = total
+
+
+def place_kernel(y_ref, wind_ref, e_ref, tab_ref, hot_ref, first_ref, main_ref, side_ref,
+                 kept_ref, s_ref, held_ref, sem):
     copies = [
         pltpu.make_async_copy(hot_ref.at[pl.ds(h * HALF, HALF)], ref, sem.at[h])
-        for h, ref in enumerate((kept_ref, held_ref))
+        for h, ref in enumerate((held_ref, kept_ref))
     ]
+    copies[0].start()
     copies[1].start()
-    copies[0].start()
     moments = e_ref[0] + e_ref[1] + e_ref[2] + e_ref[3]
     energy, inverse = moments[0:SEND], moments[SEND : 2 * SEND]
     mean = energy / inverse
@@ -219,14 +220,14 @@
     for pack in range(PACKS):
         side_ref[pack * 32 : pack * 32 + 32, :] = high[MAIN:DEPTH]
         side_ref[128 + pack * 32 : 128 + pack * 32 + 32, :] = rest[MAIN:DEPTH]
+    first_ref[:, LINES : LINES + PAD, :] = jnp.zeros((4, PAD, 128), jnp.float32)
+    copies[0].wait()
+    spread(held_ref, main_ref[...], side_ref[...], first_ref)
     copies[1].wait()
-    spread(held_ref, main_ref[...], side_ref[...], [(up_ref, i) for i in range(4)])
-    copies[0].wait()
-
-
-def place_rest_kernel(main_ref, side_ref, kept_ref, low_ref, mid_ref):
-    refs = [(low_ref, 0), (low_ref, 1), (mid_ref, 0), (mid_ref, 1)]
-    spread(kept_ref, main_ref[...], side_ref[...], refs)
+
+
+def place_rest_kernel(main_ref, side_ref, kept_ref, second_ref):
+    spread(kept_ref, main_ref[...], side_ref[...], second_ref)
 
 
 def limited(a, b):
@@ -330,51 +331,100 @@
     return put
 
 
-def inner_kernel(flag_ref, tab_ref, low_ref, mid_ref, up_ref, once_ref, twice_ref, keep_ref):
-    cells = [(low_ref, 0), (low_ref, 1), (mid_ref, 0), (mid_ref, 1)]
-    cells += [(up_ref, i) for i in range(4)]
+def field(flip, first_ref, second_ref):
+    parts = (second_ref, first_ref) if flip else (first_ref, second_ref)
+    return [(ref, i) for ref in parts for i in range(4)]
+
+
+def turned_main(ref, at, half, cols_back):
+    parts = []
+    for s in range(half * 4, half * 4 + 4):
+        start = at * LINES + s + (7 - 2 * s) * cols_back
+        parts.append(ref[pl.ds(start, PHASES, stride=8), :])
+    return jnp.concatenate(parts, axis=0).T
+
+
+def turned_side(ref, at):
+    line = at * LINES + PHASES * 8
+    empty = jnp.zeros((128 - SHORT * 8, 128), jnp.float32)
+    return jnp.concatenate([ref[line : line + SHORT * 8, :], empty], axis=0).T
+
+
+def inner_kernel(flag_ref, tab_ref, first_ref, second_ref, once_ref, done_ref, twice_ref, keep_ref):
     once = [(once_ref, i) for i in range(5)]
-    for half in halves(tab_ref):
-        base = half[1]
-        substep(cells, None, writer(once_ref, base, 0), keep_ref, *half)
-        put = last_writer(twice_ref, base, 0, flag_ref[1])
-        substep(once, cells[4:6], put, keep_ref, *half)
-
-
-def outer_kernel(flag_ref, tab_ref, below_ref, low_ref, mid_ref, up_ref, above_ref, inner_ref,
-                 inner_twice_ref, out_ref, once_ref, twice_ref, keep_ref, turn_ref, rest_ref):
-    cells = [(below_ref, i) for i in range(4)] + [(low_ref, i) for i in range(2)]
-    cells += [(mid_ref, i) for i in range(2)] + [(up_ref, i) for i in range(4)]
-    cells += [(above_ref, i) for i in range(2)]
+    for flip in range(2):
+
+        @pl.when(flag_ref[2] == flip)
+        def _():
+            cells = field(flip, first_ref, second_ref)
+            for half in halves(tab_ref):
+                base = half[1]
+                substep(cells, None, writer(once_ref, base, 0), keep_ref, *half)
+                put = last_writer(twice_ref, base, 0, flag_ref[1])
+                substep(once, cells[4:6], put, keep_ref, *half)
+
+    for i in range(2):
+        done_ref[i, 0] = turned_main(twice_ref, i, 0, flag_ref[1])
+        done_ref[i, 1] = turned_main(twice_ref, i, 1, flag_ref[1])
+        done_ref[i, 2] = turned_side(twice_ref, i)
+
+
+def outer_kernel(flag_ref, tab_ref, first_ref, second_ref, got_first_ref, got_second_ref, inner_ref,
+                 done_ref, out_hbm, once_ref, twice_ref, keep_ref, turn_ref, rest_ref, last_ref,
+                 sem):
     once = [(once_ref, i) for i in range(4)] + [(inner_ref, i) for i in range(5)]
     once += [(once_ref, i) for i in range(4, 6)]
     rows_back = flag_ref[0]
     cols_back = flag_ref[1]
-    for half in halves(tab_ref):
+    where = [(0, 0), (1, 1), (2, 2), (3, 3), (4, None), (5, None), (6, 4), (7, 5)]
+
+    def compute(half):
         base = half[1]
-        substep(cells[0:7], None, writer(once_ref, base, 0), keep_ref, *half)
-        substep(cells[9:14], None, writer(once_ref, base, 4), keep_ref, *half)
-        put = last_writer(twice_ref, base, 0, cols_back)
-        substep(once[0:7], cells[4:8], put, keep_ref, *half)
-        put = last_writer(twice_ref, base, 4, cols_back)
-        substep(once[6:11], cells[10:12], put, keep_ref, *half)
-
-    where = [(twice_ref, i) for i in range(4)] + [(inner_twice_ref, i) for i in range(2)]
-    where += [(twice_ref, i) for i in range(4, 6)]
-    for e, (ref, at) in enumerate(where):
+        for flip in range(2):
+
+            @pl.when(flag_ref[2] == flip)
+            def _():
+                below, above = got_first_ref, got_second_ref
+                if flip:
+                    below, above = above, below
+                cells = [(below, i) for i in range(4)] + field(flip, first_ref, second_ref)
+                cells += [(above, i) for i in range(2)]
+                substep(cells[0:7], None, writer(once_ref, base, 0), keep_ref, *half)
+                substep(cells[9:14], None, writer(once_ref, base, 4), keep_ref, *half)
+                put = last_writer(twice_ref, base, 0, cols_back)
+                substep(once[0:7], cells[4:8], put, keep_ref, *half)
+                put = last_writer(twice_ref, base, 4, cols_back)
+                substep(once[6:11], cells[10:12], put, keep_ref, *half)
+
+    main, side = halves(tab_ref)
+    copies = [
+        pltpu.make_async_copy(
+            turn_ref.at[half],
+            out_hbm.at[pl.ds(0, MAIN), :, pl.ds(half * 128, 128)],
+            sem.at[half],
+        )
+        for half in range(2)
+    ]
+    count = LOCAL - MAIN
+    copies.append(
+        pltpu.make_async_copy(
+            last_ref.at[pl.ds(0, count)], out_hbm.at[pl.ds(MAIN, count)], sem.at[2]
+        )
+    )
+    compute(main)
+    for half in range(2):
+        lines = turn_ref.at[half].reshape(MAIN * TROWS, 128)
+        for e, at in where:
+            r = e + (TROWS - 1 - 2 * e) * rows_back
+            block = done_ref[e - 4, half]
+            if at is not None:
+                block = turned_main(twice_ref, at, half, cols_back)
+            lines[pl.ds(r, MAIN, stride=TROWS), :] = block
+        copies[half].start()
+    compute(side)
+    for e, at in where:
         r = e + (TROWS - 1 - 2 * e) * rows_back
-        for half in range(2):
-            parts = []
-            for s in range(half * 4, half * 4 + 4):
-                start = at * LINES + s + (7 - 2 * s) * cols_back
-                parts.append(ref[pl.ds(start, PHASES, stride=8), :])
-            block = jnp.concatenate(parts, axis=0).T
-            turn_ref[half, pl.ds(r, MAIN, stride=TROWS), :] = block
-        line = at * LINES + PHASES * 8
-        block = jnp.concatenate(
-            [ref[line : line + SHORT * 8, :], jnp.zeros((128 - SHORT * 8, 128), jnp.float32)],
-            axis=0,
-        ).T
+        block = done_ref[e - 4, 2] if at is None else turned_side(twice_ref, at)
         for pack in range(PACKS):
             rest_ref[pack, pl.ds(r, 32, stride=TROWS), :] = block[pack * 32 : pack * 32 + 32]
     spot = lax.broadcasted_iota(jnp.int32, (PACKS * 128, NY), 0)
@@ -388,13 +438,11 @@
     rest = (value - high.astype(jnp.float32)).astype(jnp.bfloat16)
     value = jnp.dot(high, order, preferred_element_type=jnp.float32)
     value = value + jnp.dot(rest, order, preferred_element_type=jnp.float32)
-    for i in range(LOCAL - MAIN):
-        out_ref[MAIN + i] = value[i * TROWS : (i + 1) * TROWS, :]
-    for i in range(MAIN):
-        for half in range(2):
-            out_ref[i, :, half * 128 : half * 128 + 128] = turn_ref[
-                half, i * TROWS : (i + 1) * TROWS, :
-            ]
+    for i in range(count):
+        last_ref[i] = value[i * TROWS : (i + 1) * TROWS, :]
+    copies[2].start()
+    for copy in copies:
+        copy.wait()
 
 
 def call(kernel, shapes, scratch, ins, *args, limit=20, us=0, outs=None):
@@ -422,7 +470,9 @@
     )
     mirror_x = ((group == 1) | (group == 2)).astype(jnp.int32)
     mirror_y = (group >= 2).astype(jnp.int32)
-    flags = jnp.stack([mirror_x, mirror_y])
+    odd = lax.axis_index("comp") % 2
+    flip = (odd ^ mirror_x).astype(jnp.int32)
+    flags = jnp.stack([mirror_x, mirror_y, flip])
     hbm = pl.BlockSpec(memory_space=pltpu.HBM)
     packed = call(
         pack_kernel,
@@ -448,7 +498,7 @@
         packed.reshape(TILES, 1, SLOTS * 128), "comp", split_axis=0, concat_axis=0, tiled=True
     ).reshape(TILES * SLOTS, 128)
     cells = sea_cell.reshape(TILES, SEND).T
-    cells = cells ^ (mirror_x * (NY * (TROWS - 1)) + mirror_y * (NY - 1))
+    cells = cells ^ (mirror_x * (NY * (TROWS - 1)) + mirror_y * (NY - 1)) ^ (flip * (NY * TROWS // 2))
     hot = call(
         onehot_kernel,
         jax.ShapeDtypeStruct((TROWS * NY, SEA), jnp.bfloat16),
@@ -467,9 +517,9 @@
     )
     partial = lax.all_to_all(partial, "grp", split_axis=0, concat_axis=0, tiled=True)
     bf16 = functools.partial(jax.ShapeDtypeStruct, dtype=jnp.bfloat16)
-    up, main, side, kept = call(
+    first, main, side, kept = call(
         place_kernel,
-        (f32(4, LINES, 128), bf16((256, SEA)), bf16((256, SEA)), bf16((HALF, SEA))),
+        (f32(4, LINES + PAD, 128), bf16((256, SEA)), bf16((256, SEA)), bf16((HALF, SEA))),
         [
             pltpu.VMEM((DEPTH, SEA), jnp.float32),
             pltpu.VMEM((HALF, SEA), jnp.bfloat16),
@@ -483,9 +533,9 @@
         hot,
         limit=44,
     )
-    low, mid = call(
+    second = call(
         place_rest_kernel,
-        (f32(2, LINES, 128), f32(2, LINES, 128)),
+        f32(4, LINES, 128),
         [],
         [VMEM] * 3,
         main,
@@ -493,24 +543,22 @@
         kept,
         us=2,
     )
-    ahead, back = [], []
+    across, within = [], []
     for g in range(GROUPS):
         for i in range(TILES - 1):
-            rise, fall = (g * TILES + i, g * TILES + i + 1), (g * TILES + i + 1, g * TILES + i)
-            ahead.append(fall if g in (1, 2) else rise)
-            back.append(rise if g in (1, 2) else fall)
-    below = lax.ppermute(up, ("grp", "comp"), ahead)
-    above = lax.ppermute(low, ("grp", "comp"), back)
-    once, twice = call(
+            low, high = g * TILES + i, g * TILES + i + 1
+            (across if i % 2 else within).extend([(low, high), (high, low)])
+    got_first = lax.ppermute(first, ("grp", "comp"), across)
+    got_second = lax.ppermute(second, ("grp", "comp"), within)
+    once, done = call(
         inner_kernel,
-        (f32(5, LINES, 128), f32(2 * LINES, 128)),
-        [pltpu.VMEM((5, 2, 8, 128), jnp.float32)],
-        [SMEM] + [VMEM] * 4,
+        (f32(5, LINES, 128), f32(2, 3, 128, 128)),
+        [pltpu.VMEM((2 * LINES, 128), jnp.float32), pltpu.VMEM((5, 2, 8, 128), jnp.float32)],
+        [SMEM] + [VMEM] * 3,
         flags,
         courant,
-        low,
-        mid,
-        up,
+        first,
+        second,
         us=3,
     )
     return call(
@@ -520,19 +568,21 @@
             pltpu.VMEM((6, LINES, 128), jnp.float32),
             pltpu.VMEM((6 * LINES, 128), jnp.float32),
             pltpu.VMEM((4, 2, 8, 128), jnp.float32),
-            pltpu.VMEM((2, MAIN * TROWS, 128), jnp.float32),
+            pltpu.VMEM((2, MAIN, TROWS, 128), jnp.float32),
             pltpu.VMEM((PACKS, 32 * TROWS, 128), jnp.float32),
+            pltpu.VMEM((32, TROWS, NY), jnp.float32),
+            pltpu.SemaphoreType.DMA((3,)),
         ],
-        [SMEM] + [VMEM] * 8,
+        [SMEM] + [VMEM] * 7,
         flags,
         courant,
-        below,
-        low,
-        mid,
-        up,
-        above,
+        first,
+        second,
+        got_first,
+        got_second,
         once,
-        twice,
+        done,
+        outs=hbm,
     )
 
 

time: 84.8 us -> 84.1 us (level)
  starting transfers between devices: 25.1 us -> 21.9 us
  waiting for transfers between devices: 26.7 us -> 29 us
    ppermute x2, starting transfers between devices: 7.67 us -> 4.52 us  [the longest x1 2.6 us: local(): got_second = lax.ppermute(second, ('grp', 'comp'), within)]
    ppermute x2, waiting for transfers between devices: 2.16 us -> 4.52 us  [the longest x1 4.52 us: local(): got_first = lax.ppermute(first, ('grp', 'comp'), across)]
where the time goes in v5:
time: 84.1 us; the launch traced here: 83.8 us
  waiting for transfers between devices  29 us (34%)
  starting transfers between devices  21.9 us (26%)
  Pallas kernels  18.5 us (22%)
  blocking collectives  9.63 us (11%)
  local copies, waits for them, and re-layouts  4.42 us (5%)
    all_to_all x1, waiting for transfers between devices, local(): lax.all_to_all(packed.reshape(TILES, 1, SLOTS * 128), 'comp', split_axis=...  24.5 us
    pallas_call x7, Pallas kernels, call(): pl.pallas_call(kernel, out_shape=shapes, in_specs=ins, out_specs=outs or...  18.5 us
    all_to_all x1, starting transfers between devices, local(): lax.all_to_all(packed.reshape(TILES, 1, SLOTS * 128), 'comp', split_axis=...  17.4 us
    all_to_all x1, blocking collectives, local(): lax.all_to_all(partial, 'grp', split_axis=0, concat_axis=0, tiled=True)  9.63 us
    ppermute x1, waiting for transfers between devices, local(): got_first = lax.ppermute(first, ('grp', 'comp'), across)  4.52 us
    unnamed x4, local copies, waits for them, and re-layouts  2.67 us
    ppermute x1, starting transfers between devices, local(): got_second = lax.ppermute(second, ('grp', 'comp'), within)  2.6 us
    ppermute x1, starting transfers between devices, local(): got_first = lax.ppermute(first, ('grp', 'comp'), across)  1.92 us
  transfers between devices with their start and end apart: 3, of which 2 were waited for; matrix products, arithmetic and copies ran while one was open for 2% of the time, Pallas kernels for 7%

profile of v5, /device:TPU:8, one launch (start us, length us, event | category | flops | bytes accessed | tf_op | source)
XLA Modules:
  0.0 83.8 jit_solution(12484603503393861684)
XLA Ops:
  0.0 0.0 copy-start.1
  0.0 3.0 %shard_map.64 = f32[1920,128]{1,0:T(8,128)} custom-call(f32[150,1536]{1,0:T(8,128)} %x_hbm.1, f32[12,128]{1,0:T(8,128)} %bitcast.15, f32[12,128]{1,0:T(8,128)} %bitcast.16), custom_call_target="tpu_custom_call" | custom-call | tf_op jit(solution)/shard_map/pallas_call | solution.py:450
  3.0 17.4 %all-to-all-start = ((f32[128,1,1920]{2,1,0:T(1,128)}), f32[128,1,1920]{2,1,0:T(1,128)S(1)}, u32[]{:S(2)}, u32[]{:S(2)}) async-start(f32[128,1,1920]{2,1,0:T(1,128)} %bitcast.14), calls=%async_computation | async-start | bytes 1966080 | tf_op jit(solution)/shard_map/all_to_all | solution.py:497
  20.4 0.0 copy-done.1
  20.4 0.1 xor.26
  20.5 0.1 copy.9
  20.6 1.7 %shard_map.65.hot_ref = bf16[2048,1536]{1,0:T(8,128)(2,1)S(1)} custom-call(s32[12,128]{1,0:T(8,128)S(1)} %bitcast.13), custom_call_target="tpu_custom_call" | custom-call | tf_op jit(solution)/shard_map/pallas_call | solution.py:450
  22.3 0.0 copy-start
  22.3 2.7 %copy-done = bf16[2048,1536]{1,0:T(8,128)(2,1)} copy-done((bf16[2048,1536]{1,0:T(8,128)(2,1)}, bf16[2048,1536]{1,0:T(8,128)(2,1)S(1)}, u32[]{:S(2)}) %copy-start) | copy-done | bytes 6291480
  25.0 0.9 %dynamic-slice_bitcast_fusion.tab_ref = f32[152,128]{1,0:T(8,128)S(1)} fusion(f32[4,152,128]{2,1,0:T(8,128)} %constant.44.clone, s32[]{:T(128)S(6)} %select_n.14), kind=kLoop, calls=%fused_computation | loop fusion | bytes 155652 | tf_op jit(solution)/shard_map/jit(dynamic_index_in_dim)/squeeze | solution.py:468
  25.9 24.5 %all-to-all-done = f32[128,1,1920]{2,1,0:T(1,128)S(1)} async-done(((f32[128,1,1920]{2,1,0:T(1,128)}), f32[128,1,1920]{2,1,0:T(1,128)S(1)}, u32[]{:S(2)}, u32[]{:S(2)}) %all-to-all-start) | async-done | bytes 983072 | tf_op jit(solution)/shard_map/all_to_all | solution.py:497
  50.4 0.4 shard_map.66
  50.8 9.6 %all_to_all.10.e_ref = f32[4,24,128]{2,1,0:T(8,128)S(1)} all-to-all(f32[4,24,128]{2,1,0:T(8,128)S(1)} %get-tuple-element.19), channel_id=1, replica_groups=mesh['grp'=4,'comp'=128] {'grp'}, dimensions={0} | all-to-all | bytes 98304 | tf_op jit(solution)/shard_map/all_to_all | solution.py:518
  60.4 3.7 %shard_map.67 = (f32[4,328,128]{2,1,0:T(8,128)S(1)}, bf16[256,1536]{1,0:T(8,128)(2,1)S(1)}, bf16[256,1536]{1,0:T(8,128)(2,1)S(1)}, bf16[1024,1536]{1,0:T(8,128)(2,1)S(1)}) custom-call(f32[12,152,128]{2,1,0:T(8,128)S(1)} %get-tuple-element.17.y_ref, f32[24,128]{1,0:T(8,128)S(1)} %get-tuple-element.18.wind_ref, f32[4,24,128]{2,1,0:T(8,128)S(1)} %all_to_all.10.e_ref, ...), custom_call_target="tpu_custom_call" | custom-call | tf_op jit(solution)/shard_map/pallas_call | solution.py:450
  64.2 1.9 %collective-permute-start = (f32[4,328,128]{2,1,0:T(8,128)S(1)}, f32[4,328,128]{2,1,0:T(8,128)S(1)}, u32[]{:S(2)}, u32[]{:S(2)}) collective-permute-start(f32[4,328,128]{2,1,0:T(8,128)S(1)} %get-tuple-element.21.first_ref), channel_id=1, source_target_pairs={{1,2},{2,1},{3,4},{4,3},{5,6},{6,5},{7,8},{8,7},{9,10},{10,9},{11,... | collective-permute-start | bytes 2015240 | tf_op jit(solution)/shard_map/ppermute | solution.py:551
  66.1 1.8 %shard_map.68.second_ref = f32[4,320,128]{2,1,0:T(8,128)S(1)} custom-call(bf16[256,1536]{1,0:T(8,128)(2,1)S(1)} %get-tuple-element.22.main_ref, bf16[256,1536]{1,0:T(8,128)(2,1)S(1)} %get-tuple-element.23.side_ref, bf16[1024,1536]{1,0:T(8,128)(2,1)S(1)} %get-tuple-element.24.kept_ref), custom_call_target="tpu_custom_call" | custom-call | flops 2000000000 | bytes 6000000 | tf_op jit(solution)/shard_map/pallas_call | solution.py:450
  67.9 2.6 %collective-permute-start.1 = (f32[4,320,128]{2,1,0:T(8,128)S(1)}, f32[4,320,128]{2,1,0:T(8,128)S(1)}, u32[]{:S(2)}, u32[]{:S(2)}) collective-permute-start(f32[4,320,128]{2,1,0:T(8,128)S(1)} %shard_map.68.second_ref), channel_id=1, source_target_pairs={{0,1},{1,0},{2,3},{3,2},{4,5},{5,4},{6,7},{7,6},{8,9},{9,8},{10,11... | collective-permute-start | bytes 1966088 | tf_op jit(solution)/shard_map/ppermute | solution.py:552
  70.5 0.1 pad_add_fusion.flag_ref
  70.6 0.7 dynamic-slice_bitcast_fusion.1.tab_ref
  71.3 2.5 %shard_map.69 = (f32[5,320,128]{2,1,0:T(8,128)S(1)}, f32[2,3,128,128]{3,2,1,0:T(8,128)S(1)}) custom-call(s32[3]{0:T(128)S(1)} %pad_add_fusion.flag_ref, f32[8,256]{1,0:T(8,128)S(1)} %dynamic-slice_bitcast_fusion.1.tab_ref, f32[4,328,128]{2,1,0:T(8,128)S(1)} %get-tuple-element.21.first_ref, f32[4,320,128]{2,1,0:T(8,128)S(1)} %shard_map.68.second_ref), custom_call_target="tpu_custom_call" | custom-call | flops 3000000000 | bytes 9000000 | tf_op jit(solution)/shard_map/pallas_call | solution.py:450
  73.8 0.0 collective-permute-done.1.got_second_ref
  73.8 4.5 %collective-permute-done.got_first_ref = f32[4,328,128]{2,1,0:T(8,128)S(1)} collective-permute-done((f32[4,328,128]{2,1,0:T(8,128)S(1)}, f32[4,328,128]{2,1,0:T(8,128)S(1)}, u32[]{:S(2)}, u32[]{:S(2)}) %collective-permute-start) | collective-permute-done | bytes 671776 | tf_op jit(solution)/shard_map/ppermute | solution.py:551
  78.4 5.4 %shard_map.70 = f32[150,8,256]{2,1,0:T(8,128)} custom-call(s32[3]{0:T(128)S(1)} %pad_add_fusion.flag_ref, f32[8,256]{1,0:T(8,128)S(1)} %dynamic-slice_bitcast_fusion.1.tab_ref, f32[4,328,128]{2,1,0:T(8,128)S(1)} %get-tuple-element.21.first_ref, f32[4,320,128]{2,1,0:T(8,128)S(1)} %shard_map.68.second_ref, ...), custom_call_target="tpu_custom_call" | custom-call | tf_op jit(solution)/shard_map/pallas_call | solution.py:450
  (1 shorter events, 0.0 us)
Async XLA Ops:
  0.0 20.4 %copy-start.1 = (s32[1536]{0:T(1024)S(1)}, s32[1536]{0:T(1024)}, u32[]{:S(2)}) copy-start(s32[1536]{0:T(1024)} %param.9) | copy-start | bytes 18436
  3.0 47.4 %all-to-all-start = ((f32[128,1,1920]{2,1,0:T(1,128)}), f32[128,1,1920]{2,1,0:T(1,128)S(1)}, u32[]{:S(2)}, u32[]{:S(2)}) async-start(f32[128,1,1920]{2,1,0:T(1,128)} %bitcast.14), calls=%async_computation | async-start | bytes 1966080 | tf_op jit(solution)/shard_map/all_to_all | solution.py:497
  22.3 2.7 %copy-start = (bf16[2048,1536]{1,0:T(8,128)(2,1)}, bf16[2048,1536]{1,0:T(8,128)(2,1)S(1)}, u32[]{:S(2)}) copy-start(bf16[2048,1536]{1,0:T(8,128)(2,1)S(1)} %shard_map.65.hot_ref) | copy-start | bytes 18874372
  64.2 14.2 %collective-permute-start = (f32[4,328,128]{2,1,0:T(8,128)S(1)}, f32[4,328,128]{2,1,0:T(8,128)S(1)}, u32[]{:S(2)}, u32[]{:S(2)}) collective-permute-start(f32[4,328,128]{2,1,0:T(8,128)S(1)} %get-tuple-element.21.first_ref), channel_id=1, source_target_pairs={{1,2},{2,1},{3,4},{4,3},{5,6},{6,5},{7,8},{8,7},{9,10},{10,9},{11,... | collective-permute-start | bytes 2015240 | tf_op jit(solution)/shard_map/ppermute | solution.py:551
  67.9 5.9 %collective-permute-start.1 = (f32[4,320,128]{2,1,0:T(8,128)S(1)}, f32[4,320,128]{2,1,0:T(8,128)S(1)}, u32[]{:S(2)}, u32[]{:S(2)}) collective-permute-start(f32[4,320,128]{2,1,0:T(8,128)S(1)} %shard_map.68.second_ref), channel_id=1, source_target_pairs={{0,1},{1,0},{2,3},{3,2},{4,5},{5,4},{6,7},{7,6},{8,9},{9,8},{10,11... | collective-permute-start | bytes 1966088 | tf_op jit(solution)/shard_map/ppermute | solution.py:552

commit v6 on v5

--- a/solution.py
+++ b/solution.py
@@ -369,32 +369,61 @@
         done_ref[i, 2] = turned_side(twice_ref, i)
 
 
-def outer_kernel(flag_ref, tab_ref, first_ref, second_ref, got_first_ref, got_second_ref, inner_ref,
-                 done_ref, out_hbm, once_ref, twice_ref, keep_ref, turn_ref, rest_ref, last_ref,
-                 sem):
-    once = [(once_ref, i) for i in range(4)] + [(inner_ref, i) for i in range(5)]
-    once += [(once_ref, i) for i in range(4, 6)]
+def edge(lower, cells, got_ref, inner_ref, once_ref, twice_ref, keep_ref, cols_back, half):
+    base = half[1]
+    once = [(inner_ref, i) for i in range(5)]
+    if lower:
+        near = [(got_ref, i) for i in range(4)] + cells[0:3]
+        seas, fresh = cells[0:4], [(once_ref, i) for i in range(4)]
+        once = fresh + once[0:3]
+    else:
+        near = cells[5:8] + [(got_ref, i) for i in range(2)]
+        seas, fresh = cells[6:8], [(once_ref, i) for i in range(2)]
+        once = once[2:5] + fresh
+    substep(near, None, writer(once_ref, base, 0), keep_ref, *half)
+    substep(once, seas, last_writer(twice_ref, base, 0, cols_back), keep_ref, *half)
+    return len(seas)
+
+
+def near_kernel(flag_ref, tab_ref, first_ref, second_ref, got_ref, inner_ref, done_ref, once_ref,
+                twice_ref, keep_ref):
+    cols_back = flag_ref[1]
+    for flip in range(2):
+
+        @pl.when(flag_ref[2] == flip)
+        def _():
+            cells = field(flip, first_ref, second_ref)
+            for half in halves(tab_ref):
+                count = edge(flip == 1, cells, got_ref, inner_ref, once_ref, twice_ref, keep_ref,
+                             cols_back, half)
+            for i in range(count):
+                done_ref[i, 0] = turned_main(twice_ref, i, 0, cols_back)
+                done_ref[i, 1] = turned_main(twice_ref, i, 1, cols_back)
+                done_ref[i, 2] = turned_side(twice_ref, i)
+
+
+def outer_kernel(flag_ref, tab_ref, first_ref, second_ref, got_ref, inner_ref, done_ref, near_ref,
+                 out_hbm, once_ref, twice_ref, keep_ref, turn_ref, rest_ref, last_ref, sem):
     rows_back = flag_ref[0]
     cols_back = flag_ref[1]
-    where = [(0, 0), (1, 1), (2, 2), (3, 3), (4, None), (5, None), (6, 4), (7, 5)]
-
-    def compute(half):
-        base = half[1]
-        for flip in range(2):
-
-            @pl.when(flag_ref[2] == flip)
-            def _():
-                below, above = got_first_ref, got_second_ref
-                if flip:
-                    below, above = above, below
-                cells = [(below, i) for i in range(4)] + field(flip, first_ref, second_ref)
-                cells += [(above, i) for i in range(2)]
-                substep(cells[0:7], None, writer(once_ref, base, 0), keep_ref, *half)
-                substep(cells[9:14], None, writer(once_ref, base, 4), keep_ref, *half)
-                put = last_writer(twice_ref, base, 0, cols_back)
-                substep(once[0:7], cells[4:8], put, keep_ref, *half)
-                put = last_writer(twice_ref, base, 4, cols_back)
-                substep(once[6:11], cells[10:12], put, keep_ref, *half)
+
+    def blocks(flip, part):
+        for e in range(TROWS):
+            r = e + (TROWS - 1 - 2 * e) * rows_back
+            if e in (4, 5):
+                yield r, done_ref[e - 4, part]
+                continue
+            lower, at = e < 4, e if e < 4 else e - 6
+            if lower == (flip == 1):
+                yield r, near_ref[at, part]
+            elif part == 2:
+                yield r, turned_side(twice_ref, at)
+            else:
+                yield r, turned_main(twice_ref, at, part, cols_back)
+
+    def compute(flip, half):
+        cells = field(flip, first_ref, second_ref)
+        edge(flip == 0, cells, got_ref, inner_ref, once_ref, twice_ref, keep_ref, cols_back, half)
 
     main, side = halves(tab_ref)
     copies = [
@@ -411,22 +440,29 @@
             last_ref.at[pl.ds(0, count)], out_hbm.at[pl.ds(MAIN, count)], sem.at[2]
         )
     )
-    compute(main)
-    for half in range(2):
-        lines = turn_ref.at[half].reshape(MAIN * TROWS, 128)
-        for e, at in where:
-            r = e + (TROWS - 1 - 2 * e) * rows_back
-            block = done_ref[e - 4, half]
-            if at is not None:
-                block = turned_main(twice_ref, at, half, cols_back)
-            lines[pl.ds(r, MAIN, stride=TROWS), :] = block
-        copies[half].start()
-    compute(side)
-    for e, at in where:
-        r = e + (TROWS - 1 - 2 * e) * rows_back
-        block = done_ref[e - 4, 2] if at is None else turned_side(twice_ref, at)
-        for pack in range(PACKS):
-            rest_ref[pack, pl.ds(r, 32, stride=TROWS), :] = block[pack * 32 : pack * 32 + 32]
+    for flip in range(2):
+
+        @pl.when(flag_ref[2] == flip)
+        def _():
+            compute(flip, main)
+            for half in range(2):
+                lines = turn_ref.at[half].reshape(MAIN * TROWS, 128)
+                for r, block in blocks(flip, half):
+                    lines[pl.ds(r, MAIN, stride=TROWS), :] = block
+
+    copies[0].start()
+    copies[1].start()
+    for flip in range(2):
+
+        @pl.when(flag_ref[2] == flip)
+        def _():
+            compute(flip, side)
+            for r, block in blocks(flip, 2):
+                for pack in range(PACKS):
+                    rest_ref[pack, pl.ds(r, 32, stride=TROWS), :] = block[
+                        pack * 32 : pack * 32 + 32
+                    ]
+
     spot = lax.broadcasted_iota(jnp.int32, (PACKS * 128, NY), 0)
     col = lax.broadcasted_iota(jnp.int32, (PACKS * 128, NY), 1)
     col = col + (NY - 1 - 2 * col) * cols_back
@@ -561,12 +597,29 @@
         second,
         us=3,
     )
+    near = call(
+        near_kernel,
+        f32(4, 3, 128, 128),
+        [
+            pltpu.VMEM((4, LINES, 128), jnp.float32),
+            pltpu.VMEM((4 * LINES, 128), jnp.float32),
+            pltpu.VMEM((4, 2, 8, 128), jnp.float32),
+        ],
+        [SMEM] + [VMEM] * 5,
+        flags,
+        courant,
+        first,
+        second,
+        got_second,
+        once,
+        us=0,
+    )
     return call(
         outer_kernel,
         f32(LOCAL, TROWS, NY),
         [
-            pltpu.VMEM((6, LINES, 128), jnp.float32),
-            pltpu.VMEM((6 * LINES, 128), jnp.float32),
+            pltpu.VMEM((4, LINES, 128), jnp.float32),
+            pltpu.VMEM((4 * LINES, 128), jnp.float32),
             pltpu.VMEM((4, 2, 8, 128), jnp.float32),
             pltpu.VMEM((2, MAIN, TROWS, 128), jnp.float32),
             pltpu.VMEM((PACKS, 32 * TROWS, 128), jnp.float32),
@@ -579,9 +632,9 @@
         first,
         second,
         got_first,
-        got_second,
         once,
         done,
+        near,
         outs=hbm,
     )
 

time: 84.1 us -> 82.8 us (0.985)
  waiting for transfers between devices: 29 us -> 27 us
    ppermute x1, waiting for transfers between devices: 4.52 us -> 2.44 us  [local(): got_first = lax.ppermute(first, ('grp', 'comp'), across)]
    pallas_call x7 -> x8, Pallas kernels: 18.5 us -> 19.3 us  [call(): pl.pallas_call(kernel, out_shape=shapes, in_specs=ins, out_specs=outs or...]
  transfers between devices with their start and end apart: 3 -> 3, of which waited for: 2 -> 2; matrix products, arithmetic and copies ran while one was open for 2% -> 2% of each run, Pallas kernels for 7% -> 10%
where the time goes in v6:
time: 82.8 us; the launch traced here: 82.4 us
  waiting for transfers between devices  27 us (33%)
  starting transfers between devices  21.9 us (26%)
  Pallas kernels  19.3 us (23%)
  blocking collectives  9.63 us (12%)
  local copies, waits for them, and re-layouts  4.42 us (5%)
    all_to_all x1, waiting for transfers between devices, local(): lax.all_to_all(packed.reshape(TILES, 1, SLOTS * 128), 'comp', split_axis=...  24.5 us
    pallas_call x8, Pallas kernels, call(): pl.pallas_call(kernel, out_shape=shapes, in_specs=ins, out_specs=outs or...  19.3 us
    all_to_all x1, starting transfers between devices, local(): lax.all_to_all(packed.reshape(TILES, 1, SLOTS * 128), 'comp', split_axis=...  17.4 us
    all_to_all x1, blocking collectives, local(): lax.all_to_all(partial, 'grp', split_axis=0, concat_axis=0, tiled=True)  9.63 us
    unnamed x4, local copies, waits for them, and re-layouts  2.67 us
    ppermute x1, starting transfers between devices, local(): got_second = lax.ppermute(second, ('grp', 'comp'), within)  2.6 us
    ppermute x1, waiting for transfers between devices, local(): got_first = lax.ppermute(first, ('grp', 'comp'), across)  2.44 us
    ppermute x1, starting transfers between devices, local(): got_first = lax.ppermute(first, ('grp', 'comp'), across)  1.92 us
  transfers between devices with their start and end apart: 3, of which 2 were waited for; matrix products, arithmetic and copies ran while one was open for 2% of the time, Pallas kernels for 10%

profile of v6, /device:TPU:8, one launch (start us, length us, event | category | flops | bytes accessed | tf_op | source)
XLA Modules:
  0.0 82.4 jit_solution(6674394804234703763)
XLA Ops:
  0.0 0.0 copy-start.1
  0.0 3.0 %shard_map.64 = f32[1920,128]{1,0:T(8,128)} custom-call(f32[150,1536]{1,0:T(8,128)} %x_hbm.1, f32[12,128]{1,0:T(8,128)} %bitcast.15, f32[12,128]{1,0:T(8,128)} %bitcast.16), custom_call_target="tpu_custom_call" | custom-call | tf_op jit(solution)/shard_map/pallas_call | solution.py:486
  3.0 17.4 %all-to-all-start = ((f32[128,1,1920]{2,1,0:T(1,128)}), f32[128,1,1920]{2,1,0:T(1,128)S(1)}, u32[]{:S(2)}, u32[]{:S(2)}) async-start(f32[128,1,1920]{2,1,0:T(1,128)} %bitcast.14), calls=%async_computation | async-start | bytes 1966080 | tf_op jit(solution)/shard_map/all_to_all | solution.py:533
  20.4 0.0 copy-done.1
  20.4 0.1 xor.26
  20.5 0.1 copy.9
  20.6 1.7 %shard_map.65.hot_ref = bf16[2048,1536]{1,0:T(8,128)(2,1)S(1)} custom-call(s32[12,128]{1,0:T(8,128)S(1)} %bitcast.13), custom_call_target="tpu_custom_call" | custom-call | tf_op jit(solution)/shard_map/pallas_call | solution.py:486
  22.3 0.0 copy-start
  22.3 2.7 %copy-done = bf16[2048,1536]{1,0:T(8,128)(2,1)} copy-done((bf16[2048,1536]{1,0:T(8,128)(2,1)}, bf16[2048,1536]{1,0:T(8,128)(2,1)S(1)}, u32[]{:S(2)}) %copy-start) | copy-done | bytes 6291480
  25.0 0.9 %dynamic-slice_bitcast_fusion.tab_ref = f32[152,128]{1,0:T(8,128)S(1)} fusion(f32[4,152,128]{2,1,0:T(8,128)} %constant.44.clone, s32[]{:T(128)S(6)} %select_n.14), kind=kLoop, calls=%fused_computation | loop fusion | bytes 155652 | tf_op jit(solution)/shard_map/jit(dynamic_index_in_dim)/squeeze | solution.py:504
  25.9 24.5 %all-to-all-done = f32[128,1,1920]{2,1,0:T(1,128)S(1)} async-done(((f32[128,1,1920]{2,1,0:T(1,128)}), f32[128,1,1920]{2,1,0:T(1,128)S(1)}, u32[]{:S(2)}, u32[]{:S(2)}) %all-to-all-start) | async-done | bytes 983072 | tf_op jit(solution)/shard_map/all_to_all | solution.py:533
  50.4 0.4 shard_map.66
  50.8 9.6 %all_to_all.10.e_ref = f32[4,24,128]{2,1,0:T(8,128)S(1)} all-to-all(f32[4,24,128]{2,1,0:T(8,128)S(1)} %get-tuple-element.19), channel_id=1, replica_groups=mesh['grp'=4,'comp'=128] {'grp'}, dimensions={0} | all-to-all | bytes 98304 | tf_op jit(solution)/shard_map/all_to_all | solution.py:554
  60.4 3.7 %shard_map.67 = (f32[4,328,128]{2,1,0:T(8,128)S(1)}, bf16[256,1536]{1,0:T(8,128)(2,1)S(1)}, bf16[256,1536]{1,0:T(8,128)(2,1)S(1)}, bf16[1024,1536]{1,0:T(8,128)(2,1)S(1)}) custom-call(f32[12,152,128]{2,1,0:T(8,128)S(1)} %get-tuple-element.17.y_ref, f32[24,128]{1,0:T(8,128)S(1)} %get-tuple-element.18.wind_ref, f32[4,24,128]{2,1,0:T(8,128)S(1)} %all_to_all.10.e_ref, ...), custom_call_target="tpu_custom_call" | custom-call | tf_op jit(solution)/shard_map/pallas_call | solution.py:486
  64.2 1.9 %collective-permute-start = (f32[4,328,128]{2,1,0:T(8,128)S(1)}, f32[4,328,128]{2,1,0:T(8,128)S(1)}, u32[]{:S(2)}, u32[]{:S(2)}) collective-permute-start(f32[4,328,128]{2,1,0:T(8,128)S(1)} %get-tuple-element.21.first_ref), channel_id=1, source_target_pairs={{1,2},{2,1},{3,4},{4,3},{5,6},{6,5},{7,8},{8,7},{9,10},{10,9},{11,... | collective-permute-start | bytes 2015240 | tf_op jit(solution)/shard_map/ppermute | solution.py:587
  66.1 1.8 %shard_map.68.second_ref = f32[4,320,128]{2,1,0:T(8,128)S(1)} custom-call(bf16[256,1536]{1,0:T(8,128)(2,1)S(1)} %get-tuple-element.22.main_ref, bf16[256,1536]{1,0:T(8,128)(2,1)S(1)} %get-tuple-element.23.side_ref, bf16[1024,1536]{1,0:T(8,128)(2,1)S(1)} %get-tuple-element.24.kept_ref), custom_call_target="tpu_custom_call" | custom-call | flops 2000000000 | bytes 6000000 | tf_op jit(solution)/shard_map/pallas_call | solution.py:486
  67.9 2.6 %collective-permute-start.1 = (f32[4,320,128]{2,1,0:T(8,128)S(1)}, f32[4,320,128]{2,1,0:T(8,128)S(1)}, u32[]{:S(2)}, u32[]{:S(2)}) collective-permute-start(f32[4,320,128]{2,1,0:T(8,128)S(1)} %shard_map.68.second_ref), channel_id=1, source_target_pairs={{0,1},{1,0},{2,3},{3,2},{4,5},{5,4},{6,7},{7,6},{8,9},{9,8},{10,11... | collective-permute-start | bytes 1966088 | tf_op jit(solution)/shard_map/ppermute | solution.py:588
  70.5 0.1 pad_add_fusion.flag_ref
  70.6 0.7 dynamic-slice_bitcast_fusion.1.tab_ref
  71.3 2.5 %shard_map.69 = (f32[5,320,128]{2,1,0:T(8,128)S(1)}, f32[2,3,128,128]{3,2,1,0:T(8,128)S(1)}) custom-call(s32[3]{0:T(128)S(1)} %pad_add_fusion.flag_ref, f32[8,256]{1,0:T(8,128)S(1)} %dynamic-slice_bitcast_fusion.1.tab_ref, f32[4,328,128]{2,1,0:T(8,128)S(1)} %get-tuple-element.21.first_ref, f32[4,320,128]{2,1,0:T(8,128)S(1)} %shard_map.68.second_ref), custom_call_target="tpu_custom_call" | custom-call | flops 3000000000 | bytes 9000000 | tf_op jit(solution)/shard_map/pallas_call | solution.py:486
  73.8 0.0 collective-permute-done.1.got_ref
  73.8 2.1 %shard_map.70.near_ref = f32[4,3,128,128]{3,2,1,0:T(8,128)S(1)} custom-call(s32[3]{0:T(128)S(1)} %pad_add_fusion.flag_ref, f32[8,256]{1,0:T(8,128)S(1)} %dynamic-slice_bitcast_fusion.1.tab_ref, f32[4,328,128]{2,1,0:T(8,128)S(1)} %get-tuple-element.21.first_ref, f32[4,320,128]{2,1,0:T(8,128)S(1)} %shard_map.68.second_ref, ...), custom_call_target="tpu_custom_call" | custom-call | tf_op jit(solution)/shard_map/pallas_call | solution.py:486
  75.9 2.4 %collective-permute-done.got_ref = f32[4,328,128]{2,1,0:T(8,128)S(1)} collective-permute-done((f32[4,328,128]{2,1,0:T(8,128)S(1)}, f32[4,328,128]{2,1,0:T(8,128)S(1)}, u32[]{:S(2)}, u32[]{:S(2)}) %collective-permute-start) | collective-permute-done | bytes 671776 | tf_op jit(solution)/shard_map/ppermute | solution.py:587
  78.4 4.1 %shard_map.71 = f32[150,8,256]{2,1,0:T(8,128)} custom-call(s32[3]{0:T(128)S(1)} %pad_add_fusion.flag_ref, f32[8,256]{1,0:T(8,128)S(1)} %dynamic-slice_bitcast_fusion.1.tab_ref, f32[4,328,128]{2,1,0:T(8,128)S(1)} %get-tuple-element.21.first_ref, f32[4,320,128]{2,1,0:T(8,128)S(1)} %shard_map.68.second_ref, f32[4,328,128]{2,1,0:T(8,128)S(1)} %collective-permute-done.got_ref, ...), custom_call_target="tpu_custom_call" | custom-call | tf_op jit(solution)/shard_map/pallas_call | solution.py:486
  (1 shorter events, 0.0 us)
Async XLA Ops:
  0.0 20.4 %copy-start.1 = (s32[1536]{0:T(1024)S(1)}, s32[1536]{0:T(1024)}, u32[]{:S(2)}) copy-start(s32[1536]{0:T(1024)} %param.9) | copy-start | bytes 18436
  3.0 47.4 %all-to-all-start = ((f32[128,1,1920]{2,1,0:T(1,128)}), f32[128,1,1920]{2,1,0:T(1,128)S(1)}, u32[]{:S(2)}, u32[]{:S(2)}) async-start(f32[128,1,1920]{2,1,0:T(1,128)} %bitcast.14), calls=%async_computation | async-start | bytes 1966080 | tf_op jit(solution)/shard_map/all_to_all | solution.py:533
  22.3 2.7 %copy-start = (bf16[2048,1536]{1,0:T(8,128)(2,1)}, bf16[2048,1536]{1,0:T(8,128)(2,1)S(1)}, u32[]{:S(2)}) copy-start(bf16[2048,1536]{1,0:T(8,128)(2,1)S(1)} %shard_map.65.hot_ref) | copy-start | bytes 18874372
  64.2 14.2 %collective-permute-start = (f32[4,328,128]{2,1,0:T(8,128)S(1)}, f32[4,328,128]{2,1,0:T(8,128)S(1)}, u32[]{:S(2)}, u32[]{:S(2)}) collective-permute-start(f32[4,328,128]{2,1,0:T(8,128)S(1)} %get-tuple-element.21.first_ref), channel_id=1, source_target_pairs={{1,2},{2,1},{3,4},{4,3},{5,6},{6,5},{7,8},{8,7},{9,10},{10,9},{11,... | collective-permute-start | bytes 2015240 | tf_op jit(solution)/shard_map/ppermute | solution.py:587
  67.9 5.9 %collective-permute-start.1 = (f32[4,320,128]{2,1,0:T(8,128)S(1)}, f32[4,320,128]{2,1,0:T(8,128)S(1)}, u32[]{:S(2)}, u32[]{:S(2)}) collective-permute-start(f32[4,320,128]{2,1,0:T(8,128)S(1)} %shard_map.68.second_ref), channel_id=1, source_target_pairs={{0,1},{1,0},{2,3},{3,2},{4,5},{5,4},{6,7},{7,6},{8,9},{9,8},{10,11... | collective-permute-start | bytes 1966088 | tf_op jit(solution)/shard_map/ppermute | solution.py:588

commit v7 on v6

--- a/solution.py
+++ b/solution.py
@@ -165,18 +165,19 @@
     lax.fori_loop(0, TROWS, body, 0)
 
 
-def spread(held_ref, main, side, ref):
+def spread(held_ref, main, side, ref, packs):
     turned = (((1,), (1,)), ((), ()))
     block = SHORT * 8
-    out = lax.dot_general(held_ref[...], main, turned, preferred_element_type=jnp.float32)
+    hot = held_ref[packs[0] * 4 * block : (packs[-1] + 1) * 4 * block, :]
+    out = lax.dot_general(hot, main, turned, preferred_element_type=jnp.float32)
     out = out[:, 0:128] + out[:, 128:256]
-    rest = lax.dot_general(held_ref[...], side, turned, preferred_element_type=jnp.float32)
+    rest = lax.dot_general(hot, side, turned, preferred_element_type=jnp.float32)
     rest = rest[:, 0:128] + rest[:, 128:256]
     lane = lax.broadcasted_iota(jnp.int32, (block, 128), 1)
     for i in range(4):
-        total = None
-        for pack in range(PACKS):
-            line = (pack * 4 + i) * block
+        total = ref[i, PHASES * 8 : LINES, :] if packs[0] else None
+        for pack in packs:
+            line = ((pack - packs[0]) * 4 + i) * block
             ref[i, pack * block : (pack + 1) * block, :] = out[line : line + block]
             part = rest[line : line + block]
             total = part if total is None else jnp.where(lane < pack * 32, total, part)
@@ -185,10 +186,16 @@
 
 def place_kernel(y_ref, wind_ref, e_ref, tab_ref, hot_ref, first_ref, main_ref, side_ref,
                  kept_ref, s_ref, held_ref, sem):
+    quarter = HALF // 2
     copies = [
-        pltpu.make_async_copy(hot_ref.at[pl.ds(h * HALF, HALF)], ref, sem.at[h])
-        for h, ref in enumerate((held_ref, kept_ref))
+        pltpu.make_async_copy(
+            hot_ref.at[pl.ds(h * quarter, quarter)],
+            held_ref.at[pl.ds(h * quarter, quarter)],
+            sem.at[h],
+        )
+        for h in range(2)
     ]
+    copies.append(pltpu.make_async_copy(hot_ref.at[pl.ds(HALF, HALF)], kept_ref, sem.at[2]))
     copies[0].start()
     copies[1].start()
     moments = e_ref[0] + e_ref[1] + e_ref[2] + e_ref[3]
@@ -222,12 +229,15 @@
         side_ref[128 + pack * 32 : 128 + pack * 32 + 32, :] = rest[MAIN:DEPTH]
     first_ref[:, LINES : LINES + PAD, :] = jnp.zeros((4, PAD, 128), jnp.float32)
     copies[0].wait()
-    spread(held_ref, main_ref[...], side_ref[...], first_ref)
+    copies[2].start()
+    spread(held_ref, main_ref[...], side_ref[...], first_ref, (0, 1))
     copies[1].wait()
+    spread(held_ref, main_ref[...], side_ref[...], first_ref, (2, 3))
+    copies[2].wait()
 
 
 def place_rest_kernel(main_ref, side_ref, kept_ref, second_ref):
-    spread(kept_ref, main_ref[...], side_ref[...], second_ref)
+    spread(kept_ref, main_ref[...], side_ref[...], second_ref, (0, 1, 2, 3))
 
 
 def limited(a, b):
@@ -444,18 +454,6 @@
 
         @pl.when(flag_ref[2] == flip)
         def _():
-            compute(flip, main)
-            for half in range(2):
-                lines = turn_ref.at[half].reshape(MAIN * TROWS, 128)
-                for r, block in blocks(flip, half):
-                    lines[pl.ds(r, MAIN, stride=TROWS), :] = block
-
-    copies[0].start()
-    copies[1].start()
-    for flip in range(2):
-
-        @pl.when(flag_ref[2] == flip)
-        def _():
             compute(flip, side)
             for r, block in blocks(flip, 2):
                 for pack in range(PACKS):
@@ -477,6 +475,22 @@
     for i in range(count):
         last_ref[i] = value[i * TROWS : (i + 1) * TROWS, :]
     copies[2].start()
+    for flip in range(2):
+
+        @pl.when(flag_ref[2] == flip)
+        def _():
+            compute(flip, main)
+
+    for half in range(2):
+        lines = turn_ref.at[half].reshape(MAIN * TROWS, 128)
+        for flip in range(2):
+
+            @pl.when(flag_ref[2] == flip)
+            def _():
+                for r, block in blocks(flip, half):
+                    lines[pl.ds(r, MAIN, stride=TROWS), :] = block
+
+        copies[half].start()
     for copy in copies:
         copy.wait()
 
@@ -559,7 +573,7 @@
         [
             pltpu.VMEM((DEPTH, SEA), jnp.float32),
             pltpu.VMEM((HALF, SEA), jnp.bfloat16),
-            pltpu.SemaphoreType.DMA((2,)),
+            pltpu.SemaphoreType.DMA((3,)),
         ],
         [VMEM] * 4 + [hbm],
         points,

time: 82.8 us -> 82.8 us (level)
  no operation moved by 1% of the time
where the time goes in v7:
time: 82.8 us; the launch traced here: 82.4 us
  waiting for transfers between devices  27 us (33%)
  starting transfers between devices  21.9 us (26%)
  Pallas kernels  19.2 us (23%)
  blocking collectives  9.63 us (12%)
  local copies, waits for them, and re-layouts  4.42 us (5%)
    all_to_all x1, waiting for transfers between devices, local(): lax.all_to_all(packed.reshape(TILES, 1, SLOTS * 128), 'comp', split_axis=...  24.5 us
    pallas_call x8, Pallas kernels, call(): pl.pallas_call(kernel, out_shape=shapes, in_specs=ins, out_specs=outs or...  19.2 us
    all_to_all x1, starting transfers between devices, local(): lax.all_to_all(packed.reshape(TILES, 1, SLOTS * 128), 'comp', split_axis=...  17.4 us
    all_to_all x1, blocking collectives, local(): lax.all_to_all(partial, 'grp', split_axis=0, concat_axis=0, tiled=True)  9.63 us
    unnamed x4, local copies, waits for them, and re-layouts  2.67 us
    ppermute x1, starting transfers between devices, local(): got_second = lax.ppermute(second, ('grp', 'comp'), within)  2.6 us
    ppermute x1, waiting for transfers between devices, local(): got_first = lax.ppermute(first, ('grp', 'comp'), across)  2.45 us
    ppermute x1, starting transfers between devices, local(): got_first = lax.ppermute(first, ('grp', 'comp'), across)  1.92 us
  transfers between devices with their start and end apart: 3, of which 2 were waited for; matrix products, arithmetic and copies ran while one was open for 2% of the time, Pallas kernels for 10%

profile of v7, /device:TPU:8, one launch (start us, length us, event | category | flops | bytes accessed | tf_op | source)
XLA Modules:
  0.0 82.4 jit_solution(4063077860802951469)
XLA Ops:
  0.0 0.0 copy-start.1
  0.0 3.0 %shard_map.64 = f32[1920,128]{1,0:T(8,128)} custom-call(f32[150,1536]{1,0:T(8,128)} %x_hbm.1, f32[12,128]{1,0:T(8,128)} %bitcast.15, f32[12,128]{1,0:T(8,128)} %bitcast.16), custom_call_target="tpu_custom_call" | custom-call | tf_op jit(solution)/shard_map/pallas_call | solution.py:500
  3.0 17.4 %all-to-all-start = ((f32[128,1,1920]{2,1,0:T(1,128)}), f32[128,1,1920]{2,1,0:T(1,128)S(1)}, u32[]{:S(2)}, u32[]{:S(2)}) async-start(f32[128,1,1920]{2,1,0:T(1,128)} %bitcast.14), calls=%async_computation | async-start | bytes 1966080 | tf_op jit(solution)/shard_map/all_to_all | solution.py:547
  20.4 0.0 copy-done.1
  20.4 0.1 xor.26
  20.5 0.1 copy.9
  20.6 1.7 %shard_map.65.hot_ref = bf16[2048,1536]{1,0:T(8,128)(2,1)S(1)} custom-call(s32[12,128]{1,0:T(8,128)S(1)} %bitcast.13), custom_call_target="tpu_custom_call" | custom-call | tf_op jit(solution)/shard_map/pallas_call | solution.py:500
  22.3 0.0 copy-start
  22.3 2.7 %copy-done = bf16[2048,1536]{1,0:T(8,128)(2,1)} copy-done((bf16[2048,1536]{1,0:T(8,128)(2,1)}, bf16[2048,1536]{1,0:T(8,128)(2,1)S(1)}, u32[]{:S(2)}) %copy-start) | copy-done | bytes 6291480
  25.0 0.9 %dynamic-slice_bitcast_fusion.tab_ref = f32[152,128]{1,0:T(8,128)S(1)} fusion(f32[4,152,128]{2,1,0:T(8,128)} %constant.44.clone, s32[]{:T(128)S(6)} %select_n.14), kind=kLoop, calls=%fused_computation | loop fusion | bytes 155652 | tf_op jit(solution)/shard_map/jit(dynamic_index_in_dim)/squeeze | solution.py:518
  25.9 24.5 %all-to-all-done = f32[128,1,1920]{2,1,0:T(1,128)S(1)} async-done(((f32[128,1,1920]{2,1,0:T(1,128)}), f32[128,1,1920]{2,1,0:T(1,128)S(1)}, u32[]{:S(2)}, u32[]{:S(2)}) %all-to-all-start) | async-done | bytes 983072 | tf_op jit(solution)/shard_map/all_to_all | solution.py:547
  50.4 0.4 shard_map.66
  50.8 9.6 %all_to_all.10.e_ref = f32[4,24,128]{2,1,0:T(8,128)S(1)} all-to-all(f32[4,24,128]{2,1,0:T(8,128)S(1)} %get-tuple-element.19), channel_id=1, replica_groups=mesh['grp'=4,'comp'=128] {'grp'}, dimensions={0} | all-to-all | bytes 98304 | tf_op jit(solution)/shard_map/all_to_all | solution.py:568
  60.4 3.5 %shard_map.67 = (f32[4,328,128]{2,1,0:T(8,128)S(1)}, bf16[256,1536]{1,0:T(8,128)(2,1)S(1)}, bf16[256,1536]{1,0:T(8,128)(2,1)S(1)}, bf16[1024,1536]{1,0:T(8,128)(2,1)S(1)}) custom-call(f32[12,152,128]{2,1,0:T(8,128)S(1)} %get-tuple-element.17.y_ref, f32[24,128]{1,0:T(8,128)S(1)} %get-tuple-element.18.wind_ref, f32[4,24,128]{2,1,0:T(8,128)S(1)} %all_to_all.10.e_ref, ...), custom_call_target="tpu_custom_call" | custom-call | tf_op jit(solution)/shard_map/pallas_call | solution.py:500
  63.9 1.9 %collective-permute-start = (f32[4,328,128]{2,1,0:T(8,128)S(1)}, f32[4,328,128]{2,1,0:T(8,128)S(1)}, u32[]{:S(2)}, u32[]{:S(2)}) collective-permute-start(f32[4,328,128]{2,1,0:T(8,128)S(1)} %get-tuple-element.21.first_ref), channel_id=1, source_target_pairs={{1,2},{2,1},{3,4},{4,3},{5,6},{6,5},{7,8},{8,7},{9,10},{10,9},{11,... | collective-permute-start | bytes 2015240 | tf_op jit(solution)/shard_map/ppermute | solution.py:601
  65.8 1.8 %shard_map.68.second_ref = f32[4,320,128]{2,1,0:T(8,128)S(1)} custom-call(bf16[256,1536]{1,0:T(8,128)(2,1)S(1)} %get-tuple-element.22.main_ref, bf16[256,1536]{1,0:T(8,128)(2,1)S(1)} %get-tuple-element.23.side_ref, bf16[1024,1536]{1,0:T(8,128)(2,1)S(1)} %get-tuple-element.24.kept_ref), custom_call_target="tpu_custom_call" | custom-call | flops 2000000000 | bytes 6000000 | tf_op jit(solution)/shard_map/pallas_call | solution.py:500
  67.7 2.6 %collective-permute-start.1 = (f32[4,320,128]{2,1,0:T(8,128)S(1)}, f32[4,320,128]{2,1,0:T(8,128)S(1)}, u32[]{:S(2)}, u32[]{:S(2)}) collective-permute-start(f32[4,320,128]{2,1,0:T(8,128)S(1)} %shard_map.68.second_ref), channel_id=1, source_target_pairs={{0,1},{1,0},{2,3},{3,2},{4,5},{5,4},{6,7},{7,6},{8,9},{9,8},{10,11... | collective-permute-start | bytes 1966088 | tf_op jit(solution)/shard_map/ppermute | solution.py:602
  70.3 0.1 pad_add_fusion.flag_ref
  70.3 0.7 dynamic-slice_bitcast_fusion.1.tab_ref
  71.0 2.5 %shard_map.69 = (f32[5,320,128]{2,1,0:T(8,128)S(1)}, f32[2,3,128,128]{3,2,1,0:T(8,128)S(1)}) custom-call(s32[3]{0:T(128)S(1)} %pad_add_fusion.flag_ref, f32[8,256]{1,0:T(8,128)S(1)} %dynamic-slice_bitcast_fusion.1.tab_ref, f32[4,328,128]{2,1,0:T(8,128)S(1)} %get-tuple-element.21.first_ref, f32[4,320,128]{2,1,0:T(8,128)S(1)} %shard_map.68.second_ref), custom_call_target="tpu_custom_call" | custom-call | flops 3000000000 | bytes 9000000 | tf_op jit(solution)/shard_map/pallas_call | solution.py:500
  73.6 0.0 collective-permute-done.1.got_ref
  73.6 2.1 %shard_map.70.near_ref = f32[4,3,128,128]{3,2,1,0:T(8,128)S(1)} custom-call(s32[3]{0:T(128)S(1)} %pad_add_fusion.flag_ref, f32[8,256]{1,0:T(8,128)S(1)} %dynamic-slice_bitcast_fusion.1.tab_ref, f32[4,328,128]{2,1,0:T(8,128)S(1)} %get-tuple-element.21.first_ref, f32[4,320,128]{2,1,0:T(8,128)S(1)} %shard_map.68.second_ref, ...), custom_call_target="tpu_custom_call" | custom-call | tf_op jit(solution)/shard_map/pallas_call | solution.py:500
  75.6 2.5 %collective-permute-done.got_ref = f32[4,328,128]{2,1,0:T(8,128)S(1)} collective-permute-done((f32[4,328,128]{2,1,0:T(8,128)S(1)}, f32[4,328,128]{2,1,0:T(8,128)S(1)}, u32[]{:S(2)}, u32[]{:S(2)}) %collective-permute-start) | collective-permute-done | bytes 671776 | tf_op jit(solution)/shard_map/ppermute | solution.py:601
  78.1 4.3 %shard_map.71 = f32[150,8,256]{2,1,0:T(8,128)} custom-call(s32[3]{0:T(128)S(1)} %pad_add_fusion.flag_ref, f32[8,256]{1,0:T(8,128)S(1)} %dynamic-slice_bitcast_fusion.1.tab_ref, f32[4,328,128]{2,1,0:T(8,128)S(1)} %get-tuple-element.21.first_ref, f32[4,320,128]{2,1,0:T(8,128)S(1)} %shard_map.68.second_ref, f32[4,328,128]{2,1,0:T(8,128)S(1)} %collective-permute-done.got_ref, ...), custom_call_target="tpu_custom_call" | custom-call | tf_op jit(solution)/shard_map/pallas_call | solution.py:500
  (1 shorter events, 0.0 us)
Async XLA Ops:
  0.0 20.4 %copy-start.1 = (s32[1536]{0:T(1024)S(1)}, s32[1536]{0:T(1024)}, u32[]{:S(2)}) copy-start(s32[1536]{0:T(1024)} %param.9) | copy-start | bytes 18436
  3.0 47.4 %all-to-all-start = ((f32[128,1,1920]{2,1,0:T(1,128)}), f32[128,1,1920]{2,1,0:T(1,128)S(1)}, u32[]{:S(2)}, u32[]{:S(2)}) async-start(f32[128,1,1920]{2,1,0:T(1,128)} %bitcast.14), calls=%async_computation | async-start | bytes 1966080 | tf_op jit(solution)/shard_map/all_to_all | solution.py:547
  22.3 2.7 %copy-start = (bf16[2048,1536]{1,0:T(8,128)(2,1)}, bf16[2048,1536]{1,0:T(8,128)(2,1)S(1)}, u32[]{:S(2)}) copy-start(bf16[2048,1536]{1,0:T(8,128)(2,1)S(1)} %shard_map.65.hot_ref) | copy-start | bytes 18874372
  63.9 14.2 %collective-permute-start = (f32[4,328,128]{2,1,0:T(8,128)S(1)}, f32[4,328,128]{2,1,0:T(8,128)S(1)}, u32[]{:S(2)}, u32[]{:S(2)}) collective-permute-start(f32[4,328,128]{2,1,0:T(8,128)S(1)} %get-tuple-element.21.first_ref), channel_id=1, source_target_pairs={{1,2},{2,1},{3,4},{4,3},{5,6},{6,5},{7,8},{8,7},{9,10},{10,9},{11,... | collective-permute-start | bytes 2015240 | tf_op jit(solution)/shard_map/ppermute | solution.py:601
  67.7 5.9 %collective-permute-start.1 = (f32[4,320,128]{2,1,0:T(8,128)S(1)}, f32[4,320,128]{2,1,0:T(8,128)S(1)}, u32[]{:S(2)}, u32[]{:S(2)}) collective-permute-start(f32[4,320,128]{2,1,0:T(8,128)S(1)} %shard_map.68.second_ref), channel_id=1, source_target_pairs={{0,1},{1,0},{2,3},{3,2},{4,5},{5,4},{6,7},{7,6},{8,9},{9,8},{10,11... | collective-permute-start | bytes 1966088 | tf_op jit(solution)/shard_map/ppermute | solution.py:602

commit v8 on v7

--- a/solution.py
+++ b/solution.py
@@ -29,7 +29,6 @@
 FREQ_STEP = 1.1
 
 VMEM = pl.BlockSpec(memory_space=pltpu.VMEM)
-SMEM = pl.BlockSpec(memory_space=pltpu.SMEM)
 
 W_E, W_I, C_COS, C_SIN, C_OUT = range(5)
 PHASES = 32
@@ -90,21 +89,25 @@
     ins[0].start()
     winds[0].start()
     winds[1].start()
-    for c in range(1, PARTS):
-        ins[c].start()
-    b_ref[EXTRA:128, :] = jnp.zeros((128 - EXTRA, width), jnp.float32)
+    ins[1].start()
+    b_ref[PER_TILE * EXTRA : 128, :] = jnp.zeros((128 - PER_TILE * EXTRA, width), jnp.float32)
+    lane = lax.broadcasted_iota(jnp.int32, (tiles, 128), 1)
     for c in range(PARTS):
         ins[c].wait()
+        if c + 2 < PARTS:
+            ins[c + 2].start()
         if c == 0:
             winds[0].wait()
             winds[1].wait()
-        b_ref[0 : LOCAL - MAIN, :] = x_ref[c, MAIN:LOCAL, :]
+        for copy in range(PER_TILE):
+            b_ref[copy * EXTRA : copy * EXTRA + LOCAL - MAIN, :] = x_ref[c, MAIN:LOCAL, :]
         for block in range(width // 128):
             cols = slice(block * 128, block * 128 + 128)
             at = c * (width // 128) + block
-            for i in range(2):
-                row = LOCAL - MAIN + i
-                b_ref[row : row + 1, cols] = wind_ref[i, at : at + 1, :]
+            for copy in range(PER_TILE):
+                for i in range(2):
+                    row = copy * EXTRA + LOCAL - MAIN + i
+                    b_ref[row : row + 1, cols] = wind_ref[i, at : at + 1, :]
             z_ref[0, cols, :] = x_ref[c, 0:MAIN, cols].T
             z_ref[1, cols, :] = b_ref[:, cols].T
         first = c * tiles * SLOTS
@@ -116,9 +119,8 @@
             total = None
             for k in range(tile * PER_TILE, min(SEND, (tile + 1) * PER_TILE)):
                 piece = z_ref[1, pl.ds(k, tiles, stride=SEND), :]
-                shift = (k % PER_TILE) * EXTRA
-                piece = pltpu.roll(piece, shift, 1) if shift else piece
-                total = piece if total is None else total + piece
+                start = (k % PER_TILE) * EXTRA
+                total = piece if total is None else jnp.where(lane < start, total, piece)
             m_ref[pl.ds(first + SEND + tile, tiles, stride=SLOTS), :] = total
         outs[c].start()
     for c in range(PARTS):
@@ -313,6 +315,14 @@
     lax.fori_loop(0, phases // CHUNK, body, 0)
 
 
+def flags():
+    group = lax.axis_index("grp")
+    mirror_x = ((group == 1) | (group == 2)).astype(jnp.int32)
+    mirror_y = (group >= 2).astype(jnp.int32)
+    odd = lax.axis_index("comp").astype(jnp.int32) % 2
+    return mirror_x, mirror_y, odd ^ mirror_x
+
+
 def halves(tab_ref):
     for base, phases, lanes, after, before in (
         (0, PHASES, 0, next_main, last_main),
@@ -360,22 +370,23 @@
     return jnp.concatenate([ref[line : line + SHORT * 8, :], empty], axis=0).T
 
 
-def inner_kernel(flag_ref, tab_ref, first_ref, second_ref, once_ref, done_ref, twice_ref, keep_ref):
+def inner_kernel(tab_ref, first_ref, second_ref, once_ref, done_ref, twice_ref, keep_ref):
     once = [(once_ref, i) for i in range(5)]
+    _, cols_back, side_up = flags()
     for flip in range(2):
 
-        @pl.when(flag_ref[2] == flip)
+        @pl.when(side_up == flip)
         def _():
             cells = field(flip, first_ref, second_ref)
             for half in halves(tab_ref):
                 base = half[1]
                 substep(cells, None, writer(once_ref, base, 0), keep_ref, *half)
-                put = last_writer(twice_ref, base, 0, flag_ref[1])
+                put = last_writer(twice_ref, base, 0, cols_back)
                 substep(once, cells[4:6], put, keep_ref, *half)
 
     for i in range(2):
-        done_ref[i, 0] = turned_main(twice_ref, i, 0, flag_ref[1])
-        done_ref[i, 1] = turned_main(twice_ref, i, 1, flag_ref[1])
+        done_ref[i, 0] = turned_main(twice_ref, i, 0, cols_back)
+        done_ref[i, 1] = turned_main(twice_ref, i, 1, cols_back)
         done_ref[i, 2] = turned_side(twice_ref, i)
 
 
@@ -395,12 +406,12 @@
     return len(seas)
 
 
-def near_kernel(flag_ref, tab_ref, first_ref, second_ref, got_ref, inner_ref, done_ref, once_ref,
+def near_kernel(tab_ref, first_ref, second_ref, got_ref, inner_ref, done_ref, once_ref,
                 twice_ref, keep_ref):
-    cols_back = flag_ref[1]
+    _, cols_back, side_up = flags()
     for flip in range(2):
 
-        @pl.when(flag_ref[2] == flip)
+        @pl.when(side_up == flip)
         def _():
             cells = field(flip, first_ref, second_ref)
             for half in halves(tab_ref):
@@ -412,10 +423,9 @@
                 done_ref[i, 2] = turned_side(twice_ref, i)
 
 
-def outer_kernel(flag_ref, tab_ref, first_ref, second_ref, got_ref, inner_ref, done_ref, near_ref,
+def outer_kernel(tab_ref, first_ref, second_ref, got_ref, inner_ref, done_ref, near_ref,
                  out_hbm, once_ref, twice_ref, keep_ref, turn_ref, rest_ref, last_ref, sem):
-    rows_back = flag_ref[0]
-    cols_back = flag_ref[1]
+    rows_back, cols_back, side_up = flags()
 
     def blocks(flip, part):
         for e in range(TROWS):
@@ -452,7 +462,7 @@
     )
     for flip in range(2):
 
-        @pl.when(flag_ref[2] == flip)
+        @pl.when(side_up == flip)
         def _():
             compute(flip, side)
             for r, block in blocks(flip, 2):
@@ -477,7 +487,7 @@
     copies[2].start()
     for flip in range(2):
 
-        @pl.when(flag_ref[2] == flip)
+        @pl.when(side_up == flip)
         def _():
             compute(flip, main)
 
@@ -485,7 +495,7 @@
         lines = turn_ref.at[half].reshape(MAIN * TROWS, 128)
         for flip in range(2):
 
-            @pl.when(flag_ref[2] == flip)
+            @pl.when(side_up == flip)
             def _():
                 for r, block in blocks(flip, half):
                     lines[pl.ds(r, MAIN, stride=TROWS), :] = block
@@ -518,11 +528,7 @@
         lax.dynamic_index_in_dim(jnp.asarray(t), group, 0, keepdims=False)
         for t in coefficient_tables()
     )
-    mirror_x = ((group == 1) | (group == 2)).astype(jnp.int32)
-    mirror_y = (group >= 2).astype(jnp.int32)
-    odd = lax.axis_index("comp") % 2
-    flip = (odd ^ mirror_x).astype(jnp.int32)
-    flags = jnp.stack([mirror_x, mirror_y, flip])
+    mirror_x, mirror_y, flip = flags()
     hbm = pl.BlockSpec(memory_space=pltpu.HBM)
     packed = call(
         pack_kernel,
@@ -604,8 +610,7 @@
         inner_kernel,
         (f32(5, LINES, 128), f32(2, 3, 128, 128)),
         [pltpu.VMEM((2 * LINES, 128), jnp.float32), pltpu.VMEM((5, 2, 8, 128), jnp.float32)],
-        [SMEM] + [VMEM] * 3,
-        flags,
+        [VMEM] * 3,
         courant,
         first,
         second,
@@ -619,8 +624,7 @@
             pltpu.VMEM((4 * LINES, 128), jnp.float32),
             pltpu.VMEM((4, 2, 8, 128), jnp.float32),
         ],
-        [SMEM] + [VMEM] * 5,
-        flags,
+        [VMEM] * 5,
         courant,
         first,
         second,
@@ -640,8 +644,7 @@
             pltpu.VMEM((32, TROWS, NY), jnp.float32),
             pltpu.SemaphoreType.DMA((3,)),
         ],
-        [SMEM] + [VMEM] * 7,
-        flags,
+        [VMEM] * 7,
         courant,
         first,
         second,

time: 82.8 us -> 82.2 us (level)
  Pallas kernels: 19.2 us -> 17.6 us
  waiting for transfers between devices: 27 us -> 28.1 us
    pallas_call x8, Pallas kernels: 19.2 us -> 17.6 us  [call(): pl.pallas_call(kernel, out_shape=shapes, in_specs=ins, out_specs=outs or...]
    ppermute x1, waiting for transfers between devices: 2.45 us -> 3.61 us  [local(): got_first = lax.ppermute(first, ('grp', 'comp'), across)]
  transfers between devices with their start and end apart: 3 -> 3, of which waited for: 2 -> 2; matrix products, arithmetic and copies ran while one was open for 2% -> 2% of each run, Pallas kernels for 10% -> 9%
where the time goes in v8:
time: 82.2 us; the launch traced here: 81.8 us
  waiting for transfers between devices  28.1 us (34%)
  starting transfers between devices  21.9 us (27%)
  Pallas kernels  17.6 us (21%)
  blocking collectives  9.63 us (12%)
  local copies, waits for them, and re-layouts  4.42 us (5%)
    all_to_all x1, waiting for transfers between devices, local(): lax.all_to_all(packed.reshape(TILES, 1, SLOTS * 128), 'comp', split_axis=...  24.5 us
    pallas_call x8, Pallas kernels, call(): pl.pallas_call(kernel, out_shape=shapes, in_specs=ins, out_specs=outs or...  17.6 us
    all_to_all x1, starting transfers between devices, local(): lax.all_to_all(packed.reshape(TILES, 1, SLOTS * 128), 'comp', split_axis=...  17.4 us
    all_to_all x1, blocking collectives, local(): lax.all_to_all(partial, 'grp', split_axis=0, concat_axis=0, tiled=True)  9.63 us
    ppermute x1, waiting for transfers between devices, local(): got_first = lax.ppermute(first, ('grp', 'comp'), across)  3.61 us
    unnamed x4, local copies, waits for them, and re-layouts  2.67 us
    ppermute x1, starting transfers between devices, local(): got_second = lax.ppermute(second, ('grp', 'comp'), within)  2.6 us
    ppermute x1, starting transfers between devices, local(): got_first = lax.ppermute(first, ('grp', 'comp'), across)  1.92 us
  transfers between devices with their start and end apart: 3, of which 2 were waited for; matrix products, arithmetic and copies ran while one was open for 2% of the time, Pallas kernels for 9%

profile of v8, /device:TPU:8, one launch (start us, length us, event | category | flops | bytes accessed | tf_op | source)
XLA Modules:
  0.0 81.8 jit_solution(9081220079212975269)
XLA Ops:
  0.0 0.0 copy-start.1
  0.0 3.2 %shard_map.64 = f32[1920,128]{1,0:T(8,128)} custom-call(f32[150,1536]{1,0:T(8,128)} %x_hbm.1, f32[12,128]{1,0:T(8,128)} %bitcast.12, f32[12,128]{1,0:T(8,128)} %bitcast.13), custom_call_target="tpu_custom_call" | custom-call | tf_op jit(solution)/shard_map/pallas_call | solution.py:510
  3.2 17.4 %all-to-all-start = ((f32[128,1,1920]{2,1,0:T(1,128)}), f32[128,1,1920]{2,1,0:T(1,128)S(1)}, u32[]{:S(2)}, u32[]{:S(2)}) async-start(f32[128,1,1920]{2,1,0:T(1,128)} %bitcast.11), calls=%async_computation | async-start | bytes 1966080 | tf_op jit(solution)/shard_map/all_to_all | solution.py:553
  20.6 0.0 copy-done.1
  20.6 0.1 xor.26
  20.7 0.1 copy.9
  20.8 1.7 %shard_map.65.hot_ref = bf16[2048,1536]{1,0:T(8,128)(2,1)S(1)} custom-call(s32[12,128]{1,0:T(8,128)S(1)} %bitcast.10), custom_call_target="tpu_custom_call" | custom-call | tf_op jit(solution)/shard_map/pallas_call | solution.py:510
  22.5 0.0 copy-start
  22.5 2.7 %copy-done = bf16[2048,1536]{1,0:T(8,128)(2,1)} copy-done((bf16[2048,1536]{1,0:T(8,128)(2,1)}, bf16[2048,1536]{1,0:T(8,128)(2,1)S(1)}, u32[]{:S(2)}) %copy-start) | copy-done | bytes 6291480
  25.2 0.9 %dynamic-slice_bitcast_fusion.tab_ref = f32[152,128]{1,0:T(8,128)S(1)} fusion(f32[4,152,128]{2,1,0:T(8,128)} %constant.44.clone, s32[]{:T(128)S(6)} %select_n.13), kind=kLoop, calls=%fused_computation | loop fusion | bytes 155652 | tf_op jit(solution)/shard_map/jit(dynamic_index_in_dim)/squeeze | solution.py:528
  26.1 24.5 %all-to-all-done = f32[128,1,1920]{2,1,0:T(1,128)S(1)} async-done(((f32[128,1,1920]{2,1,0:T(1,128)}), f32[128,1,1920]{2,1,0:T(1,128)S(1)}, u32[]{:S(2)}, u32[]{:S(2)}) %all-to-all-start) | async-done | bytes 983072 | tf_op jit(solution)/shard_map/all_to_all | solution.py:553
  50.6 0.4 shard_map.66
  51.0 9.6 %all_to_all.10.e_ref = f32[4,24,128]{2,1,0:T(8,128)S(1)} all-to-all(f32[4,24,128]{2,1,0:T(8,128)S(1)} %get-tuple-element.19), channel_id=1, replica_groups=mesh['grp'=4,'comp'=128] {'grp'}, dimensions={0} | all-to-all | bytes 98304 | tf_op jit(solution)/shard_map/all_to_all | solution.py:574
  60.6 3.5 %shard_map.67 = (f32[4,328,128]{2,1,0:T(8,128)S(1)}, bf16[256,1536]{1,0:T(8,128)(2,1)S(1)}, bf16[256,1536]{1,0:T(8,128)(2,1)S(1)}, bf16[1024,1536]{1,0:T(8,128)(2,1)S(1)}) custom-call(f32[12,152,128]{2,1,0:T(8,128)S(1)} %get-tuple-element.17.y_ref, f32[24,128]{1,0:T(8,128)S(1)} %get-tuple-element.18.wind_ref, f32[4,24,128]{2,1,0:T(8,128)S(1)} %all_to_all.10.e_ref, ...), custom_call_target="tpu_custom_call" | custom-call | tf_op jit(solution)/shard_map/pallas_call | solution.py:510
  64.1 1.9 %collective-permute-start = (f32[4,328,128]{2,1,0:T(8,128)S(1)}, f32[4,328,128]{2,1,0:T(8,128)S(1)}, u32[]{:S(2)}, u32[]{:S(2)}) collective-permute-start(f32[4,328,128]{2,1,0:T(8,128)S(1)} %get-tuple-element.21.first_ref), channel_id=1, source_target_pairs={{1,2},{2,1},{3,4},{4,3},{5,6},{6,5},{7,8},{8,7},{9,10},{10,9},{11,... | collective-permute-start | bytes 2015240 | tf_op jit(solution)/shard_map/ppermute | solution.py:607
  66.0 1.8 %shard_map.68.second_ref = f32[4,320,128]{2,1,0:T(8,128)S(1)} custom-call(bf16[256,1536]{1,0:T(8,128)(2,1)S(1)} %get-tuple-element.22.main_ref, bf16[256,1536]{1,0:T(8,128)(2,1)S(1)} %get-tuple-element.23.side_ref, bf16[1024,1536]{1,0:T(8,128)(2,1)S(1)} %get-tuple-element.24.kept_ref), custom_call_target="tpu_custom_call" | custom-call | flops 2000000000 | bytes 6000000 | tf_op jit(solution)/shard_map/pallas_call | solution.py:510
  67.9 2.6 %collective-permute-start.1 = (f32[4,320,128]{2,1,0:T(8,128)S(1)}, f32[4,320,128]{2,1,0:T(8,128)S(1)}, u32[]{:S(2)}, u32[]{:S(2)}) collective-permute-start(f32[4,320,128]{2,1,0:T(8,128)S(1)} %shard_map.68.second_ref), channel_id=1, source_target_pairs={{0,1},{1,0},{2,3},{3,2},{4,5},{5,4},{6,7},{7,6},{8,9},{9,8},{10,11... | collective-permute-start | bytes 1966088 | tf_op jit(solution)/shard_map/ppermute | solution.py:608
  70.5 0.7 dynamic-slice_bitcast_fusion.1.tab_ref
  71.2 2.0 %shard_map.69 = (f32[5,320,128]{2,1,0:T(8,128)S(1)}, f32[2,3,128,128]{3,2,1,0:T(8,128)S(1)}) custom-call(f32[8,256]{1,0:T(8,128)S(1)} %dynamic-slice_bitcast_fusion.1.tab_ref, f32[4,328,128]{2,1,0:T(8,128)S(1)} %get-tuple-element.21.first_ref, f32[4,320,128]{2,1,0:T(8,128)S(1)} %shard_map.68.second_ref), custom_call_target="tpu_custom_call" | custom-call | flops 3000000000 | bytes 9000000 | tf_op jit(solution)/shard_map/pallas_call | solution.py:510
  73.1 0.0 collective-permute-done.1.got_ref
  73.1 1.5 %shard_map.70.near_ref = f32[4,3,128,128]{3,2,1,0:T(8,128)S(1)} custom-call(f32[8,256]{1,0:T(8,128)S(1)} %dynamic-slice_bitcast_fusion.1.tab_ref, f32[4,328,128]{2,1,0:T(8,128)S(1)} %get-tuple-element.21.first_ref, f32[4,320,128]{2,1,0:T(8,128)S(1)} %shard_map.68.second_ref, f32[4,320,128]{2,1,0:T(8,128)S(1)} %collective-permute-done.1.got_ref, ...), custom_call_target="tpu_custom_call" | custom-call | tf_op jit(solution)/shard_map/pallas_call | solution.py:510
  74.7 3.6 %collective-permute-done.got_ref = f32[4,328,128]{2,1,0:T(8,128)S(1)} collective-permute-done((f32[4,328,128]{2,1,0:T(8,128)S(1)}, f32[4,328,128]{2,1,0:T(8,128)S(1)}, u32[]{:S(2)}, u32[]{:S(2)}) %collective-permute-start) | collective-permute-done | bytes 671776 | tf_op jit(solution)/shard_map/ppermute | solution.py:607
  78.3 3.5 %shard_map.71 = f32[150,8,256]{2,1,0:T(8,128)} custom-call(f32[8,256]{1,0:T(8,128)S(1)} %dynamic-slice_bitcast_fusion.1.tab_ref, f32[4,328,128]{2,1,0:T(8,128)S(1)} %get-tuple-element.21.first_ref, f32[4,320,128]{2,1,0:T(8,128)S(1)} %shard_map.68.second_ref, f32[4,328,128]{2,1,0:T(8,128)S(1)} %collective-permute-done.got_ref, ...), custom_call_target="tpu_custom_call" | custom-call | tf_op jit(solution)/shard_map/pallas_call | solution.py:510
  (1 shorter events, 0.0 us)
Async XLA Ops:
  0.0 20.6 %copy-start.1 = (s32[1536]{0:T(1024)S(1)}, s32[1536]{0:T(1024)}, u32[]{:S(2)}) copy-start(s32[1536]{0:T(1024)} %param.9) | copy-start | bytes 18436
  3.2 47.4 %all-to-all-start = ((f32[128,1,1920]{2,1,0:T(1,128)}), f32[128,1,1920]{2,1,0:T(1,128)S(1)}, u32[]{:S(2)}, u32[]{:S(2)}) async-start(f32[128,1,1920]{2,1,0:T(1,128)} %bitcast.11), calls=%async_computation | async-start | bytes 1966080 | tf_op jit(solution)/shard_map/all_to_all | solution.py:553
  22.5 2.7 %copy-start = (bf16[2048,1536]{1,0:T(8,128)(2,1)}, bf16[2048,1536]{1,0:T(8,128)(2,1)S(1)}, u32[]{:S(2)}) copy-start(bf16[2048,1536]{1,0:T(8,128)(2,1)S(1)} %shard_map.65.hot_ref) | copy-start | bytes 18874372
  64.1 14.2 %collective-permute-start = (f32[4,328,128]{2,1,0:T(8,128)S(1)}, f32[4,328,128]{2,1,0:T(8,128)S(1)}, u32[]{:S(2)}, u32[]{:S(2)}) collective-permute-start(f32[4,328,128]{2,1,0:T(8,128)S(1)} %get-tuple-element.21.first_ref), channel_id=1, source_target_pairs={{1,2},{2,1},{3,4},{4,3},{5,6},{6,5},{7,8},{8,7},{9,10},{10,9},{11,... | collective-permute-start | bytes 2015240 | tf_op jit(solution)/shard_map/ppermute | solution.py:607
  67.9 5.3 %collective-permute-start.1 = (f32[4,320,128]{2,1,0:T(8,128)S(1)}, f32[4,320,128]{2,1,0:T(8,128)S(1)}, u32[]{:S(2)}, u32[]{:S(2)}) collective-permute-start(f32[4,320,128]{2,1,0:T(8,128)S(1)} %shard_map.68.second_ref), channel_id=1, source_target_pairs={{0,1},{1,0},{2,3},{3,2},{4,5},{5,4},{6,7},{7,6},{8,9},{9,8},{10,11... | collective-permute-start | bytes 1966088 | tf_op jit(solution)/shard_map/ppermute | solution.py:608

commit v9 on v8

--- a/solution.py
+++ b/solution.py
@@ -89,13 +89,12 @@
     ins[0].start()
     winds[0].start()
     winds[1].start()
-    ins[1].start()
+    for c in range(1, PARTS):
+        ins[c].start()
     b_ref[PER_TILE * EXTRA : 128, :] = jnp.zeros((128 - PER_TILE * EXTRA, width), jnp.float32)
     lane = lax.broadcasted_iota(jnp.int32, (tiles, 128), 1)
     for c in range(PARTS):
         ins[c].wait()
-        if c + 2 < PARTS:
-            ins[c + 2].start()
         if c == 0:
             winds[0].wait()
             winds[1].wait()

time: 82.2 us -> 81.6 us (level)
  no operation moved by 1% of the time
where the time goes in v9:
time: 81.6 us; the launch traced here: 81.3 us
  waiting for transfers between devices  28.1 us (34%)
  starting transfers between devices  21.9 us (27%)
  Pallas kernels  17 us (21%)
  blocking collectives  9.63 us (12%)
  local copies, waits for them, and re-layouts  4.42 us (5%)
    all_to_all x1, waiting for transfers between devices, local(): lax.all_to_all(packed.reshape(TILES, 1, SLOTS * 128), 'comp', split_axis=...  24.5 us
    all_to_all x1, starting transfers between devices, local(): lax.all_to_all(packed.reshape(TILES, 1, SLOTS * 128), 'comp', split_axis=...  17.4 us
    pallas_call x8, Pallas kernels, call(): pl.pallas_call(kernel, out_shape=shapes, in_specs=ins, out_specs=outs or...  17 us
    all_to_all x1, blocking collectives, local(): lax.all_to_all(partial, 'grp', split_axis=0, concat_axis=0, tiled=True)  9.63 us
    ppermute x1, waiting for transfers between devices, local(): got_first = lax.ppermute(first, ('grp', 'comp'), across)  3.61 us
    unnamed x4, local copies, waits for them, and re-layouts  2.67 us
    ppermute x1, starting transfers between devices, local(): got_second = lax.ppermute(second, ('grp', 'comp'), within)  2.6 us
    ppermute x1, starting transfers between devices, local(): got_first = lax.ppermute(first, ('grp', 'comp'), across)  1.92 us
  transfers between devices with their start and end apart: 3, of which 2 were waited for; matrix products, arithmetic and copies ran while one was open for 2% of the time, Pallas kernels for 9%

profile of v9, /device:TPU:8, one launch (start us, length us, event | category | flops | bytes accessed | tf_op | source)
XLA Modules:
  0.0 81.3 jit_solution(3123883800514217823)
XLA Ops:
  0.0 0.0 copy-start.1
  0.0 2.6 %shard_map.64 = f32[1920,128]{1,0:T(8,128)} custom-call(f32[150,1536]{1,0:T(8,128)} %x_hbm.1, f32[12,128]{1,0:T(8,128)} %bitcast.12, f32[12,128]{1,0:T(8,128)} %bitcast.13), custom_call_target="tpu_custom_call" | custom-call | tf_op jit(solution)/shard_map/pallas_call | solution.py:509
  2.6 17.4 %all-to-all-start = ((f32[128,1,1920]{2,1,0:T(1,128)}), f32[128,1,1920]{2,1,0:T(1,128)S(1)}, u32[]{:S(2)}, u32[]{:S(2)}) async-start(f32[128,1,1920]{2,1,0:T(1,128)} %bitcast.11), calls=%async_computation | async-start | bytes 1966080 | tf_op jit(solution)/shard_map/all_to_all | solution.py:552
  20.0 0.0 copy-done.1
  20.1 0.1 xor.26
  20.2 0.1 copy.9
  20.2 1.7 %shard_map.65.hot_ref = bf16[2048,1536]{1,0:T(8,128)(2,1)S(1)} custom-call(s32[12,128]{1,0:T(8,128)S(1)} %bitcast.10), custom_call_target="tpu_custom_call" | custom-call | tf_op jit(solution)/shard_map/pallas_call | solution.py:509
  21.9 0.0 copy-start
  22.0 2.7 %copy-done = bf16[2048,1536]{1,0:T(8,128)(2,1)} copy-done((bf16[2048,1536]{1,0:T(8,128)(2,1)}, bf16[2048,1536]{1,0:T(8,128)(2,1)S(1)}, u32[]{:S(2)}) %copy-start) | copy-done | bytes 6291480
  24.6 0.9 %dynamic-slice_bitcast_fusion.tab_ref = f32[152,128]{1,0:T(8,128)S(1)} fusion(f32[4,152,128]{2,1,0:T(8,128)} %constant.44.clone, s32[]{:T(128)S(6)} %select_n.13), kind=kLoop, calls=%fused_computation | loop fusion | bytes 155652 | tf_op jit(solution)/shard_map/jit(dynamic_index_in_dim)/squeeze | solution.py:527
  25.5 24.5 %all-to-all-done = f32[128,1,1920]{2,1,0:T(1,128)S(1)} async-done(((f32[128,1,1920]{2,1,0:T(1,128)}), f32[128,1,1920]{2,1,0:T(1,128)S(1)}, u32[]{:S(2)}, u32[]{:S(2)}) %all-to-all-start) | async-done | bytes 983072 | tf_op jit(solution)/shard_map/all_to_all | solution.py:552
  50.0 0.4 shard_map.66
  50.4 9.6 %all_to_all.10.e_ref = f32[4,24,128]{2,1,0:T(8,128)S(1)} all-to-all(f32[4,24,128]{2,1,0:T(8,128)S(1)} %get-tuple-element.19), channel_id=1, replica_groups=mesh['grp'=4,'comp'=128] {'grp'}, dimensions={0} | all-to-all | bytes 98304 | tf_op jit(solution)/shard_map/all_to_all | solution.py:573
  60.1 3.5 %shard_map.67 = (f32[4,328,128]{2,1,0:T(8,128)S(1)}, bf16[256,1536]{1,0:T(8,128)(2,1)S(1)}, bf16[256,1536]{1,0:T(8,128)(2,1)S(1)}, bf16[1024,1536]{1,0:T(8,128)(2,1)S(1)}) custom-call(f32[12,152,128]{2,1,0:T(8,128)S(1)} %get-tuple-element.17.y_ref, f32[24,128]{1,0:T(8,128)S(1)} %get-tuple-element.18.wind_ref, f32[4,24,128]{2,1,0:T(8,128)S(1)} %all_to_all.10.e_ref, ...), custom_call_target="tpu_custom_call" | custom-call | tf_op jit(solution)/shard_map/pallas_call | solution.py:509
  63.5 1.9 %collective-permute-start = (f32[4,328,128]{2,1,0:T(8,128)S(1)}, f32[4,328,128]{2,1,0:T(8,128)S(1)}, u32[]{:S(2)}, u32[]{:S(2)}) collective-permute-start(f32[4,328,128]{2,1,0:T(8,128)S(1)} %get-tuple-element.21.first_ref), channel_id=1, source_target_pairs={{1,2},{2,1},{3,4},{4,3},{5,6},{6,5},{7,8},{8,7},{9,10},{10,9},{11,... | collective-permute-start | bytes 2015240 | tf_op jit(solution)/shard_map/ppermute | solution.py:606
  65.5 1.8 %shard_map.68.second_ref = f32[4,320,128]{2,1,0:T(8,128)S(1)} custom-call(bf16[256,1536]{1,0:T(8,128)(2,1)S(1)} %get-tuple-element.22.main_ref, bf16[256,1536]{1,0:T(8,128)(2,1)S(1)} %get-tuple-element.23.side_ref, bf16[1024,1536]{1,0:T(8,128)(2,1)S(1)} %get-tuple-element.24.kept_ref), custom_call_target="tpu_custom_call" | custom-call | flops 2000000000 | bytes 6000000 | tf_op jit(solution)/shard_map/pallas_call | solution.py:509
  67.3 2.6 %collective-permute-start.1 = (f32[4,320,128]{2,1,0:T(8,128)S(1)}, f32[4,320,128]{2,1,0:T(8,128)S(1)}, u32[]{:S(2)}, u32[]{:S(2)}) collective-permute-start(f32[4,320,128]{2,1,0:T(8,128)S(1)} %shard_map.68.second_ref), channel_id=1, source_target_pairs={{0,1},{1,0},{2,3},{3,2},{4,5},{5,4},{6,7},{7,6},{8,9},{9,8},{10,11... | collective-permute-start | bytes 1966088 | tf_op jit(solution)/shard_map/ppermute | solution.py:607
  69.9 0.7 dynamic-slice_bitcast_fusion.1.tab_ref
  70.6 2.0 %shard_map.69 = (f32[5,320,128]{2,1,0:T(8,128)S(1)}, f32[2,3,128,128]{3,2,1,0:T(8,128)S(1)}) custom-call(f32[8,256]{1,0:T(8,128)S(1)} %dynamic-slice_bitcast_fusion.1.tab_ref, f32[4,328,128]{2,1,0:T(8,128)S(1)} %get-tuple-element.21.first_ref, f32[4,320,128]{2,1,0:T(8,128)S(1)} %shard_map.68.second_ref), custom_call_target="tpu_custom_call" | custom-call | flops 3000000000 | bytes 9000000 | tf_op jit(solution)/shard_map/pallas_call | solution.py:509
  72.6 0.0 collective-permute-done.1.got_ref
  72.6 1.5 %shard_map.70.near_ref = f32[4,3,128,128]{3,2,1,0:T(8,128)S(1)} custom-call(f32[8,256]{1,0:T(8,128)S(1)} %dynamic-slice_bitcast_fusion.1.tab_ref, f32[4,328,128]{2,1,0:T(8,128)S(1)} %get-tuple-element.21.first_ref, f32[4,320,128]{2,1,0:T(8,128)S(1)} %shard_map.68.second_ref, f32[4,320,128]{2,1,0:T(8,128)S(1)} %collective-permute-done.1.got_ref, ...), custom_call_target="tpu_custom_call" | custom-call | tf_op jit(solution)/shard_map/pallas_call | solution.py:509
  74.1 3.6 %collective-permute-done.got_ref = f32[4,328,128]{2,1,0:T(8,128)S(1)} collective-permute-done((f32[4,328,128]{2,1,0:T(8,128)S(1)}, f32[4,328,128]{2,1,0:T(8,128)S(1)}, u32[]{:S(2)}, u32[]{:S(2)}) %collective-permute-start) | collective-permute-done | bytes 671776 | tf_op jit(solution)/shard_map/ppermute | solution.py:606
  77.7 3.5 %shard_map.71 = f32[150,8,256]{2,1,0:T(8,128)} custom-call(f32[8,256]{1,0:T(8,128)S(1)} %dynamic-slice_bitcast_fusion.1.tab_ref, f32[4,328,128]{2,1,0:T(8,128)S(1)} %get-tuple-element.21.first_ref, f32[4,320,128]{2,1,0:T(8,128)S(1)} %shard_map.68.second_ref, f32[4,328,128]{2,1,0:T(8,128)S(1)} %collective-permute-done.got_ref, ...), custom_call_target="tpu_custom_call" | custom-call | tf_op jit(solution)/shard_map/pallas_call | solution.py:509
  (1 shorter events, 0.0 us)
Async XLA Ops:
  0.0 20.0 %copy-start.1 = (s32[1536]{0:T(1024)S(1)}, s32[1536]{0:T(1024)}, u32[]{:S(2)}) copy-start(s32[1536]{0:T(1024)} %param.9) | copy-start | bytes 18436
  2.6 47.4 %all-to-all-start = ((f32[128,1,1920]{2,1,0:T(1,128)}), f32[128,1,1920]{2,1,0:T(1,128)S(1)}, u32[]{:S(2)}, u32[]{:S(2)}) async-start(f32[128,1,1920]{2,1,0:T(1,128)} %bitcast.11), calls=%async_computation | async-start | bytes 1966080 | tf_op jit(solution)/shard_map/all_to_all | solution.py:552
  21.9 2.7 %copy-start = (bf16[2048,1536]{1,0:T(8,128)(2,1)}, bf16[2048,1536]{1,0:T(8,128)(2,1)S(1)}, u32[]{:S(2)}) copy-start(bf16[2048,1536]{1,0:T(8,128)(2,1)S(1)} %shard_map.65.hot_ref) | copy-start | bytes 18874372
  63.5 14.2 %collective-permute-start = (f32[4,328,128]{2,1,0:T(8,128)S(1)}, f32[4,328,128]{2,1,0:T(8,128)S(1)}, u32[]{:S(2)}, u32[]{:S(2)}) collective-permute-start(f32[4,328,128]{2,1,0:T(8,128)S(1)} %get-tuple-element.21.first_ref), channel_id=1, source_target_pairs={{1,2},{2,1},{3,4},{4,3},{5,6},{6,5},{7,8},{8,7},{9,10},{10,9},{11,... | collective-permute-start | bytes 2015240 | tf_op jit(solution)/shard_map/ppermute | solution.py:606
  67.3 5.3 %collective-permute-start.1 = (f32[4,320,128]{2,1,0:T(8,128)S(1)}, f32[4,320,128]{2,1,0:T(8,128)S(1)}, u32[]{:S(2)}, u32[]{:S(2)}) collective-permute-start(f32[4,320,128]{2,1,0:T(8,128)S(1)} %shard_map.68.second_ref), channel_id=1, source_target_pairs={{0,1},{1,0},{2,3},{3,2},{4,5},{5,4},{6,7},{7,6},{8,9},{9,8},{10,11... | collective-permute-start | bytes 1966088 | tf_op jit(solution)/shard_map/ppermute | solution.py:607

commit v10 on v9

--- a/solution.py
+++ b/solution.py
@@ -35,7 +35,7 @@
 PACKS = 4
 SHORT = PHASES // PACKS
 LINES = (PHASES + SHORT) * 8
-CHUNK = 4
+CHUNK = 8
 PAD = 8
 PARTS = 4
 HALF = TROWS * NY // 2
@@ -94,10 +94,13 @@
     b_ref[PER_TILE * EXTRA : 128, :] = jnp.zeros((128 - PER_TILE * EXTRA, width), jnp.float32)
     lane = lax.broadcasted_iota(jnp.int32, (tiles, 128), 1)
     for c in range(PARTS):
-        ins[c].wait()
         if c == 0:
             winds[0].wait()
             winds[1].wait()
+            speed, heading = wind_ref[0], wind_ref[1]
+            wind_ref[0] = speed * jnp.cos(heading)
+            wind_ref[1] = speed * jnp.sin(heading)
+        ins[c].wait()
         for copy in range(PER_TILE):
             b_ref[copy * EXTRA : copy * EXTRA + LOCAL - MAIN, :] = x_ref[c, MAIN:LOCAL, :]
         for block in range(width // 128):
@@ -206,9 +209,7 @@
     steepness = energy * wavenumber * wavenumber
     ratio = steepness / (steepness + 0.02)
     decay = ratio / (mean * mean)
-    speed, heading = wind_ref[0:SEND, :], wind_ref[SEND : 2 * SEND, :]
-    along = speed * jnp.cos(heading)
-    across = speed * jnp.sin(heading)
+    along, across = wind_ref[0:SEND, :], wind_ref[SEND : 2 * SEND, :]
     ccos = jnp.broadcast_to(tab_ref[:, C_COS : C_COS + 1], (ROWS, 128))
     csin = jnp.broadcast_to(tab_ref[:, C_SIN : C_SIN + 1], (ROWS, 128))
     cout = jnp.broadcast_to(tab_ref[:, C_OUT : C_OUT + 1], (ROWS, 128))

time: 81.6 us -> 81.4 us (level)
  Pallas kernels: 17 us -> 16 us
    pallas_call x8, Pallas kernels: 17 us -> 16 us  [call(): pl.pallas_call(kernel, out_shape=shapes, in_specs=ins, out_specs=outs or...]
  transfers between devices with their start and end apart: 3 -> 3, of which waited for: 2 -> 2; matrix products, arithmetic and copies ran while one was open for 2% -> 2% of each run, Pallas kernels for 9% -> 8%
where the time goes in v10:
time: 81.4 us; the launch traced here: 81 us
  waiting for transfers between devices  28.9 us (36%)
  starting transfers between devices  21.9 us (27%)
  Pallas kernels  16 us (20%)
  blocking collectives  9.63 us (12%)
  local copies, waits for them, and re-layouts  4.42 us (5%)
    all_to_all x1, waiting for transfers between devices, local(): lax.all_to_all(packed.reshape(TILES, 1, SLOTS * 128), 'comp', split_axis=...  24.5 us
    all_to_all x1, starting transfers between devices, local(): lax.all_to_all(packed.reshape(TILES, 1, SLOTS * 128), 'comp', split_axis=...  17.4 us
    pallas_call x8, Pallas kernels, call(): pl.pallas_call(kernel, out_shape=shapes, in_specs=ins, out_specs=outs or...  16 us
    all_to_all x1, blocking collectives, local(): lax.all_to_all(partial, 'grp', split_axis=0, concat_axis=0, tiled=True)  9.63 us
    ppermute x1, waiting for transfers between devices, local(): got_first = lax.ppermute(first, ('grp', 'comp'), across)  4.34 us
    unnamed x4, local copies, waits for them, and re-layouts  2.67 us
    ppermute x1, starting transfers between devices, local(): got_second = lax.ppermute(second, ('grp', 'comp'), within)  2.6 us
    ppermute x1, starting transfers between devices, local(): got_first = lax.ppermute(first, ('grp', 'comp'), across)  1.92 us
  transfers between devices with their start and end apart: 3, of which 2 were waited for; matrix products, arithmetic and copies ran while one was open for 2% of the time, Pallas kernels for 8%

profile of v10, /device:TPU:8, one launch (start us, length us, event | category | flops | bytes accessed | tf_op | source)
XLA Modules:
  0.0 81.0 jit_solution(532896614289139569)
XLA Ops:
  0.0 0.0 copy-start.1
  0.0 2.7 %shard_map.64 = f32[1920,128]{1,0:T(8,128)} custom-call(f32[150,1536]{1,0:T(8,128)} %x_hbm.1, f32[12,128]{1,0:T(8,128)} %bitcast.12, f32[12,128]{1,0:T(8,128)} %bitcast.13), custom_call_target="tpu_custom_call" | custom-call | tf_op jit(solution)/shard_map/pallas_call | solution.py:510
  2.7 17.4 %all-to-all-start = ((f32[128,1,1920]{2,1,0:T(1,128)}), f32[128,1,1920]{2,1,0:T(1,128)S(1)}, u32[]{:S(2)}, u32[]{:S(2)}) async-start(f32[128,1,1920]{2,1,0:T(1,128)} %bitcast.11), calls=%async_computation | async-start | bytes 1966080 | tf_op jit(solution)/shard_map/all_to_all | solution.py:553
  20.1 0.0 copy-done.1
  20.1 0.1 xor.26
  20.2 0.1 copy.9
  20.3 1.7 %shard_map.65.hot_ref = bf16[2048,1536]{1,0:T(8,128)(2,1)S(1)} custom-call(s32[12,128]{1,0:T(8,128)S(1)} %bitcast.10), custom_call_target="tpu_custom_call" | custom-call | tf_op jit(solution)/shard_map/pallas_call | solution.py:510
  22.0 0.0 copy-start
  22.0 2.7 %copy-done = bf16[2048,1536]{1,0:T(8,128)(2,1)} copy-done((bf16[2048,1536]{1,0:T(8,128)(2,1)}, bf16[2048,1536]{1,0:T(8,128)(2,1)S(1)}, u32[]{:S(2)}) %copy-start) | copy-done | bytes 6291480
  24.7 0.9 %dynamic-slice_bitcast_fusion.tab_ref = f32[152,128]{1,0:T(8,128)S(1)} fusion(f32[4,152,128]{2,1,0:T(8,128)} %constant.44.clone, s32[]{:T(128)S(6)} %select_n.13), kind=kLoop, calls=%fused_computation | loop fusion | bytes 155652 | tf_op jit(solution)/shard_map/jit(dynamic_index_in_dim)/squeeze | solution.py:528
  25.6 24.5 %all-to-all-done = f32[128,1,1920]{2,1,0:T(1,128)S(1)} async-done(((f32[128,1,1920]{2,1,0:T(1,128)}), f32[128,1,1920]{2,1,0:T(1,128)S(1)}, u32[]{:S(2)}, u32[]{:S(2)}) %all-to-all-start) | async-done | bytes 983072 | tf_op jit(solution)/shard_map/all_to_all | solution.py:553
  50.1 0.4 shard_map.66
  50.5 9.6 %all_to_all.10.e_ref = f32[4,24,128]{2,1,0:T(8,128)S(1)} all-to-all(f32[4,24,128]{2,1,0:T(8,128)S(1)} %get-tuple-element.19), channel_id=1, replica_groups=mesh['grp'=4,'comp'=128] {'grp'}, dimensions={0} | all-to-all | bytes 98304 | tf_op jit(solution)/shard_map/all_to_all | solution.py:574
  60.1 3.5 %shard_map.67 = (f32[4,328,128]{2,1,0:T(8,128)S(1)}, bf16[256,1536]{1,0:T(8,128)(2,1)S(1)}, bf16[256,1536]{1,0:T(8,128)(2,1)S(1)}, bf16[1024,1536]{1,0:T(8,128)(2,1)S(1)}) custom-call(f32[12,152,128]{2,1,0:T(8,128)S(1)} %get-tuple-element.17.y_ref, f32[24,128]{1,0:T(8,128)S(1)} %get-tuple-element.18.wind_ref, f32[4,24,128]{2,1,0:T(8,128)S(1)} %all_to_all.10.e_ref, ...), custom_call_target="tpu_custom_call" | custom-call | tf_op jit(solution)/shard_map/pallas_call | solution.py:510
  63.6 1.9 %collective-permute-start = (f32[4,328,128]{2,1,0:T(8,128)S(1)}, f32[4,328,128]{2,1,0:T(8,128)S(1)}, u32[]{:S(2)}, u32[]{:S(2)}) collective-permute-start(f32[4,328,128]{2,1,0:T(8,128)S(1)} %get-tuple-element.21.first_ref), channel_id=1, source_target_pairs={{1,2},{2,1},{3,4},{4,3},{5,6},{6,5},{7,8},{8,7},{9,10},{10,9},{11,... | collective-permute-start | bytes 2015240 | tf_op jit(solution)/shard_map/ppermute | solution.py:607
  65.5 1.8 %shard_map.68.second_ref = f32[4,320,128]{2,1,0:T(8,128)S(1)} custom-call(bf16[256,1536]{1,0:T(8,128)(2,1)S(1)} %get-tuple-element.22.main_ref, bf16[256,1536]{1,0:T(8,128)(2,1)S(1)} %get-tuple-element.23.side_ref, bf16[1024,1536]{1,0:T(8,128)(2,1)S(1)} %get-tuple-element.24.kept_ref), custom_call_target="tpu_custom_call" | custom-call | flops 2000000000 | bytes 6000000 | tf_op jit(solution)/shard_map/pallas_call | solution.py:510
  67.3 2.6 %collective-permute-start.1 = (f32[4,320,128]{2,1,0:T(8,128)S(1)}, f32[4,320,128]{2,1,0:T(8,128)S(1)}, u32[]{:S(2)}, u32[]{:S(2)}) collective-permute-start(f32[4,320,128]{2,1,0:T(8,128)S(1)} %shard_map.68.second_ref), channel_id=1, source_target_pairs={{0,1},{1,0},{2,3},{3,2},{4,5},{5,4},{6,7},{7,6},{8,9},{9,8},{10,11... | collective-permute-start | bytes 1966088 | tf_op jit(solution)/shard_map/ppermute | solution.py:608
  69.9 0.7 dynamic-slice_bitcast_fusion.1.tab_ref
  70.6 1.6 %shard_map.69 = (f32[5,320,128]{2,1,0:T(8,128)S(1)}, f32[2,3,128,128]{3,2,1,0:T(8,128)S(1)}) custom-call(f32[8,256]{1,0:T(8,128)S(1)} %dynamic-slice_bitcast_fusion.1.tab_ref, f32[4,328,128]{2,1,0:T(8,128)S(1)} %get-tuple-element.21.first_ref, f32[4,320,128]{2,1,0:T(8,128)S(1)} %shard_map.68.second_ref), custom_call_target="tpu_custom_call" | custom-call | flops 3000000000 | bytes 9000000 | tf_op jit(solution)/shard_map/pallas_call | solution.py:510
  72.3 0.0 collective-permute-done.1.got_ref
  72.3 1.1 %shard_map.70.near_ref = f32[4,3,128,128]{3,2,1,0:T(8,128)S(1)} custom-call(f32[8,256]{1,0:T(8,128)S(1)} %dynamic-slice_bitcast_fusion.1.tab_ref, f32[4,328,128]{2,1,0:T(8,128)S(1)} %get-tuple-element.21.first_ref, f32[4,320,128]{2,1,0:T(8,128)S(1)} %shard_map.68.second_ref, f32[4,320,128]{2,1,0:T(8,128)S(1)} %collective-permute-done.1.got_ref, ...), custom_call_target="tpu_custom_call" | custom-call | tf_op jit(solution)/shard_map/pallas_call | solution.py:510
  73.4 4.3 %collective-permute-done.got_ref = f32[4,328,128]{2,1,0:T(8,128)S(1)} collective-permute-done((f32[4,328,128]{2,1,0:T(8,128)S(1)}, f32[4,328,128]{2,1,0:T(8,128)S(1)}, u32[]{:S(2)}, u32[]{:S(2)}) %collective-permute-start) | collective-permute-done | bytes 671776 | tf_op jit(solution)/shard_map/ppermute | solution.py:607
  77.8 3.2 %shard_map.71 = f32[150,8,256]{2,1,0:T(8,128)} custom-call(f32[8,256]{1,0:T(8,128)S(1)} %dynamic-slice_bitcast_fusion.1.tab_ref, f32[4,328,128]{2,1,0:T(8,128)S(1)} %get-tuple-element.21.first_ref, f32[4,320,128]{2,1,0:T(8,128)S(1)} %shard_map.68.second_ref, f32[4,328,128]{2,1,0:T(8,128)S(1)} %collective-permute-done.got_ref, ...), custom_call_target="tpu_custom_call" | custom-call | tf_op jit(solution)/shard_map/pallas_call | solution.py:510
  (1 shorter events, 0.0 us)
Async XLA Ops:
  0.0 20.1 %copy-start.1 = (s32[1536]{0:T(1024)S(1)}, s32[1536]{0:T(1024)}, u32[]{:S(2)}) copy-start(s32[1536]{0:T(1024)} %param.9) | copy-start | bytes 18436
  2.7 47.4 %all-to-all-start = ((f32[128,1,1920]{2,1,0:T(1,128)}), f32[128,1,1920]{2,1,0:T(1,128)S(1)}, u32[]{:S(2)}, u32[]{:S(2)}) async-start(f32[128,1,1920]{2,1,0:T(1,128)} %bitcast.11), calls=%async_computation | async-start | bytes 1966080 | tf_op jit(solution)/shard_map/all_to_all | solution.py:553
  22.0 2.7 %copy-start = (bf16[2048,1536]{1,0:T(8,128)(2,1)}, bf16[2048,1536]{1,0:T(8,128)(2,1)S(1)}, u32[]{:S(2)}) copy-start(bf16[2048,1536]{1,0:T(8,128)(2,1)S(1)} %shard_map.65.hot_ref) | copy-start | bytes 18874372
  63.6 14.2 %collective-permute-start = (f32[4,328,128]{2,1,0:T(8,128)S(1)}, f32[4,328,128]{2,1,0:T(8,128)S(1)}, u32[]{:S(2)}, u32[]{:S(2)}) collective-permute-start(f32[4,328,128]{2,1,0:T(8,128)S(1)} %get-tuple-element.21.first_ref), channel_id=1, source_target_pairs={{1,2},{2,1},{3,4},{4,3},{5,6},{6,5},{7,8},{8,7},{9,10},{10,9},{11,... | collective-permute-start | bytes 2015240 | tf_op jit(solution)/shard_map/ppermute | solution.py:607
  67.3 5.0 %collective-permute-start.1 = (f32[4,320,128]{2,1,0:T(8,128)S(1)}, f32[4,320,128]{2,1,0:T(8,128)S(1)}, u32[]{:S(2)}, u32[]{:S(2)}) collective-permute-start(f32[4,320,128]{2,1,0:T(8,128)S(1)} %shard_map.68.second_ref), channel_id=1, source_target_pairs={{0,1},{1,0},{2,3},{3,2},{4,5},{5,4},{6,7},{7,6},{8,9},{9,8},{10,11... | collective-permute-start | bytes 1966088 | tf_op jit(solution)/shard_map/ppermute | solution.py:608

commit v11 on v10

--- a/solution.py
+++ b/solution.py
@@ -35,7 +35,7 @@
 PACKS = 4
 SHORT = PHASES // PACKS
 LINES = (PHASES + SHORT) * 8
-CHUNK = 8
+CHUNK = 16
 PAD = 8
 PARTS = 4
 HALF = TROWS * NY // 2
@@ -272,6 +272,7 @@
 def substep(rows, seas, put, keep_ref, coef, base, phases, after, before):
     ux, kx, uy, ky = coef
     count = len(rows) - 3
+    width = min(CHUNK, phases)
 
     def load(spot, phase):
         ref, at = spot
@@ -286,22 +287,22 @@
         keep_ref[i, 1] = uy * before(end) + ky * limited(prior, ahead)
 
     def body(chunk, carry):
-        first = chunk * CHUNK
-        following = jnp.where(first + CHUNK == phases, 0, first + CHUNK)
-        wraps = first + CHUNK == phases
-        q = [load(rows[1], first + j) for j in range(CHUNK)]
-        diff = [q[j] - load(rows[0], first + j) for j in range(CHUNK)]
+        first = chunk * width
+        following = jnp.where(first + width == phases, 0, first + width)
+        wraps = first + width == phases
+        q = [load(rows[1], first + j) for j in range(width)]
+        diff = [q[j] - load(rows[0], first + j) for j in range(width)]
         flux = None
         for i in range(-1, count):
-            up = [load(rows[i + 3], first + j) for j in range(CHUNK)]
-            slope = [up[j] - q[j] for j in range(CHUNK)]
-            gone = [ux * q[j] + kx * limited(diff[j], slope[j]) for j in range(CHUNK)]
+            up = [load(rows[i + 3], first + j) for j in range(width)]
+            slope = [up[j] - q[j] for j in range(width)]
+            gone = [ux * q[j] + kx * limited(diff[j], slope[j]) for j in range(width)]
             if i >= 0:
                 behind, past = keep_ref[i, 0], keep_ref[i, 1]
                 edge = load(rows[i + 2], following)
                 edge = jnp.where(wraps, after(edge), edge)
-                for j in range(CHUNK):
-                    ahead = (q[j + 1] if j + 1 < CHUNK else edge) - q[j]
+                for j in range(width):
+                    ahead = (q[j + 1] if j + 1 < width else edge) - q[j]
                     side = uy * q[j] + ky * limited(behind, ahead)
                     new = q[j] - ((gone[j] - flux[j]) + (side - past))
                     sea = q[j] if seas is None else load(seas[i], first + j)
@@ -312,7 +313,7 @@
             q, diff, flux = up, slope, gone
         return carry
 
-    lax.fori_loop(0, phases // CHUNK, body, 0)
+    lax.fori_loop(0, phases // width, body, 0)
 
 
 def flags():

time: 81.4 us -> 81.3 us (level)
  no operation moved by 1% of the time
where the time goes in v11:
time: 81.3 us; the launch traced here: 81 us
  waiting for transfers between devices  29 us (36%)
  starting transfers between devices  21.9 us (27%)
  Pallas kernels  15.9 us (20%)
  blocking collectives  9.63 us (12%)
  local copies, waits for them, and re-layouts  4.42 us (5%)
    all_to_all x1, waiting for transfers between devices, local(): lax.all_to_all(packed.reshape(TILES, 1, SLOTS * 128), 'comp', split_axis=...  24.5 us
    all_to_all x1, starting transfers between devices, local(): lax.all_to_all(packed.reshape(TILES, 1, SLOTS * 128), 'comp', split_axis=...  17.4 us
    pallas_call x8, Pallas kernels, call(): pl.pallas_call(kernel, out_shape=shapes, in_specs=ins, out_specs=outs or...  15.9 us
    all_to_all x1, blocking collectives, local(): lax.all_to_all(partial, 'grp', split_axis=0, concat_axis=0, tiled=True)  9.63 us
    ppermute x1, waiting for transfers between devices, local(): got_first = lax.ppermute(first, ('grp', 'comp'), across)  4.43 us
    unnamed x4, local copies, waits for them, and re-layouts  2.67 us
    ppermute x1, starting transfers between devices, local(): got_second = lax.ppermute(second, ('grp', 'comp'), within)  2.6 us
    ppermute x1, starting transfers between devices, local(): got_first = lax.ppermute(first, ('grp', 'comp'), across)  1.92 us
  transfers between devices with their start and end apart: 3, of which 2 were waited for; matrix products, arithmetic and copies ran while one was open for 2% of the time, Pallas kernels for 8%

profile of v11, /device:TPU:8, one launch (start us, length us, event | category | flops | bytes accessed | tf_op | source)
XLA Modules:
  0.0 81.0 jit_solution(6259787021446592041)
XLA Ops:
  0.0 0.0 copy-start.1
  0.0 2.7 %shard_map.64 = f32[1920,128]{1,0:T(8,128)} custom-call(f32[150,1536]{1,0:T(8,128)} %x_hbm.1, f32[12,128]{1,0:T(8,128)} %bitcast.12, f32[12,128]{1,0:T(8,128)} %bitcast.13), custom_call_target="tpu_custom_call" | custom-call | tf_op jit(solution)/shard_map/pallas_call | solution.py:511
  2.7 17.4 %all-to-all-start = ((f32[128,1,1920]{2,1,0:T(1,128)}), f32[128,1,1920]{2,1,0:T(1,128)S(1)}, u32[]{:S(2)}, u32[]{:S(2)}) async-start(f32[128,1,1920]{2,1,0:T(1,128)} %bitcast.11), calls=%async_computation | async-start | bytes 1966080 | tf_op jit(solution)/shard_map/all_to_all | solution.py:554
  20.1 0.0 copy-done.1
  20.1 0.1 xor.26
  20.2 0.1 copy.9
  20.3 1.7 %shard_map.65.hot_ref = bf16[2048,1536]{1,0:T(8,128)(2,1)S(1)} custom-call(s32[12,128]{1,0:T(8,128)S(1)} %bitcast.10), custom_call_target="tpu_custom_call" | custom-call | tf_op jit(solution)/shard_map/pallas_call | solution.py:511
  22.0 0.0 copy-start
  22.0 2.7 %copy-done = bf16[2048,1536]{1,0:T(8,128)(2,1)} copy-done((bf16[2048,1536]{1,0:T(8,128)(2,1)}, bf16[2048,1536]{1,0:T(8,128)(2,1)S(1)}, u32[]{:S(2)}) %copy-start) | copy-done | bytes 6291480
  24.7 0.9 %dynamic-slice_bitcast_fusion.tab_ref = f32[152,128]{1,0:T(8,128)S(1)} fusion(f32[4,152,128]{2,1,0:T(8,128)} %constant.44.clone, s32[]{:T(128)S(6)} %select_n.13), kind=kLoop, calls=%fused_computation | loop fusion | bytes 155652 | tf_op jit(solution)/shard_map/jit(dynamic_index_in_dim)/squeeze | solution.py:529
  25.6 24.5 %all-to-all-done = f32[128,1,1920]{2,1,0:T(1,128)S(1)} async-done(((f32[128,1,1920]{2,1,0:T(1,128)}), f32[128,1,1920]{2,1,0:T(1,128)S(1)}, u32[]{:S(2)}, u32[]{:S(2)}) %all-to-all-start) | async-done | bytes 983072 | tf_op jit(solution)/shard_map/all_to_all | solution.py:554
  50.1 0.4 shard_map.66
  50.5 9.6 %all_to_all.10.e_ref = f32[4,24,128]{2,1,0:T(8,128)S(1)} all-to-all(f32[4,24,128]{2,1,0:T(8,128)S(1)} %get-tuple-element.19), channel_id=1, replica_groups=mesh['grp'=4,'comp'=128] {'grp'}, dimensions={0} | all-to-all | bytes 98304 | tf_op jit(solution)/shard_map/all_to_all | solution.py:575
  60.1 3.5 %shard_map.67 = (f32[4,328,128]{2,1,0:T(8,128)S(1)}, bf16[256,1536]{1,0:T(8,128)(2,1)S(1)}, bf16[256,1536]{1,0:T(8,128)(2,1)S(1)}, bf16[1024,1536]{1,0:T(8,128)(2,1)S(1)}) custom-call(f32[12,152,128]{2,1,0:T(8,128)S(1)} %get-tuple-element.17.y_ref, f32[24,128]{1,0:T(8,128)S(1)} %get-tuple-element.18.wind_ref, f32[4,24,128]{2,1,0:T(8,128)S(1)} %all_to_all.10.e_ref, ...), custom_call_target="tpu_custom_call" | custom-call | tf_op jit(solution)/shard_map/pallas_call | solution.py:511
  63.6 1.9 %collective-permute-start = (f32[4,328,128]{2,1,0:T(8,128)S(1)}, f32[4,328,128]{2,1,0:T(8,128)S(1)}, u32[]{:S(2)}, u32[]{:S(2)}) collective-permute-start(f32[4,328,128]{2,1,0:T(8,128)S(1)} %get-tuple-element.21.first_ref), channel_id=1, source_target_pairs={{1,2},{2,1},{3,4},{4,3},{5,6},{6,5},{7,8},{8,7},{9,10},{10,9},{11,... | collective-permute-start | bytes 2015240 | tf_op jit(solution)/shard_map/ppermute | solution.py:608
  65.5 1.8 %shard_map.68.second_ref = f32[4,320,128]{2,1,0:T(8,128)S(1)} custom-call(bf16[256,1536]{1,0:T(8,128)(2,1)S(1)} %get-tuple-element.22.main_ref, bf16[256,1536]{1,0:T(8,128)(2,1)S(1)} %get-tuple-element.23.side_ref, bf16[1024,1536]{1,0:T(8,128)(2,1)S(1)} %get-tuple-element.24.kept_ref), custom_call_target="tpu_custom_call" | custom-call | flops 2000000000 | bytes 6000000 | tf_op jit(solution)/shard_map/pallas_call | solution.py:511
  67.3 2.6 %collective-permute-start.1 = (f32[4,320,128]{2,1,0:T(8,128)S(1)}, f32[4,320,128]{2,1,0:T(8,128)S(1)}, u32[]{:S(2)}, u32[]{:S(2)}) collective-permute-start(f32[4,320,128]{2,1,0:T(8,128)S(1)} %shard_map.68.second_ref), channel_id=1, source_target_pairs={{0,1},{1,0},{2,3},{3,2},{4,5},{5,4},{6,7},{7,6},{8,9},{9,8},{10,11... | collective-permute-start | bytes 1966088 | tf_op jit(solution)/shard_map/ppermute | solution.py:609
  69.9 0.7 dynamic-slice_bitcast_fusion.1.tab_ref
  70.6 1.6 %shard_map.69 = (f32[5,320,128]{2,1,0:T(8,128)S(1)}, f32[2,3,128,128]{3,2,1,0:T(8,128)S(1)}) custom-call(f32[8,256]{1,0:T(8,128)S(1)} %dynamic-slice_bitcast_fusion.1.tab_ref, f32[4,328,128]{2,1,0:T(8,128)S(1)} %get-tuple-element.21.first_ref, f32[4,320,128]{2,1,0:T(8,128)S(1)} %shard_map.68.second_ref), custom_call_target="tpu_custom_call" | custom-call | flops 3000000000 | bytes 9000000 | tf_op jit(solution)/shard_map/pallas_call | solution.py:511
  72.3 0.0 collective-permute-done.1.got_ref
  72.3 1.1 %shard_map.70.near_ref = f32[4,3,128,128]{3,2,1,0:T(8,128)S(1)} custom-call(f32[8,256]{1,0:T(8,128)S(1)} %dynamic-slice_bitcast_fusion.1.tab_ref, f32[4,328,128]{2,1,0:T(8,128)S(1)} %get-tuple-element.21.first_ref, f32[4,320,128]{2,1,0:T(8,128)S(1)} %shard_map.68.second_ref, f32[4,320,128]{2,1,0:T(8,128)S(1)} %collective-permute-done.1.got_ref, ...), custom_call_target="tpu_custom_call" | custom-call | tf_op jit(solution)/shard_map/pallas_call | solution.py:511
  73.3 4.4 %collective-permute-done.got_ref = f32[4,328,128]{2,1,0:T(8,128)S(1)} collective-permute-done((f32[4,328,128]{2,1,0:T(8,128)S(1)}, f32[4,328,128]{2,1,0:T(8,128)S(1)}, u32[]{:S(2)}, u32[]{:S(2)}) %collective-permute-start) | collective-permute-done | bytes 671776 | tf_op jit(solution)/shard_map/ppermute | solution.py:608
  77.8 3.2 %shard_map.71 = f32[150,8,256]{2,1,0:T(8,128)} custom-call(f32[8,256]{1,0:T(8,128)S(1)} %dynamic-slice_bitcast_fusion.1.tab_ref, f32[4,328,128]{2,1,0:T(8,128)S(1)} %get-tuple-element.21.first_ref, f32[4,320,128]{2,1,0:T(8,128)S(1)} %shard_map.68.second_ref, f32[4,328,128]{2,1,0:T(8,128)S(1)} %collective-permute-done.got_ref, ...), custom_call_target="tpu_custom_call" | custom-call | tf_op jit(solution)/shard_map/pallas_call | solution.py:511
  (1 shorter events, 0.0 us)
Async XLA Ops:
  0.0 20.1 %copy-start.1 = (s32[1536]{0:T(1024)S(1)}, s32[1536]{0:T(1024)}, u32[]{:S(2)}) copy-start(s32[1536]{0:T(1024)} %param.9) | copy-start | bytes 18436
  2.7 47.4 %all-to-all-start = ((f32[128,1,1920]{2,1,0:T(1,128)}), f32[128,1,1920]{2,1,0:T(1,128)S(1)}, u32[]{:S(2)}, u32[]{:S(2)}) async-start(f32[128,1,1920]{2,1,0:T(1,128)} %bitcast.11), calls=%async_computation | async-start | bytes 1966080 | tf_op jit(solution)/shard_map/all_to_all | solution.py:554
  22.0 2.7 %copy-start = (bf16[2048,1536]{1,0:T(8,128)(2,1)}, bf16[2048,1536]{1,0:T(8,128)(2,1)S(1)}, u32[]{:S(2)}) copy-start(bf16[2048,1536]{1,0:T(8,128)(2,1)S(1)} %shard_map.65.hot_ref) | copy-start | bytes 18874372
  63.6 14.2 %collective-permute-start = (f32[4,328,128]{2,1,0:T(8,128)S(1)}, f32[4,328,128]{2,1,0:T(8,128)S(1)}, u32[]{:S(2)}, u32[]{:S(2)}) collective-permute-start(f32[4,328,128]{2,1,0:T(8,128)S(1)} %get-tuple-element.21.first_ref), channel_id=1, source_target_pairs={{1,2},{2,1},{3,4},{4,3},{5,6},{6,5},{7,8},{8,7},{9,10},{10,9},{11,... | collective-permute-start | bytes 2015240 | tf_op jit(solution)/shard_map/ppermute | solution.py:608
  67.3 4.9 %collective-permute-start.1 = (f32[4,320,128]{2,1,0:T(8,128)S(1)}, f32[4,320,128]{2,1,0:T(8,128)S(1)}, u32[]{:S(2)}, u32[]{:S(2)}) collective-permute-start(f32[4,320,128]{2,1,0:T(8,128)S(1)} %shard_map.68.second_ref), channel_id=1, source_target_pairs={{0,1},{1,0},{2,3},{3,2},{4,5},{5,4},{6,7},{7,6},{8,9},{9,8},{10,11... | collective-permute-start | bytes 1966088 | tf_op jit(solution)/shard_map/ppermute | solution.py:609
